TPU v7x, 128 devices: a whole 4x4x4 slice. The times are simulated.
128 devices in a mesh: row: 8 (over x_lo, z), col: 8 (over y, x_hi), head: 2 (over core).
Axes of the slice: x: 4 (x_hi: 2, x_lo: 2; x = x_hi * 2 + x_lo), y: 4, z: 4, core: 2. Of those that a mesh axis runs over, the one named last changes fastest.
Arguments:
- query_vectors: bfloat16 [8192, 768], P(('row', 'col'), 'head'), may hold values from -4.5 to 4.5
- key_vectors: bfloat16 [8192, 768], P(('row', 'col'), 'head'), may hold values from -4.5 to 4.5
- value_vectors: bfloat16 [8192, 768], P(('row', 'col'), 'head'), may hold values from -6 to 6
- segment_ids: int32 [8192], P(('row', 'col')), may hold values from 0 to 7, never falling along the last dimension, each value on 1 to 5120 neighbouring positions
- out_weight: bfloat16 [768, 1536], P('head'), may hold values from -0.21875 to 0.21875
- grad_output: bfloat16 [8192, 1536], P(('row', 'col')), may hold values from -6 to 6
Outputs:
- mixed_output: bfloat16 [8192, 1536], P(('row', 'col'))
- grad_queries: bfloat16 [8192, 768], P(('row', 'col'), 'head')
- grad_keys: bfloat16 [8192, 768], P(('row', 'col'), 'head')
- grad_values: bfloat16 [8192, 768], P(('row', 'col'), 'head')
Inputs may be any that keep to these rules, and one draw needn't show every extreme that they name: `segment_ids`: nondecreasing along the tokens; each of the 8 images holds 1 to 5120 tokens, and one holds exactly 5120.
All inputs are finite; a program needn't handle non-finite values.
Results may differ from a plain program's by a relative error of at most 0.019.
Values may be sent and summed in bfloat16 or wider, within the bound.
No kernel may reach another device: no remote copies, remote signals or barrier semaphores. Data moves between devices by JAX's collectives and lax.ppermute only.
A program may use at most 128 MiB of HBM per device.

v0:
```python
import math

import jax
import jax.numpy as jnp
from jax import lax
from jax.sharding import PartitionSpec as P

HD = 128


def score_scale():
    return 1.0 / math.sqrt(HD)


def split_heads(matrix):
    return matrix.reshape(matrix.shape[0], matrix.shape[1] // HD, HD)


def join_heads(stacked):
    return jnp.transpose(stacked, (1, 0, 2)).reshape(stacked.shape[1], -1)


def masked_scores(query_part, key_part, seg_query, seg_key):
    raw_scores = (
        jnp.einsum("qhd,khd->hqk", query_part, key_part, preferred_element_type=jnp.float32)
        * score_scale()
    )
    allowed = (seg_query[:, None] == seg_key[None, :])[None, :, :]
    return (jnp.where(allowed, raw_scores, -1e30), allowed)


def on_device(query_vectors, key_vectors, value_vectors, segment_ids, out_weight, grad_output):
    query_heads = split_heads(query_vectors)
    key_heads = split_heads(key_vectors)
    value_heads = split_heads(value_vectors)
    head_count = query_heads.shape[1]
    row_count = query_vectors.shape[0]
    grad_attn = jnp.einsum(
        "tw,cw->tc", grad_output, out_weight, preferred_element_type=jnp.float32
    ).astype(jnp.bfloat16)
    grad_heads = split_heads(grad_attn)
    start_max = jnp.full((head_count, row_count, 1), -1e30, jnp.float32)
    zero_stat = jnp.zeros((head_count, row_count, 1), jnp.float32)
    zero_accum = jnp.zeros((head_count, row_count, HD), jnp.float32)
    shard_piece = (
        lax.all_gather(key_vectors, ("row", "col"), axis=0, tiled=True),
        lax.all_gather(segment_ids, ("row", "col"), axis=0, tiled=True),
    )

    def update(current):
        running_max, running_sum = current
        scores, allowed = masked_scores(
            query_heads, split_heads(shard_piece[0]), segment_ids, shard_piece[-1]
        )
        new_max = jnp.maximum(running_max, jnp.max(scores, axis=2, keepdims=True))
        exp_terms = jnp.where(allowed, jnp.exp(scores - new_max), 0.0)
        running_sum = jnp.sum(exp_terms, axis=2, keepdims=True)
        return (new_max, running_sum)

    running_max, running_sum = update((start_max, zero_stat))
    log_norm = running_max + jnp.log(running_sum)
    make_shard_piece = (
        lax.all_gather(key_vectors, ("row", "col"), axis=0, tiled=True),
        lax.all_gather(value_vectors, ("row", "col"), axis=0, tiled=True),
        lax.all_gather(segment_ids, ("row", "col"), axis=0, tiled=True),
    )

    def update(current):
        key_part = split_heads(make_shard_piece[0])
        value_part = split_heads(make_shard_piece[1])
        scores, allowed = masked_scores(query_heads, key_part, segment_ids, make_shard_piece[2])
        prob_full = jnp.where(allowed, jnp.exp(scores - log_norm), 0.0)
        weights = prob_full.astype(jnp.bfloat16)
        grad_prob = jnp.einsum(
            "qhd,khd->hqk", grad_heads, value_part, preferred_element_type=jnp.float32
        )
        mix_weight = (prob_full * grad_prob).astype(jnp.bfloat16)
        acc_out = jnp.einsum(
            "hqk,khd->hqd", weights, value_part, preferred_element_type=jnp.float32
        )
        acc_mixed = jnp.einsum(
            "hqk,khd->hqd", mix_weight, key_part, preferred_element_type=jnp.float32
        )
        acc_plain = jnp.einsum(
            "hqk,khd->hqd", weights, key_part, preferred_element_type=jnp.float32
        )
        return (acc_out, acc_mixed, acc_plain)

    acc_out, acc_mixed, acc_plain = update((zero_accum, zero_accum, zero_accum))
    attn_heads = acc_out.astype(jnp.bfloat16)
    row_delta = jnp.einsum(
        "hqd,qhd->hq", attn_heads, grad_heads, preferred_element_type=jnp.float32
    )[:, :, None]
    query_grad = ((acc_mixed - row_delta * acc_plain) * score_scale()).astype(jnp.bfloat16)
    attn_rows = join_heads(attn_heads)
    partial_out = jnp.dot(attn_rows, out_weight, preferred_element_type=jnp.float32)
    mixed_output = lax.psum(partial_out.astype(jnp.bfloat16), "head")
    norm_rows = jnp.transpose(log_norm[:, :, 0])
    delta_rows = jnp.transpose(row_delta[:, :, 0])
    all_norms, all_deltas = (
        lax.all_gather(norm_rows, ("row", "col"), axis=0, tiled=True),
        lax.all_gather(delta_rows, ("row", "col"), axis=0, tiled=True),
    )
    zero_keys = jnp.zeros((row_count, head_count, HD), jnp.float32)
    query_piece = lax.all_gather(query_vectors, ("row", "col"), axis=0, tiled=True)
    grad_piece = lax.all_gather(grad_attn, ("row", "col"), axis=0, tiled=True)
    seg_piece = lax.all_gather(segment_ids, ("row", "col"), axis=0, tiled=True)

    def update(current):
        query_part = split_heads(query_piece)
        grad_part = split_heads(grad_piece)
        norm_part = jnp.transpose(all_norms)[:, :, None]
        delta_part = jnp.transpose(all_deltas)[:, :, None]
        scores, allowed = masked_scores(query_part, key_heads, seg_piece, segment_ids)
        prob_full = jnp.where(allowed, jnp.exp(scores - norm_part), 0.0)
        weights = prob_full.astype(jnp.bfloat16)
        grad_prob = jnp.einsum(
            "qhd,khd->hqk", grad_part, value_heads, preferred_element_type=jnp.float32
        )
        grad_scores = (prob_full * (grad_prob - delta_part) * score_scale()).astype(jnp.bfloat16)
        acc_key = jnp.einsum(
            "hqk,qhd->khd", grad_scores, query_part, preferred_element_type=jnp.float32
        )
        acc_value = jnp.einsum(
            "hqk,qhd->khd", weights, grad_part, preferred_element_type=jnp.float32
        )
        return (acc_key, acc_value)

    acc_key, acc_value = update((zero_keys, zero_keys))
    grad_keys = acc_key.reshape(row_count, -1).astype(jnp.bfloat16)
    grad_values = acc_value.reshape(row_count, -1).astype(jnp.bfloat16)
    grad_queries = join_heads(query_grad)
    return (mixed_output, grad_queries, grad_keys, grad_values)


def solution(mesh):
    in_specs = (
        P(("row", "col"), "head"),
        P(("row", "col"), "head"),
        P(("row", "col"), "head"),
        P(("row", "col")),
        P("head", None),
        P(("row", "col"), None),
    )
    out_specs = (
        P(("row", "col"), None),
        P(("row", "col"), "head"),
        P(("row", "col"), "head"),
        P(("row", "col"), "head"),
    )
    return jax.shard_map(
        on_device, mesh=mesh, in_specs=in_specs, out_specs=out_specs, check_vma=False
    )
```

profile of v0, /device:TPU:0, one launch (start us, length us, event | category | flops | bytes accessed | tf_op | source)
XLA Modules:
  0.0 1367.7 jit_solution(1729225022353792383)
XLA Ops:
  7.2 0.0 copy-start
  7.2 0.0 all-gather.8.cloned.1.call-start
  7.2 0.7 all-gather.8.cloned.1.call-update
  7.9 0.0 all-gather.6.cloned.1.call-start
  8.0 1.6 copy.36
  9.6 0.0 all-gather.6.cloned.1.call-update
  9.6 0.0 all-gather.10.cloned.1.call-start
  9.7 1.6 copy.35
  11.3 0.0 all-gather.10.cloned.1.call-update
  11.3 0.0 all-gather.12.cloned.1.call-start
  11.4 0.0 copy-done
  11.4 2.1 convolution_convert_fusion.2
  13.5 0.0 all-gather.12.cloned.1.call-update
  13.6 0.0 all-reduce.2.cloned.1.call-start
  13.6 1.0 copy.40
  14.6 1.7 copy.48
  16.3 177.8 %all-gather = s32[64,1,128]{2,1,0:T(1,128)S(1)} all-gather(s32[1,1,128]{2,1,0:T(1,128)} %bitcast.78), channel_id=1, replica_groups=mesh['row'=8,'col'=8,'head'=2] {'row','col'}, dimensions={0}, use_global_device_ids=true | all-gather | bytes 33280 | tf_op jit(solution)/shard_map/all_gather | solution.py:65
  194.1 1.3 broadcast_compare_fusion.1
  195.4 4.4 broadcast_compare_fusion
  199.8 0.0 copy-start.2
  199.9 156.8 %all-gather.8.cloned.1.call-done = bf16[8192,384]{1,0:T(8,128)(2,1)} async-done(((bf16[128,384]{1,0:T(8,128)(2,1)}), bf16[8192,384]{1,0:T(8,128)(2,1)}) %all-gather.8.cloned.1.call-update) | async-done | bytes 6291472 | tf_op jit(solution)/shard_map/all_gather | solution.py:64
  356.7 8.7 copy.39
  365.3 301.0 %all-gather.6.cloned.1.call-done = bf16[8192,384]{0,1:T(8,128)(2,1)} async-done(((bf16[128,384]{0,1:T(8,128)(2,1)}), bf16[8192,384]{0,1:T(8,128)(2,1)}) %all-gather.6.cloned.1.call-update) | async-done | bytes 6291472 | tf_op jit(solution)/shard_map/all_gather | solution.py:63
  666.4 0.0 copy-done.2
  666.4 10.5 fusion.17
  676.9 7.6 select_reduce_fusion
  684.5 176.8 %all_gather.28 = f32[8192,3]{0,1:T(4,128)S(1)} all-gather(f32[128,3]{0,1:T(4,128)S(1)} %bitcast.77), channel_id=1, replica_groups=mesh['row'=8,'col'=8,'head'=2] {'row','col'}, dimensions={0}, use_global_device_ids=true | all-gather | bytes 99840 | tf_op jit(solution)/shard_map/all_gather | solution.py:101
  861.3 0.0 copy-done.5
  861.3 9.6 fusion.12
  870.9 171.9 %all_gather.30 = f32[8192,3]{0,1:T(4,128)S(1)} all-gather(f32[128,3]{0,1:T(4,128)S(1)} %get-tuple-element.18), channel_id=1, replica_groups=mesh['row'=8,'col'=8,'head'=2] {'row','col'}, dimensions={0}, use_global_device_ids=true | all-gather | bytes 99840 | tf_op jit(solution)/shard_map/all_gather | solution.py:102
  1042.8 2.0 convolution_convert_fusion
  1044.9 12.0 convolution_bitcast_fusion.1
  1056.9 0.0 copy-start.4
  1056.9 9.6 fusion.9
  1066.5 0.0 all-reduce.2.cloned.1.call-update
  1066.5 0.0 all-gather.10.cloned.1.call-done
  1066.5 0.0 copy-done.4
  1066.5 10.2 exponential_select_fusion
  1076.7 252.3 %all-gather.12.cloned.1.call-done = bf16[8192,384]{1,0:T(8,128)(2,1)} async-done(((bf16[128,384]{1,0:T(8,128)(2,1)}), bf16[8192,384]{1,0:T(8,128)(2,1)}) %all-gather.12.cloned.1.call-update) | async-done | bytes 6291472 | tf_op jit(solution)/shard_map/all_gather | solution.py:106
  1329.0 8.7 copy.47
  1337.7 0.0 copy-done.3
  1337.7 10.9 convolution_convert_fusion.1
  1348.7 0.0 copy-start.1
  1348.7 8.5 fusion.6
  1357.2 0.8 copy.51
  1357.9 0.8 copy.52
  1358.7 0.8 copy.53
  1359.4 1.8 copy.70
  (8 shorter events, 0.0 us)
Async XLA Ops:
  7.2 4.2 copy-start
  7.2 349.5 %all-gather.8.cloned.1.call-start = ((), (), s32[]{:S(2)}) async-start(), calls=%async_computation.1 | async-start | bytes 6389760 | tf_op jit(solution)/shard_map/all_gather | solution.py:64
  7.9 658.5 %all-gather.6.cloned.1.call-start = ((), (), s32[]{:S(2)}) async-start(), calls=%async_computation | async-start | bytes 6389760 | tf_op jit(solution)/shard_map/all_gather | solution.py:63
  9.6 1056.9 %all-gather.10.cloned.1.call-start = ((), (), s32[]{:S(2)}) async-start(), calls=%async_computation.3 | async-start | bytes 6389760 | tf_op jit(solution)/shard_map/all_gather | solution.py:105
  11.3 1317.7 %all-gather.12.cloned.1.call-start = ((), (), s32[]{:S(2)}) async-start(), calls=%async_computation.4 | async-start | bytes 6389760 | tf_op jit(solution)/shard_map/all_gather | solution.py:106
  13.6 1345.9 %all-reduce.2.cloned.1.call-start = ((), (), s32[]{:S(2)}) async-start(), calls=%async_computation.2 | async-start | bytes 786432 | tf_op jit(solution)/shard_map/psum | solution.py:97
  14.6 846.7 %copy-start.5 = (bf16[128,384]{0,1:T(8,128)(2,1)}, bf16[128,384]{0,1:T(8,128)(2,1)S(1)}, u32[]{:S(2)}) copy-start(bf16[128,384]{0,1:T(8,128)(2,1)S(1)} %copy.40) | copy-start | bytes 294916
  199.8 466.5 %copy-start.2 = (bf16[128,384]{0,1:T(8,128)(2,1)S(1)}, bf16[128,384]{0,1:T(8,128)(2,1)}, u32[]{:S(2)}) copy-start(bf16[128,384]{0,1:T(8,128)(2,1)} %copy.35) | copy-start | bytes 294916
  1056.9 9.7 copy-start.4
  1076.7 261.0 %copy-start.3 = (bf16[128,384]{0,1:T(8,128)(2,1)S(1)}, bf16[128,384]{0,1:T(8,128)(2,1)}, u32[]{:S(2)}) copy-start(bf16[128,384]{0,1:T(8,128)(2,1)} %copy.48) | copy-start | bytes 294916
  1348.7 8.5 copy-start.6
  1348.7 12.5 copy-start.1
Sparse Core Ops, SparseCore 0:
  9.7 346.9 all-gather.7
  358.8 307.5 all-gather.5
  668.5 314.5 all-gather.9
  985.2 343.7 all-gather.11
  1331.9 21.4 all-reduce.1
where the time goes:
time: 1370 us
  waiting for transfers between devices  711 us (52%)
  blocking collectives  527 us (38%)
  matrix products  75.5 us (6%)
  local copies, waits for them, and re-layouts  27.4 us (2%)
  between operations  13.9 us (1%)
    all_gather x1, waiting for transfers between devices, on_device(): lax.all_gather(key_vectors, ('row', 'col'), axis=0, tiled=True)  301 us
    all_gather x1, waiting for transfers between devices, on_device(): grad_piece = lax.all_gather(grad_attn, ('row', 'col'), axis=0, tiled=True)  252 us
    all_gather x1, blocking collectives, on_device(): lax.all_gather(segment_ids, ('row', 'col'), axis=0, tiled=True)  178 us
    all_gather x1, blocking collectives, on_device(): lax.all_gather(norm_rows, ('row', 'col'), axis=0, tiled=True)  177 us
    all_gather x1, blocking collectives, on_device(): lax.all_gather(delta_rows, ('row', 'col'), axis=0, tiled=True)  172 us
    all_gather x1, waiting for transfers between devices, on_device(): lax.all_gather(value_vectors, ('row', 'col'), axis=0, tiled=True)  157 us
  transfers between devices with their start and end apart: 5, of which 3 were waited for; matrix products, arithmetic and copies ran while one was open for 8% of the time, Pallas kernels for 0%

commit v1 on v0

v1 whole, which is shorter than its diff:
```python
import functools
import math

import jax
import jax.numpy as jnp
from jax import lax
from jax.experimental import pallas as pl
from jax.experimental.pallas import tpu as pltpu
from jax.sharding import PartitionSpec as P

HD = 128
TB = 128
HP = 3
PR = 2 * HP * TB
SR = 16
SCALE = 1.0 / math.sqrt(HD)
C2 = SCALE * math.log2(math.e)
FAR = 128.0
SEGS = 8
VMEM_BYTES = 48 * 1024 * 1024
F32 = jnp.float32
BF16 = jnp.bfloat16


def params():
    return pltpu.CompilerParams(vmem_limit_bytes=VMEM_BYTES)


def dot_nn(a, b):
    return lax.dot_general(a, b, (((1,), (0,)), ((), ())), preferred_element_type=F32)


def dot_nt(a, b):
    return lax.dot_general(a, b, (((1,), (1,)), ((), ())), preferred_element_type=F32)


def pack_kernel(copies, first_ref, second_ref, seg_ref, out_ref):
    seg = jnp.broadcast_to(seg_ref[...].astype(F32), (SR, TB)).astype(BF16)
    for b in range(copies):
        for h in range(HP):
            cols = slice(h * HD, (h + 1) * HD)
            out_ref[b, h * TB : (h + 1) * TB, :] = first_ref[:, cols]
            out_ref[b, (HP + h) * TB : (HP + h + 1) * TB, :] = second_ref[:, cols]
        out_ref[b, PR : PR + SR, :] = seg


def pack_grad_kernel(copies, query_ref, grad_ref, weight_ref, seg_ref, out_ref):
    seg = jnp.broadcast_to(seg_ref[...].astype(F32), (SR, TB)).astype(BF16)
    g = dot_nt(grad_ref[...], weight_ref[...]).astype(BF16)
    for b in range(copies):
        for h in range(HP):
            cols = slice(h * HD, (h + 1) * HD)
            out_ref[b, h * TB : (h + 1) * TB, :] = query_ref[:, cols]
            out_ref[b, (HP + h) * TB : (HP + h + 1) * TB, :] = g[:, cols]
        out_ref[b, PR : PR + SR, :] = seg


def pack(copies, first, second, seg):
    return pl.pallas_call(
        functools.partial(pack_kernel, copies),
        out_shape=jax.ShapeDtypeStruct((copies, PR + SR, HD), BF16),
        compiler_params=params(),
        name="pack_kv",
    )(first, second, seg)


def pack_grad(copies, query, grad_output, weight, seg):
    return pl.pallas_call(
        functools.partial(pack_grad_kernel, copies),
        out_shape=jax.ShapeDtypeStruct((copies, PR + SR, HD), BF16),
        compiler_params=params(),
        name="pack_qg",
    )(query, grad_output, weight, seg)


def fill_marks(part_ref, mark_ref, for_keys):
    for b in range(part_ref.shape[0]):
        seg = part_ref[b, PR : PR + SR, :][0:1].astype(F32)
        place = lax.broadcasted_iota(jnp.int32, (TB, TB), 0).astype(F32)
        if for_keys:
            marks = jnp.where((place != seg) & (place < SEGS), -FAR, 0.0)
        else:
            marks = jnp.where(place == seg, FAR, 0.0)
        mark_ref[b * TB : (b + 1) * TB, :] = jnp.transpose(marks).astype(BF16)


def head_rows(ref, slot):
    blocks = ref.shape[0]
    return ref[:, slot * TB : (slot + 1) * TB, :].reshape(blocks * TB, HD)


def forward_kernel(qg_ref, kv_ref, out_ref, plain_ref, mixed_ref, stat_ref, qmark, kmark, cols):
    blocks = qg_ref.shape[0]
    fill_marks(qg_ref, qmark, False)
    fill_marks(kv_ref, kmark, True)
    step = 2
    rows = step * TB
    cols[...] = jnp.zeros_like(cols)
    lane = lax.broadcasted_iota(jnp.int32, (rows, HD), 1)
    for h in range(HP):
        k = head_rows(kv_ref, h)
        v = head_rows(kv_ref, HP + h)
        k_marked = jnp.concatenate([k, kmark[...]], axis=1)
        vk = jnp.concatenate([v, k], axis=1)

        @pl.loop(0, blocks // step)
        def _(i):
            here = pl.ds(pl.multiple_of(i * rows, rows), rows)
            q = qg_ref[pl.ds(i * step, step), h * TB : (h + 1) * TB, :].reshape(rows, HD)
            g = qg_ref[pl.ds(i * step, step), (HP + h) * TB : (HP + h + 1) * TB, :].reshape(rows, HD)
            scores = dot_nt(jnp.concatenate([q, qmark[here, :]], axis=1), k_marked)
            top = jnp.max(scores, axis=1, keepdims=True)
            e = jnp.exp2((scores - top) * C2)
            total = jnp.sum(e, axis=1, keepdims=True)
            mix = e * dot_nt(g, v)
            delta = jnp.sum(mix, axis=1, keepdims=True)
            both = dot_nn(e.astype(BF16), vk)
            mixed = dot_nn(mix.astype(BF16), k)
            inv = 1.0 / total
            out_ref[h, here, :] = both[:, :HD] * inv
            plain_ref[h, here, :] = both[:, HD:] * inv
            mixed_ref[h, here, :] = mixed * inv
            norm = top * C2 + jnp.log2(total)
            cols[here, :] += jnp.where(lane == 2 * h, norm, 0.0) + jnp.where(
                lane == 2 * h + 1, delta * inv, 0.0
            )

    stat_ref[...] = jnp.transpose(cols[...])[:8, :]


def forward(qg, kv):
    n = qg.shape[0] * TB
    part = jax.ShapeDtypeStruct((HP, n, HD), F32)
    return pl.pallas_call(
        forward_kernel,
        out_shape=(part, part, part, jax.ShapeDtypeStruct((8, n), F32)),
        scratch_shapes=[
            pltpu.VMEM((n, HD), BF16),
            pltpu.VMEM((kv.shape[0] * TB, HD), BF16),
            pltpu.VMEM((n, HD), F32),
        ],
        compiler_params=params(),
        name="forward_tile",
    )(qg, kv)


def combine_kernel(all_ref, own_ref, out_ref, plain_ref, mixed_ref, send_ref, stat_ref):
    parts = all_ref.shape[0]
    n = own_ref.shape[1]
    blocks = n // TB
    stat_ref[...] = jnp.zeros_like(stat_ref)
    rows = []
    for h in range(HP):
        norms = [all_ref[c, 2 * h : 2 * h + 1, :] for c in range(parts)]
        top = functools.reduce(jnp.maximum, norms)
        norm = top + jnp.log2(sum(jnp.exp2(x - top) for x in norms))
        delta = sum(
            jnp.exp2(x - norm) * all_ref[c, 2 * h + 1 : 2 * h + 2, :] for c, x in enumerate(norms)
        )
        stat_ref[2 * h : 2 * h + 1, :] = norm
        stat_ref[2 * h + 1 : 2 * h + 2, :] = delta
        rows.append(jnp.exp2(own_ref[2 * h : 2 * h + 1, :] - norm))
        rows.append(delta)
    rows.append(jnp.zeros((TB - 2 * HP, n), F32))
    cols = jnp.transpose(jnp.concatenate(rows, axis=0))
    for h in range(HP):
        share = cols[:, 2 * h : 2 * h + 1]
        delta = cols[:, 2 * h + 1 : 2 * h + 2]
        attn = (share * out_ref[h]).astype(BF16)
        grad = (share * SCALE * (mixed_ref[h] - delta * plain_ref[h])).astype(BF16)
        send_ref[:, h * TB : (h + 1) * TB, :] = attn.reshape(blocks, TB, HD)
        send_ref[:, (HP + h) * TB : (HP + h + 1) * TB, :] = grad.reshape(blocks, TB, HD)


def combine(all_stats, own, out, plain, mixed):
    n = own.shape[1]
    return pl.pallas_call(
        combine_kernel,
        out_shape=(
            jax.ShapeDtypeStruct((n // TB, PR, HD), BF16),
            jax.ShapeDtypeStruct((8, n), F32),
        ),
        compiler_params=params(),
        name="combine_rows",
    )(all_stats, own, out, plain, mixed)


def backward_kernel(qg_ref, kv_ref, stat_ref, send_ref, qmark, kmark):
    blocks = kv_ref.shape[0]
    fill_marks(qg_ref, qmark, False)
    fill_marks(kv_ref, kmark, True)
    step = 2
    rows = step * TB
    for h in range(HP):
        q = head_rows(qg_ref, h)
        g = head_rows(qg_ref, HP + h)
        q_marked = jnp.concatenate([q, qmark[...]], axis=1)
        norm = stat_ref[2 * h : 2 * h + 1, :]
        delta = stat_ref[2 * h + 1 : 2 * h + 2, :]

        @pl.loop(0, blocks // step)
        def _(i):
            here = pl.ds(pl.multiple_of(i * rows, rows), rows)
            these = pl.ds(i * step, step)
            k = kv_ref[these, h * TB : (h + 1) * TB, :].reshape(rows, HD)
            v = kv_ref[these, (HP + h) * TB : (HP + h + 1) * TB, :].reshape(rows, HD)
            scores = dot_nt(jnp.concatenate([k, kmark[here, :]], axis=1), q_marked)
            probs = jnp.exp2(scores * C2 - norm)
            change = probs * (dot_nt(v, g) - delta)
            grad_k = dot_nn(change.astype(BF16), q) * SCALE
            grad_v = dot_nn(probs.astype(BF16), g)
            send_ref[these, h * TB : (h + 1) * TB, :] = grad_k.astype(BF16).reshape(step, TB, HD)
            send_ref[these, (HP + h) * TB : (HP + h + 1) * TB, :] = grad_v.astype(BF16).reshape(
                step, TB, HD
            )


def backward(qg, kv, stats):
    blocks = kv.shape[0]
    return pl.pallas_call(
        backward_kernel,
        out_shape=jax.ShapeDtypeStruct((blocks, PR, HD), BF16),
        scratch_shapes=[
            pltpu.VMEM((qg.shape[0] * TB, HD), BF16),
            pltpu.VMEM((blocks * TB, HD), BF16),
        ],
        compiler_params=params(),
        name="backward_tile",
    )(qg, kv, stats)


def sum_kernel(parts_ref, first_ref, second_ref):
    total = parts_ref[0].astype(F32)
    for b in range(1, parts_ref.shape[0]):
        total = total + parts_ref[b].astype(F32)
    total = total.astype(BF16)
    for h in range(HP):
        cols = slice(h * HD, (h + 1) * HD)
        first_ref[:, cols] = total[h * TB : (h + 1) * TB, :]
        second_ref[:, cols] = total[(HP + h) * TB : (HP + h + 1) * TB, :]


def sum_parts(parts, name):
    out = jax.ShapeDtypeStruct((TB, HP * HD), BF16)
    return pl.pallas_call(
        sum_kernel, out_shape=(out, out), compiler_params=params(), name=name
    )(parts)


def project_kernel(own_ref, other_ref, own_weight, other_weight, out_ref):
    out_ref[...] = (
        dot_nn(own_ref[...], own_weight[...]) + dot_nn(other_ref[...], other_weight[...])
    ).astype(BF16)


def project(own, other, own_weight, other_weight):
    return pl.pallas_call(
        project_kernel,
        out_shape=jax.ShapeDtypeStruct((TB, own_weight.shape[1]), BF16),
        compiler_params=params(),
        name="project",
    )(own, other, own_weight, other_weight)


def on_device(n_row, n_col, query, key, value, segment_ids, out_weight, grad_output):
    swap = [(0, 1), (1, 0)]
    seg = segment_ids.reshape(1, TB)
    kv = lax.all_to_all(pack(n_row, key, value, seg), "row", 0, 0)
    other_weight = lax.ppermute(out_weight, "head", swap)
    qg = lax.all_to_all(pack_grad(n_col, query, grad_output, out_weight, seg), "col", 0, 0)
    out, plain, mixed, own = forward(qg, kv)
    all_stats = lax.all_to_all(
        jnp.broadcast_to(own[None], (n_col,) + own.shape), "col", 0, 0
    )
    row_parts, stats = combine(all_stats, own, out, plain, mixed)
    row_parts = lax.all_to_all(row_parts, "col", 0, 0)
    key_parts = lax.all_to_all(backward(qg, kv, stats), "row", 0, 0)
    attn, grad_queries = sum_parts(row_parts, "sum_rows")
    other_attn = lax.ppermute(attn, "head", swap)
    mixed_output = project(attn, other_attn, out_weight, other_weight)
    grad_keys, grad_values = sum_parts(key_parts, "sum_keys")
    return (mixed_output, grad_queries, grad_keys, grad_values)


def solution(mesh):
    tokens = P(("row", "col"))
    heads = P(("row", "col"), "head")
    whole = P(("row", "col"), None)
    return jax.shard_map(
        functools.partial(on_device, mesh.shape["row"], mesh.shape["col"]),
        mesh=mesh,
        in_specs=(heads, heads, heads, tokens, P("head", None), whole),
        out_specs=(whole, heads, heads, heads),
        check_vma=False,
    )
```

time: 1370 us -> 144 us (0.11)
  waiting for transfers between devices: 711 us -> 46.5 us
  blocking collectives: 527 us -> 39.4 us
  matrix products: 75.5 us -> 0 us
  Pallas kernels: 0 us -> 33.3 us
  local copies, waits for them, and re-layouts: 27.4 us -> 7.4 us
  starting transfers between devices: 0.2 us -> 15.7 us
    all_gather x4 -> x0, waiting for transfers between devices: 710 us -> none  [the longest x1 301 us: on_device(): lax.all_gather(key_vectors, ('row', 'col'), axis=0, tiled=True)]
    all_gather x3 -> x0, blocking collectives: 527 us -> none  [the longest x1 178 us: on_device(): lax.all_gather(segment_ids, ('row', 'col'), axis=0, tiled=True)]
    dot_general x9 -> x0, matrix products: 75.5 us -> none  [the longest x2 20.7 us: masked_scores(): jnp.einsum('qhd,khd->hqk', query_part, key_part, preferred_element_type=j...]
    all_to_all x0 -> x3, waiting for transfers between devices: none -> 46.5 us  [the longest x1 23 us: on_device(): lax.all_to_all(pack_grad(n_col, query, grad_output, out_weight, seg), 'co...]
    all_to_all x0 -> x2, blocking collectives: none -> 39.4 us  [the longest x1 26.1 us: on_device(): kv = lax.all_to_all(pack(n_row, key, value, seg), 'row', 0, 0)]
    pallas_call x0 -> x8, Pallas kernels: none -> 33.3 us  [the longest x1 13.1 us: forward(): pl.pallas_call(forward_kernel, out_shape=(part, part, part, jax.ShapeDtyp...]
    all_gather x2 -> x0, local copies, waits for them, and re-layouts: 17.4 us -> none  [the longest x1 8.74 us: on_device(): grad_piece = lax.all_gather(grad_attn, ('row', 'col'), axis=0, tiled=True)]
    all_to_all x0 -> x3, starting transfers between devices: none -> 15.1 us  [the longest x1 7.14 us: on_device(): lax.all_to_all(pack_grad(n_col, query, grad_output, out_weight, seg), 'co...]
  transfers between devices with their start and end apart: 5 -> 5, of which waited for: 3 -> 3; matrix products, arithmetic and copies ran while one was open for 8% -> 0% of each run, Pallas kernels for 0% -> 9%
where the time goes in v1:
time: 144 us; the launch traced here: 143 us
  waiting for transfers between devices  46.5 us (32%)
  blocking collectives  39.4 us (27%)
  Pallas kernels  33.3 us (23%)
  starting transfers between devices  15.7 us (11%)
  local copies, waits for them, and re-layouts  7.4 us (5%)
    all_to_all x1, blocking collectives, on_device(): kv = lax.all_to_all(pack(n_row, key, value, seg), 'row', 0, 0)  26.1 us
    all_to_all x1, waiting for transfers between devices, on_device(): lax.all_to_all(pack_grad(n_col, query, grad_output, out_weight, seg), 'co...  23 us
    all_to_all x1, waiting for transfers between devices, on_device(): key_parts = lax.all_to_all(backward(qg, kv, stats), 'row', 0, 0)  14 us
    all_to_all x1, blocking collectives, on_device(): lax.all_to_all(jnp.broadcast_to(own[None], (n_col,) + own.shape), 'col',...  13.3 us
    pallas_call x1, Pallas kernels, forward(): pl.pallas_call(forward_kernel, out_shape=(part, part, part, jax.ShapeDtyp...  13.1 us
    pallas_call x1, Pallas kernels, backward(): pl.pallas_call(backward_kernel, out_shape=jax.ShapeDtypeStruct((blocks, P...  9.58 us
    all_to_all x1, waiting for transfers between devices, on_device(): row_parts = lax.all_to_all(row_parts, 'col', 0, 0)  9.57 us
    unnamed x28, local copies, waits for them, and re-layouts  7.39 us
  transfers between devices with their start and end apart: 5, of which 3 were waited for; matrix products, arithmetic and copies ran while one was open for 0% of the time, Pallas kernels for 9%

profile of v1, /device:TPU:0, one launch (start us, length us, event | category | flops | bytes accessed | tf_op | source)
XLA Modules:
  0.0 143.1 jit_solution(9950796986236722461)
XLA Ops:
  0.6 0.0 copy-start.4
  0.6 1.3 copy-done.4
  1.9 0.0 copy-start.8
  1.9 1.0 copy-done.8
  2.9 0.0 copy-start.9
  2.9 0.9 copy-done.9
  3.8 0.0 copy-start.12
  3.8 0.7 copy-done.12
  4.4 1.8 %pack_qg.1 = bf16[8,784,128]{2,1,0:T(8,128)(2,1)} custom-call(bf16[128,384]{1,0:T(8,128)(2,1)S(1)} %copy-done.9, bf16[128,1536]{1,0:T(8,128)(2,1)S(1)} %copy-done.8, bf16[384,1536]{1,0:T(8,128)(2,1)S(1)} %copy-done.4, s32[1,128]{1,0:T(1,128)S(1)} %bitcast.1), custom_call_target="tpu_custom_call" | custom-call | tf_op jit(solution)/shard_map/pack_qg/pallas_call | solution.py:68
  6.2 0.0 copy-start.10
  6.2 0.0 copy-start.11
  6.2 0.0 copy-start.13
  6.2 7.1 %all-to-all-start = ((bf16[8,784,128]{2,1,0:T(8,128)(2,1)}), bf16[8,784,128]{2,1,0:T(8,128)(2,1)S(1)}, u32[]{:S(2)}, u32[]{:S(2)}) async-start(bf16[8,784,128]{2,1,0:T(8,128)(2,1)} %pack_qg.1), calls=%async_computation | async-start | bytes 3211264 | tf_op jit(solution)/shard_map/all_to_all | solution.py:270
  13.4 0.0 copy-done.10
  13.4 0.0 copy-done.11
  13.4 0.0 copy-done.13
  13.4 0.2 pack_kv.1
  13.6 23.0 %all-to-all-done.qg_ref = bf16[8,784,128]{2,1,0:T(8,128)(2,1)S(1)} async-done(((bf16[8,784,128]{2,1,0:T(8,128)(2,1)}), bf16[8,784,128]{2,1,0:T(8,128)(2,1)S(1)}, u32[]{:S(2)}, u32[]{:S(2)}) %all-to-all-start) | async-done | bytes 1605664 | tf_op jit(solution)/shard_map/all_to_all | solution.py:270
  36.6 0.0 copy-start
  36.6 26.1 %all_to_all.25.kv_ref = bf16[8,784,128]{2,1,0:T(8,128)(2,1)} all-to-all(bf16[8,784,128]{2,1,0:T(8,128)(2,1)S(1)} %pack_kv.1), channel_id=1, replica_groups=mesh['row'=8,'col'=8,'head'=2] {'row'}, dimensions={0} | all-to-all | bytes 3211264 | tf_op jit(solution)/shard_map/all_to_all | solution.py:268
  62.6 0.0 copy-done
  62.6 13.1 %forward_tile.1 = (f32[3,1024,128]{2,1,0:T(8,128)S(1)}, f32[3,1024,128]{2,1,0:T(8,128)S(1)}, f32[3,1024,128]{2,1,0:T(8,128)S(1)}, f32[8,1024]{1,0:T(8,128)S(1)}) custom-call(bf16[8,784,128]{2,1,0:T(8,128)(2,1)} %copy-done, bf16[8,784,128]{2,1,0:T(8,128)(2,1)} %all_to_all.25.kv_ref), custom_call_target="tpu_custom_call" | custom-call | tf_op jit(solution)/shard_map/forward_tile/pallas_call | solution.py:134
  75.7 0.0 copy-start.6
  75.7 1.2 copy-done.6
  76.9 13.3 %all_to_all.26.all_ref = f32[8,8,1024]{2,1,0:T(8,128)S(1)} all-to-all(f32[8,8,1024]{2,1,0:T(8,128)S(1)} %broadcast_in_dim.2), channel_id=1, replica_groups=mesh['row'=8,'col'=8,'head'=2] {'col'}, dimensions={0} | all-to-all | bytes 524288 | tf_op jit(solution)/shard_map/all_to_all | solution.py:272
  90.2 0.0 copy-start.2
  90.2 3.1 %combine_rows.1 = (bf16[8,768,128]{2,1,0:T(8,128)(2,1)S(1)}, f32[8,1024]{1,0:T(8,128)S(1)}) custom-call(f32[8,8,1024]{2,1,0:T(8,128)S(1)} %all_to_all.26.all_ref, f32[8,1024]{1,0:T(8,128)S(1)} %get-tuple-element.14.own_ref, f32[3,1024,128]{2,1,0:T(8,128)S(1)} %get-tuple-element.15.out_ref, f32[3,1024,128]{2,1,0:T(8,128)S(1)} %get-tuple-element.16.plain_ref, ...), custom_call_target="tpu_custom_call" | custom-call | tf_op jit(solution)/shard_map/combine_rows/pallas_call | solution.py:177
  93.3 0.0 copy-start.7
  93.3 1.2 copy-done.7
  94.5 0.0 copy-start.1
  94.5 4.4 %all-to-all-start.3 = ((bf16[8,768,128]{2,1,0:T(8,128)(2,1)}), bf16[8,768,128]{2,1,0:T(8,128)(2,1)}, u32[]{:S(2)}, u32[]{:S(2)}) async-start(bf16[8,768,128]{2,1,0:T(8,128)(2,1)} %copy-done.7), calls=%async_computation.3 | async-start | bytes 3145728 | tf_op jit(solution)/shard_map/all_to_all | solution.py:276
  98.9 0.0 copy-done.2
  99.0 0.0 copy-done.1
  99.0 9.6 %backward_tile.1 = bf16[8,768,128]{2,1,0:T(8,128)(2,1)S(1)} custom-call(bf16[8,784,128]{2,1,0:T(8,128)(2,1)S(1)} %copy-done.1, bf16[8,784,128]{2,1,0:T(8,128)(2,1)S(1)} %copy-done.2, f32[8,1024]{1,0:T(8,128)S(1)} %get-tuple-element.21.stat_ref), custom_call_target="tpu_custom_call" | custom-call | tf_op jit(solution)/shard_map/backward_tile/pallas_call | solution.py:220
  108.6 0.0 copy-start.3
  108.6 1.2 copy-done.3
  109.7 0.0 copy-start.5
  109.7 9.6 %all-to-all-done.3.parts_ref = bf16[8,768,128]{2,1,0:T(8,128)(2,1)} async-done(((bf16[8,768,128]{2,1,0:T(8,128)(2,1)}), bf16[8,768,128]{2,1,0:T(8,128)(2,1)}, u32[]{:S(2)}, u32[]{:S(2)}) %all-to-all-start.3) | async-done | bytes 1572896 | tf_op jit(solution)/shard_map/all_to_all | solution.py:276
  119.3 3.6 %all-to-all-start.4 = ((bf16[8,768,128]{2,1,0:T(8,128)(2,1)}), bf16[8,768,128]{2,1,0:T(8,128)(2,1)S(1)}, u32[]{:S(2)}, u32[]{:S(2)}) async-start(bf16[8,768,128]{2,1,0:T(8,128)(2,1)} %copy-done.3), calls=%async_computation.4 | async-start | bytes 3145728 | tf_op jit(solution)/shard_map/all_to_all | solution.py:277
  122.9 0.0 copy-done.5
  122.9 0.1 collective-permute-start.1
  123.0 2.2 %sum_rows.1 = (bf16[128,384]{1,0:T(8,128)(2,1)S(1)}, bf16[128,384]{1,0:T(8,128)(2,1)}) custom-call(bf16[8,768,128]{2,1,0:T(8,128)(2,1)} %all-to-all-done.3.parts_ref), custom_call_target="tpu_custom_call" | custom-call | tf_op jit(solution)/shard_map/sum_rows/pallas_call | solution.py:245
  125.1 0.5 collective-permute-start
  125.6 14.0 %all-to-all-done.4.parts_ref = bf16[8,768,128]{2,1,0:T(8,128)(2,1)S(1)} async-done(((bf16[8,768,128]{2,1,0:T(8,128)(2,1)}), bf16[8,768,128]{2,1,0:T(8,128)(2,1)S(1)}, u32[]{:S(2)}, u32[]{:S(2)}) %all-to-all-start.4) | async-done | bytes 1572896 | tf_op jit(solution)/shard_map/all_to_all | solution.py:277
  139.6 0.8 sum_keys.1
  140.4 0.0 collective-permute-done.1.other_weight
  140.5 0.0 collective-permute-done.other_ref
  140.5 2.6 %project.1 = bf16[128,1536]{1,0:T(8,128)(2,1)} custom-call(bf16[128,384]{1,0:T(8,128)(2,1)S(1)} %get-tuple-element.19.own_ref, bf16[128,384]{1,0:T(8,128)(2,1)S(1)} %collective-permute-done.other_ref, bf16[384,1536]{1,0:T(8,128)(2,1)S(1)} %copy-done.5, bf16[384,1536]{1,0:T(8,128)(2,1)} %collective-permute-done.1.other_weight), custom_call_target="tpu_custom_call" | custom-call | tf_op jit(solution)/shard_map/project/pallas_call | solution.py:257
  (1 shorter events, 0.0 us)
Async XLA Ops:
  0.6 1.3 copy-start.4
  1.9 1.0 copy-start.8
  2.9 0.9 copy-start.9
  3.8 0.7 copy-start.12
  6.2 7.2 %copy-start.10 = (bf16[128,384]{1,0:T(8,128)(2,1)S(1)}, bf16[128,384]{1,0:T(8,128)(2,1)}, u32[]{:S(2)}) copy-start(bf16[128,384]{1,0:T(8,128)(2,1)} %first_ref.1) | copy-start | bytes 294916
  6.2 7.2 %copy-start.11 = (bf16[128,384]{1,0:T(8,128)(2,1)S(1)}, bf16[128,384]{1,0:T(8,128)(2,1)}, u32[]{:S(2)}) copy-start(bf16[128,384]{1,0:T(8,128)(2,1)} %second_ref.1) | copy-start | bytes 294916
  6.2 7.2 %copy-start.13 = (s32[128]{0:T(128)S(1)}, s32[128]{0:T(128)}, u32[]{:S(2)}) copy-start(s32[128]{0:T(128)} %param.9) | copy-start | bytes 1540
  6.2 30.4 %all-to-all-start = ((bf16[8,784,128]{2,1,0:T(8,128)(2,1)}), bf16[8,784,128]{2,1,0:T(8,128)(2,1)S(1)}, u32[]{:S(2)}, u32[]{:S(2)}) async-start(bf16[8,784,128]{2,1,0:T(8,128)(2,1)} %pack_qg.1), calls=%async_computation | async-start | bytes 3211264 | tf_op jit(solution)/shard_map/all_to_all | solution.py:270
  36.6 26.1 %copy-start = (bf16[8,784,128]{2,1,0:T(8,128)(2,1)}, bf16[8,784,128]{2,1,0:T(8,128)(2,1)S(1)}, u32[]{:S(2)}) copy-start(bf16[8,784,128]{2,1,0:T(8,128)(2,1)S(1)} %all-to-all-done.qg_ref) | copy-start | bytes 4816900
  75.7 1.2 copy-start.6
  90.2 8.7 %copy-start.2 = (bf16[8,784,128]{2,1,0:T(8,128)(2,1)S(1)}, bf16[8,784,128]{2,1,0:T(8,128)(2,1)}, u32[]{:S(2)}) copy-start(bf16[8,784,128]{2,1,0:T(8,128)(2,1)} %all_to_all.25.kv_ref) | copy-start | bytes 4816900
  93.3 1.2 copy-start.7
  94.5 4.4 %copy-start.1 = (bf16[8,784,128]{2,1,0:T(8,128)(2,1)S(1)}, bf16[8,784,128]{2,1,0:T(8,128)(2,1)}, u32[]{:S(2)}) copy-start(bf16[8,784,128]{2,1,0:T(8,128)(2,1)} %copy-done) | copy-start | bytes 4816900
  94.5 24.8 %all-to-all-start.3 = ((bf16[8,768,128]{2,1,0:T(8,128)(2,1)}), bf16[8,768,128]{2,1,0:T(8,128)(2,1)}, u32[]{:S(2)}, u32[]{:S(2)}) async-start(bf16[8,768,128]{2,1,0:T(8,128)(2,1)} %copy-done.7), calls=%async_computation.3 | async-start | bytes 3145728 | tf_op jit(solution)/shard_map/all_to_all | solution.py:276
  108.6 1.2 copy-start.3
  109.7 13.2 %copy-start.5 = (bf16[384,1536]{1,0:T(8,128)(2,1)S(1)}, bf16[384,1536]{1,0:T(8,128)(2,1)}, u32[]{:S(2)}) copy-start(bf16[384,1536]{1,0:T(8,128)(2,1)} %own_weight.1) | copy-start | bytes 3538948
  119.3 20.3 %all-to-all-start.4 = ((bf16[8,768,128]{2,1,0:T(8,128)(2,1)}), bf16[8,768,128]{2,1,0:T(8,128)(2,1)S(1)}, u32[]{:S(2)}, u32[]{:S(2)}) async-start(bf16[8,768,128]{2,1,0:T(8,128)(2,1)} %copy-done.3), calls=%async_computation.4 | async-start | bytes 3145728 | tf_op jit(solution)/shard_map/all_to_all | solution.py:277
  122.9 17.6 %collective-permute-start.1 = (bf16[384,1536]{1,0:T(8,128)(2,1)S(1)}, bf16[384,1536]{1,0:T(8,128)(2,1)}, u32[]{:S(2)}, u32[]{:S(2)}) collective-permute-start(bf16[384,1536]{1,0:T(8,128)(2,1)S(1)} %copy-done.5), channel_id=1, source_target_pairs={{0,1},{1,0},{2,3},{3,2},{4,5},{5,4},{6,7},{7,6},{8,9},{9,8},{10,11... | collective-permute-start | bytes 3538952 | tf_op jit(solution)/shard_map/ppermute | solution.py:269
  125.1 15.3 %collective-permute-start = (bf16[128,384]{1,0:T(8,128)(2,1)S(1)}, bf16[128,384]{1,0:T(8,128)(2,1)S(1)}, u32[]{:S(2)}, u32[]{:S(2)}) collective-permute-start(bf16[128,384]{1,0:T(8,128)(2,1)S(1)} %get-tuple-element.19.own_ref), channel_id=1, source_target_pairs={{0,1},{1,0},{2,3},{3,2},{4,5},{5,4},{6,7},{7,6},{8,9},{9,8},{10,11... | collective-permute-start | bytes 294920 | tf_op jit(solution)/shard_map/ppermute | solution.py:279

commit v2 on v0

v2 whole, which is shorter than its diff:
```python
import functools
import math

import jax
import jax.numpy as jnp
from jax import lax
from jax.experimental import pallas as pl
from jax.experimental.pallas import tpu as pltpu
from jax.sharding import PartitionSpec as P

HD = 128
TB = 128
HP = 3
PR = 2 * HP * TB
SR = 16
SCALE = 1.0 / math.sqrt(HD)
C2 = SCALE * math.log2(math.e)
FAR = 128.0
SEGS = 8
VMEM_BYTES = 12 * 1024 * 1024
ALL_VMEM = 63_000_000
F32 = jnp.float32
BF16 = jnp.bfloat16
WHOLE = pl.BlockSpec(memory_space=pltpu.VMEM)
ANYWHERE = pl.BlockSpec(memory_space=pl.ANY)


def call(
    kernel, name, out_shape, args, scratch=(), anywhere=0, vmem=VMEM_BYTES, flops=0, moved=0, exps=0
):
    return pl.pallas_call(
        kernel,
        out_shape=out_shape,
        in_specs=[ANYWHERE] * anywhere + [WHOLE] * (len(args) - anywhere),
        out_specs=jax.tree.map(lambda _: WHOLE, out_shape),
        scratch_shapes=list(scratch),
        compiler_params=pltpu.CompilerParams(vmem_limit_bytes=vmem),
        cost_estimate=pl.CostEstimate(flops=flops, bytes_accessed=moved, transcendentals=exps),
        name=name,
    )(*args)


def shape(dims, dtype):
    return jax.ShapeDtypeStruct(dims, dtype)


def dot_nn(a, b):
    return lax.dot_general(a, b, (((1,), (0,)), ((), ())), preferred_element_type=F32)


def dot_nt(a, b):
    return lax.dot_general(a, b, (((1,), (1,)), ((), ())), preferred_element_type=F32)


def write_block(first, second, seg_ref, out_ref):
    for h in range(HP):
        cols = slice(h * HD, (h + 1) * HD)
        out_ref[h * TB : (h + 1) * TB, :] = first[:, cols]
        out_ref[(HP + h) * TB : (HP + h + 1) * TB, :] = second[:, cols]
    out_ref[PR : PR + SR, :] = jnp.broadcast_to(seg_ref[...].astype(F32), (SR, TB)).astype(BF16)


def fetch(sources, held, sems):
    copies = [pltpu.make_async_copy(a, b, sems.at[i]) for i, (a, b) in enumerate(zip(sources, held))]
    for copy in copies:
        copy.start()
    for copy in copies:
        copy.wait()


def pack_kernel(*refs):
    sources, (out_ref, *held, sems) = refs[1:4], refs[4:]
    fetch(sources, held, sems)
    seg, first, second = held
    write_block(first[...], second[...], seg, out_ref)


def pack_grad_kernel(*refs):
    sources, (out_ref, *held, sems) = refs[:4], refs[4:]
    fetch(sources, held, sems)
    seg, query, grad, weight = held
    write_block(query[...], dot_nt(grad[...], weight[...]).astype(BF16), seg, out_ref)


def pack(kernel, name, later, *args):
    block = shape((PR + SR, HD), BF16)
    scratch = [pltpu.VMEM(a.shape, a.dtype) for a in args] + [pltpu.SemaphoreType.DMA((len(args),))]
    args = later + args
    return call(kernel, name, block, args, scratch, len(args), ALL_VMEM, moved=2**22)


def stack_kernel(*refs):
    *sources, out_ref, sems = refs
    sources = sources[-out_ref.shape[0] :]
    fetch(sources, [out_ref.at[i] for i in range(len(sources))], sems)


def stack(name, blocks, later=()):
    out = shape((len(blocks),) + blocks[0].shape, BF16)
    return pl.pallas_call(
        stack_kernel,
        out_shape=out,
        in_specs=[ANYWHERE] * (len(later) + len(blocks)),
        out_specs=ANYWHERE,
        scratch_shapes=[pltpu.SemaphoreType.DMA((len(blocks),))],
        compiler_params=pltpu.CompilerParams(vmem_limit_bytes=VMEM_BYTES),
        cost_estimate=pl.CostEstimate(flops=0, bytes_accessed=2 * out.size * 2, transcendentals=0),
        name=name,
    )(*later, *blocks)


def fill_marks(part_refs, mark_ref, for_keys):
    place = lax.broadcasted_iota(jnp.int32, (TB, TB), 0).astype(F32)
    start = 0
    for part_ref in part_refs:
        for b in range(part_ref.shape[0]):
            seg = part_ref[b, PR : PR + SR, :][0:1].astype(F32)
            if for_keys:
                marks = jnp.where((place != seg) & (place < SEGS), -FAR, 0.0)
            else:
                marks = jnp.where(place == seg, FAR, 0.0)
            mark_ref[start : start + TB, :] = jnp.transpose(marks).astype(BF16)
            start += TB


def head_rows(refs, slot):
    return jnp.concatenate(
        [
            ref[:, slot * TB : (slot + 1) * TB, :].reshape(ref.shape[0] * TB, HD)
            for ref in refs
        ],
        axis=0,
    )


STEP = 2
ROWS = STEP * TB


def merge(first, second):
    top = jnp.maximum(first[0], second[0])
    norm = top + jnp.log2(jnp.exp2(first[0] - top) + jnp.exp2(second[0] - top))
    delta = jnp.exp2(first[0] - norm) * first[1] + jnp.exp2(second[0] - norm) * second[1]
    return norm, delta


def chunk_rows(ref, slot):
    return ref[:, slot * TB : (slot + 1) * TB, :].reshape(ROWS, HD)


def stats_kernel(count, first, *refs):
    chunks, (ko_ref, kx_ref), refs = refs[:count], refs[count : count + 2], refs[count + 2 :]
    kmark, (cols_ref, rows_ref, qmark) = (refs[3], refs[:3]) if first else (refs[0], refs[1:])
    if first:
        fill_marks((ko_ref, kx_ref), kmark, True)
    fill_marks(chunks, qmark, False)
    cols_ref[...] = jnp.zeros_like(cols_ref)
    lane = lax.broadcasted_iota(jnp.int32, (ROWS, HD), 1)
    for h in range(HP):
        k = jnp.concatenate([head_rows((ko_ref, kx_ref), h), kmark[...]], axis=1)
        v = head_rows((ko_ref, kx_ref), HP + h)
        for i, chunk in enumerate(chunks):
            here = slice(i * ROWS, (i + 1) * ROWS)
            q, g = chunk_rows(chunk, h), chunk_rows(chunk, HP + h)
            scores = dot_nt(jnp.concatenate([q, qmark[here, :]], axis=1), k)
            top = jnp.max(scores, axis=1, keepdims=True)
            e = jnp.exp2((scores - top) * C2)
            total = jnp.sum(e, axis=1, keepdims=True)
            delta = jnp.sum(e * dot_nt(g, v), axis=1, keepdims=True) / total
            norm = top * C2 + jnp.log2(total)
            cols_ref[here, :] += jnp.where(lane == 2 * h, norm, 0.0) + jnp.where(
                lane == 2 * h + 1, delta, 0.0
            )
    rows_ref[...] = jnp.transpose(cols_ref[...])[:8, :]


def stats(name, chunks, ko, kx, kmark=None):
    n, m = len(chunks) * ROWS, 2 * ko.shape[0] * TB
    out = (shape((n, HD), F32), shape((8, n), F32), shape((n, HD), BF16))
    args = tuple(chunks) + (ko, kx)
    if kmark is None:
        out += (shape((m, HD), BF16),)
    else:
        args += (kmark,)
    return call(
        functools.partial(stats_kernel, len(chunks), kmark is None), name, out, args,
        flops=12 * n * m * HP * HD, moved=2**22, exps=n * m * HP,
    )


def forward_kernel(count, *refs):
    chunks, (ko_ref, kx_ref, kmark), refs = refs[:count], refs[count : count + 3], refs[count + 3 :]
    qmarks, cols, out_ref = refs[:count], refs[count : 2 * count], refs[-1]
    for h in range(HP):
        k = head_rows((ko_ref, kx_ref), h)
        v = head_rows((ko_ref, kx_ref), HP + h)
        k_marked = jnp.concatenate([k, kmark[...]], axis=1)
        vk = jnp.concatenate([v, k], axis=1)
        for i, (chunk, (qmark, at), (norm, _)) in enumerate(zip(chunks, qmarks, cols)):
            here, there = slice(i * ROWS, (i + 1) * ROWS), slice(at, at + ROWS)
            q, g = chunk_rows(chunk, h), chunk_rows(chunk, HP + h)
            scores = dot_nt(jnp.concatenate([q, qmark[there, :]], axis=1), k_marked)
            p = jnp.exp2(scores * C2 - norm[there, 2 * h : 2 * h + 1])
            mix = p * dot_nt(g, v)
            out_ref[h, here, : 2 * HD] = dot_nn(p.astype(BF16), vk)
            out_ref[h, here, 2 * HD :] = dot_nn(mix.astype(BF16), k)


def forward(name, chunks, ko, kx, kmark, qmarks, cols):
    n, m = len(chunks) * ROWS, 2 * ko.shape[0] * TB
    starts = [at for _, at in qmarks]

    def kernel(*refs):
        fixed = len(chunks) + 3
        marks = list(zip(refs[fixed : fixed + len(chunks)], starts))
        norms = list(zip(refs[fixed + len(chunks) : -1], starts))
        forward_kernel(len(chunks), *refs[:fixed], *marks, *norms, refs[-1])

    args = tuple(chunks) + (ko, kx, kmark) + tuple(a for a, _ in qmarks) + tuple(a for a, _ in cols)
    return call(
        kernel, name, shape((HP, n, 3 * HD), F32), args,
        flops=12 * n * m * 2 * HD * HP, moved=8 * 2**20, exps=n * m * HP,
    )


def pair_kernel(later_ref, *refs):
    del later_ref
    mine_ref, got_ref, out_ref = refs
    out_ref[...] = jnp.zeros_like(out_ref)
    for block in range(mine_ref.shape[1] // TB):
        mine = slice(block * TB, (block + 1) * TB)
        theirs = slice((block ^ 1) * TB, ((block ^ 1) + 1) * TB)
        for r in range(0, 2 * HP, 2):
            norm, delta = merge(
                (mine_ref[r : r + 1, mine], mine_ref[r + 1 : r + 2, mine]),
                (got_ref[r : r + 1, theirs], got_ref[r + 1 : r + 2, theirs]),
            )
            out_ref[r : r + 1, mine] = norm
            out_ref[r + 1 : r + 2, mine] = delta


def pair(later, mine, got):
    return call(pair_kernel, "pair_rows", shape(mine.shape, F32), (later, mine, got), anywhere=1)


def combine_kernel(steps, *refs):
    chunks = len(steps)
    members, refs = refs[:chunks], refs[chunks:]
    rows_ref, outs, sends, stat_ref = refs[0], refs[1:3], refs[3:-1], refs[-1]
    stat_ref[...] = jnp.zeros_like(stat_ref)
    for i, mine in enumerate(steps):
        here = slice(i * ROWS, (i + 1) * ROWS)
        found = []
        for member, step in zip(members, steps):
            at = steps.index((mine - step) % chunks) * ROWS
            found.append(member[:, at : at + ROWS])
        for r in range(0, 2 * HP, 2):
            norm, delta = functools.reduce(merge, [(f[r : r + 1], f[r + 1 : r + 2]) for f in found])
            stat_ref[r : r + 1, here] = norm
            stat_ref[r + 1 : r + 2, here] = delta
    rows = []
    for r in range(0, 2 * HP, 2):
        rows.append(jnp.exp2(rows_ref[r : r + 1, :] - stat_ref[r : r + 1, :]))
        rows.append(stat_ref[r + 1 : r + 2, :])
    rows.append(jnp.zeros((TB - 2 * HP, chunks * ROWS), F32))
    cols = jnp.transpose(jnp.concatenate(rows, axis=0))
    for i, send_ref in enumerate(sends):
        here = slice(i * ROWS, (i + 1) * ROWS)
        out_ref, start = outs[i // (chunks // 2)], i % (chunks // 2) * ROWS
        there = slice(start, start + ROWS)
        for h in range(HP):
            share = cols[here, 2 * h : 2 * h + 1]
            delta = cols[here, 2 * h + 1 : 2 * h + 2]
            attn, plain, mixed = (out_ref[h, there, c * HD : (c + 1) * HD] for c in range(3))
            attn = (share * attn).astype(BF16)
            grad = (share * SCALE * (mixed - delta * plain)).astype(BF16)
            send_ref[:, h * TB : (h + 1) * TB, :] = attn.reshape(STEP, TB, HD)
            send_ref[:, (HP + h) * TB : (HP + h + 1) * TB, :] = grad.reshape(STEP, TB, HD)


def combine(steps, *args):
    rows = args[0].shape[1]
    send = shape((STEP, PR, HD), BF16)
    return call(
        functools.partial(combine_kernel, steps), "combine_rows",
        (send,) * len(steps) + (shape((8, rows), F32),), args,
        flops=5 * rows * HD * HP * 2, moved=6 * 2**20,
    )


def backward_kernel(count, first, k_ref, *refs):
    chunks, (kmark, *qmarks, stat_ref, send_ref) = refs[:count], refs[count:]
    marks = jnp.concatenate([m[...] for m in qmarks], axis=0)
    for h in range(HP):
        q = head_rows(chunks, h)
        g = head_rows(chunks, HP + h)
        q_marked = jnp.concatenate([q, marks], axis=1)
        norm, delta = (stat_ref[r : r + 1, :] for r in (2 * h, 2 * h + 1))

        for i in range(k_ref.shape[0] // STEP):
            here = slice(first * TB + i * ROWS, first * TB + (i + 1) * ROWS)
            these = slice(i * STEP, (i + 1) * STEP)
            k, v = (
                k_ref[these, slot * TB : (slot + 1) * TB, :].reshape(ROWS, HD)
                for slot in (h, HP + h)
            )
            scores = dot_nt(jnp.concatenate([k, kmark[here, :]], axis=1), q_marked)
            probs = jnp.exp2(scores * C2 - norm)
            change = probs * (dot_nt(v, g) - delta)
            grad_k = (dot_nn(change.astype(BF16), q) * SCALE).astype(BF16)
            grad_v = dot_nn(probs.astype(BF16), g).astype(BF16)
            send_ref[these, h * TB : (h + 1) * TB, :] = grad_k.reshape(STEP, TB, HD)
            send_ref[these, (HP + h) * TB : (HP + h + 1) * TB, :] = grad_v.reshape(STEP, TB, HD)


def backward(name, first, k, chunks, kmark, qmarks, stat):
    n, m = len(chunks) * ROWS, k.shape[0] * TB
    args = (k, *chunks, kmark, *qmarks, stat)
    return call(
        functools.partial(backward_kernel, len(chunks), first), name,
        shape((k.shape[0], PR, HD), BF16), args,
        flops=10 * n * m * 2 * HD * HP, moved=8 * 2**20, exps=n * m * HP,
    )


def partner_sum_kernel(later_ref, *refs):
    del later_ref
    *parts, all_ref, attn_ref, own_ref = refs
    total = sum(ref[1].astype(F32) for ref in parts).astype(BF16)
    all_ref[...] = total
    attn_ref[...] = total[: PR // 2]
    own_ref[...] = sum(ref[0, : PR // 2, :].astype(F32) for ref in parts).astype(BF16)


def partner_sum(parts, later):
    out = (shape((PR, HD), BF16), shape((PR // 2, HD), BF16), shape((PR // 2, HD), BF16))
    return call(
        partner_sum_kernel, "sum_partner", out, (later, *parts), anywhere=1,
        moved=len(parts) * PR * HD * 2,
    )


def add_kernel(later_ref, own_ref, got_ref, *out_refs):
    del later_ref
    for j, out_ref in enumerate(out_refs):
        out_ref[...] = (own_ref[j].astype(F32) + got_ref[j].astype(F32)).astype(BF16)


def add(own, got, name, later):
    out = tuple(shape(own.shape[1:], BF16) for _ in range(own.shape[0]))
    args = (later, own, got)
    return call(add_kernel, name, out, args, anywhere=1, flops=own.size, moved=6 * own.size)


def sum_kernel(*refs):
    parts, (first_ref, second_ref) = refs[:-2], refs[-2:]
    parts = [part[0] if len(part.shape) == 3 else part[...] for part in parts]
    total = sum(part.astype(F32) for part in parts).astype(BF16)
    for h in range(HP):
        cols = slice(h * HD, (h + 1) * HD)
        first_ref[:, cols] = total[h * TB : (h + 1) * TB, :]
        second_ref[:, cols] = total[(HP + h) * TB : (HP + h + 1) * TB, :]


def sum_parts(parts, name):
    out = shape((TB, HP * HD), BF16)
    size = sum(p.size for p in parts)
    return call(sum_kernel, name, (out, out), tuple(parts), flops=size, moved=2 * size)


def finish_kernel(*refs):
    *parts, got, other_own, other_got, weight, other_weight, out_ref, query_ref = refs
    total = sum(part[0].astype(F32) for part in parts) + got[...].astype(F32)
    total = total.astype(BF16)
    other = (other_own[...].astype(F32) + other_got[...].astype(F32)).astype(BF16)
    for h in range(HP):
        query_ref[:, h * HD : (h + 1) * HD] = total[(HP + h) * TB : (HP + h + 1) * TB, :]
    attn, other = (
        jnp.concatenate([rows[h * TB : (h + 1) * TB, :] for h in range(HP)], axis=1)
        for rows in (total, other)
    )
    out_ref[...] = (dot_nn(attn, weight[...]) + dot_nn(other, other_weight[...])).astype(BF16)


def finish(parts, got, other_own, other_got, weight, other_weight):
    out = (shape((TB, weight.shape[1]), BF16), shape((TB, HP * HD), BF16))
    args = (*parts, got, other_own, other_got, weight, other_weight)
    return call(
        finish_kernel, "finish_rows", out, args,
        flops=4 * TB * weight.size, moved=4 * weight.size,
    )


class Places:
    def __init__(self, n_row, n_col):
        self.n_row, self.n_col = n_row, n_col
        self.ny, self.nz = n_col // 2, n_row // 2

    def of(self, index):
        row, col = divmod(index, self.n_col)
        low, z = divmod(row, self.nz)
        y, high = divmod(col, 2)
        return high, low, y, z

    def index(self, high, low, y, z):
        return (low * self.nz + z) * self.n_col + y * 2 + high

    def send(self, array, move, turn=0):
        pairs = []
        for i in range(self.n_row * self.n_col):
            for core in range(2):
                target = self.index(*move(core, *self.of(i)))
                pairs.append((2 * i + core, 2 * target + (core ^ turn)))
        return lax.ppermute(array, ("row", "col", "head"), pairs)

    def along_y(self, array, by):
        return self.send(array, lambda core, high, low, y, z: (high, low, (y + by) % self.ny, z))

    def along_z(self, array, by):
        return self.send(array, lambda core, high, low, y, z: (high, low, y, (z + by) % self.nz))

    def query_partner(self, array):
        return self.send(array, lambda core, high, low, y, z: (high ^ 1 ^ core, low ^ 1, y, z))

    def query_partner_other_core(self, array):
        return self.send(
            array, lambda core, high, low, y, z: (high ^ 1 ^ core, low ^ 1, y, z), 1
        )

    def key_partner(self, array):
        return self.send(array, lambda core, high, low, y, z: (high ^ core, low ^ 1, y, z))


def shifts(n):
    return [0] + sorted(range(1, n), key=lambda d: min(d, n - d))


def on_device(places, query, key, value, segment_ids, out_weight, grad_output):
    swap = [(0, 1), (1, 0)]
    y_shifts, z_shifts = shifts(places.ny), shifts(places.nz)
    seg = segment_ids.reshape(1, TB)

    qg = pack(pack_grad_kernel, "pack_qg", (), seg, query, grad_output, out_weight)
    kv = pack(pack_kernel, "pack_kv", (qg,), seg, key, value)
    pair0 = stack("stack_qg", [qg, places.query_partner(qg)])
    chunks = [pair0] + [places.along_y(pair0, d) for d in y_shifts[1:]]
    ko = stack("stack_kv", [kv] + [places.along_z(kv, d) for d in z_shifts[1:]], (pair0,))
    kx = places.key_partner(ko)
    other_weight = lax.ppermute(out_weight, "head", swap)

    count = len(chunks)
    parts, marked = [], []
    kmark = None
    for name, some in (("first", range(0, 1)), ("near", range(1, count - 1)), ("last", [count - 1])):
        if len(some) == 0:
            continue
        cols, rows, qmark, *made = stats("stats_" + name, [chunks[i] for i in some], ko, kx, kmark)
        kmark = made[0] if made else kmark
        parts.append(rows)
        marked.append(qmark)
        if name == "first":
            where = []
        where += [((qmark, j * ROWS), (cols, j * ROWS)) for j in range(len(some))]
    rows = jnp.concatenate(parts, axis=1)
    got = places.query_partner(rows)
    outs = []
    for name, some in (
        ("forward_near", range(count // 2)), ("forward_far", range(count // 2, count))
    ):
        if outs:
            pair_rows = pair(outs[0], rows, got)
            all_rows = [pair_rows] + [places.along_y(pair_rows, d) for d in y_shifts[1:]]
        outs.append(
            forward(
                name, [chunks[i] for i in some], ko, kx, kmark,
                [where[i][0] for i in some], [where[i][1] for i in some],
            )
        )
    *sends, stat = combine(y_shifts, *all_rows, rows, *outs)

    row_parts = [sends[0]] + [
        places.along_y(part, -d) for part, d in zip(sends[1:], y_shifts[1:])
    ]
    key_partner = backward("backward_partner", places.nz, kx, chunks, kmark, marked, stat)
    key_got = places.key_partner(key_partner)
    key_own = backward("backward_own", 0, ko, chunks, kmark, marked, stat)

    key_parts = add(key_own, key_got, "add_keys", stat)
    key_parts = [key_parts[0]] + [
        places.along_z(part, -d) for part, d in zip(key_parts[1:], z_shifts[1:])
    ]
    partner_rows, partner_attn, own_attn = partner_sum(row_parts, key_parts[0])
    mixed_output, grad_queries = finish(
        row_parts,
        places.query_partner(partner_rows),
        lax.ppermute(own_attn, "head", swap),
        places.query_partner_other_core(partner_attn),
        out_weight,
        other_weight,
    )
    grad_keys, grad_values = sum_parts(key_parts, "sum_keys")
    return (mixed_output, grad_queries, grad_keys, grad_values)


def solution(mesh):
    tokens = P(("row", "col"))
    heads = P(("row", "col"), "head")
    whole = P(("row", "col"), None)
    places = Places(mesh.shape["row"], mesh.shape["col"])
    return jax.shard_map(
        functools.partial(on_device, places),
        mesh=mesh,
        in_specs=(heads, heads, heads, tokens, P("head", None), whole),
        out_specs=(whole, heads, heads, heads),
        check_vma=False,
    )
```

time: 1370 us -> 99.6 us (0.07)
  the two profiles are of different devices: /device:TPU:0 before, /device:TPU:25 now
where the time goes in v2:
time: 99.6 us; the launch traced here: 99.4 us
  starting transfers between devices  37.3 us (37%)
  Pallas kernels  30.5 us (31%)
  waiting for transfers between devices  28.9 us (29%)
  local copies, waits for them, and re-layouts  1.88 us (2%)
    ppermute x21, waiting for transfers between devices, send(): return lax.ppermute(array, ('row', 'col', 'head'), pairs)  28.9 us
    pallas_call x15, Pallas kernels, call(): pl.pallas_call(kernel, out_shape=out_shape, in_specs=[ANYWHERE] * anywher...  28.9 us
    ppermute x21, starting transfers between devices, send(): return lax.ppermute(array, ('row', 'col', 'head'), pairs)  28 us
    ppermute x1, starting transfers between devices, on_device(): lax.ppermute(own_attn, 'head', swap)  8.54 us
  transfers between devices with their start and end apart: 23, of which 10 were waited for; matrix products, arithmetic and copies ran while one was open for 0% of the time, Pallas kernels for 25%

profile of v2, /device:TPU:25, one launch (start us, length us, event | category | flops | bytes accessed | tf_op | source)
XLA Modules:
  0.0 99.4 jit_solution(8351941988637407967)
XLA Ops:
  0.6 2.8 %pack_qg.1.refs_0_ = bf16[784,128]{1,0:T(8,128)(2,1)} custom-call(s32[1,128]{1,0:T(1,128)} %bitcast.1, bf16[128,384]{1,0:T(8,128)(2,1)} %refs_1_.1, bf16[128,1536]{1,0:T(8,128)(2,1)} %refs_2_.2, bf16[384,1536]{1,0:T(8,128)(2,1)} %refs_7_.1), custom_call_target="tpu_custom_call" | custom-call | bytes 4194304 | tf_op jit(solution)/shard_map/pack_qg/pallas_call | solution.py:31
  3.4 1.3 %collective-permute-start = (bf16[784,128]{1,0:T(8,128)(2,1)}, bf16[784,128]{1,0:T(8,128)(2,1)S(1)}, u32[]{:S(2)}, u32[]{:S(2)}) collective-permute-start(bf16[784,128]{1,0:T(8,128)(2,1)} %pack_qg.1.refs_0_), channel_id=1, source_target_pairs={{0,66},{1,65},{2,64},{3,67},{4,70},{5,69},{6,68},{7,71},{8,74},{9,... | collective-permute-start | bytes 602120 | tf_op jit(solution)/shard_map/ppermute | solution.py:414
  4.7 1.7 %pack_kv.1.refs_1_ = bf16[784,128]{1,0:T(8,128)(2,1)} custom-call(bf16[784,128]{1,0:T(8,128)(2,1)} %pack_qg.1.refs_0_, s32[1,128]{1,0:T(1,128)} %bitcast.2, bf16[128,384]{1,0:T(8,128)(2,1)} %refs_2_.3, bf16[128,384]{1,0:T(8,128)(2,1)} %refs_3_.3), custom_call_target="tpu_custom_call" | custom-call | bytes 4194304 | tf_op jit(solution)/shard_map/pack_kv/pallas_call | solution.py:31
  6.4 1.7 %collective-permute-start.2 = (bf16[784,128]{1,0:T(8,128)(2,1)}, bf16[784,128]{1,0:T(8,128)(2,1)S(1)}, u32[]{:S(2)}, u32[]{:S(2)}) collective-permute-start(bf16[784,128]{1,0:T(8,128)(2,1)} %pack_kv.1.refs_1_), channel_id=1, source_target_pairs={{0,16},{1,17},{2,18},{3,19},{4,20},{5,21},{6,22},{7,23},{8,24},{9,... | collective-permute-start | bytes 602120 | tf_op jit(solution)/shard_map/ppermute | solution.py:414
  8.1 2.2 %collective-permute-start.3 = (bf16[784,128]{1,0:T(8,128)(2,1)}, bf16[784,128]{1,0:T(8,128)(2,1)S(1)}, u32[]{:S(2)}, u32[]{:S(2)}) collective-permute-start(bf16[784,128]{1,0:T(8,128)(2,1)} %pack_kv.1.refs_1_), channel_id=1, source_target_pairs={{0,48},{1,49},{2,50},{3,51},{4,52},{5,53},{6,54},{7,55},{8,56},{9,... | collective-permute-start | bytes 602120 | tf_op jit(solution)/shard_map/ppermute | solution.py:414
  10.3 1.2 %collective-permute-start.4 = (bf16[784,128]{1,0:T(8,128)(2,1)}, bf16[784,128]{1,0:T(8,128)(2,1)S(1)}, u32[]{:S(2)}, u32[]{:S(2)}) collective-permute-start(bf16[784,128]{1,0:T(8,128)(2,1)} %pack_kv.1.refs_1_), channel_id=1, source_target_pairs={{0,32},{1,33},{2,34},{3,35},{4,36},{5,37},{6,38},{7,39},{8,40},{9,... | collective-permute-start | bytes 602120 | tf_op jit(solution)/shard_map/ppermute | solution.py:414
  11.5 0.9 copy-done.1
  12.5 0.5 stack_qg.1.refs_0_
  13.0 0.6 collective-permute-done.2.refs_2_
  13.5 0.3 collective-permute-done.3.refs_3_
  13.9 4.5 %collective-permute-done.4.refs_4_ = bf16[784,128]{1,0:T(8,128)(2,1)S(1)} collective-permute-done((bf16[784,128]{1,0:T(8,128)(2,1)}, bf16[784,128]{1,0:T(8,128)(2,1)S(1)}, u32[]{:S(2)}, u32[]{:S(2)}) %collective-permute-start.4) | collective-permute-done | bytes 200736 | tf_op jit(solution)/shard_map/ppermute | solution.py:414
  18.4 0.9 copy-done.2
  19.3 1.0 %stack_kv.1.refs_1_.refs_2_.k_ref = bf16[4,784,128]{2,1,0:T(8,128)(2,1)S(1)} custom-call(bf16[2,784,128]{2,1,0:T(8,128)(2,1)S(1)} %stack_qg.1.refs_0_, bf16[784,128]{1,0:T(8,128)(2,1)S(1)} %copy-done.2, bf16[784,128]{1,0:T(8,128)(2,1)S(1)} %collective-permute-done.2.refs_2_, bf16[784,128]{1,0:T(8,128)(2,1)S(1)} %collective-permute-done.3.refs_3_, ...), custom_call_target="tpu_custom_call" | custom-call | bytes 1605632 | tf_op jit(solution)/shard_map/stack_kv/pallas_call | solution.py:100
  20.4 3.9 %collective-permute-start.5 = (bf16[4,784,128]{2,1,0:T(8,128)(2,1)S(1)}, bf16[4,784,128]{2,1,0:T(8,128)(2,1)S(1)}, u32[]{:S(2)}, u32[]{:S(2)}) collective-permute-start(bf16[4,784,128]{2,1,0:T(8,128)(2,1)S(1)} %stack_kv.1.refs_1_.refs_2_.k_ref), channel_id=1, source_target_pairs={{0,64},{1,67},{2,66},{3,65},{4,68},{5,71},{6,70},{7,69},{8,72},{9,... | collective-permute-start | bytes 2408456 | tf_op jit(solution)/shard_map/ppermute | solution.py:414
  24.3 1.5 %collective-permute-start.6 = (bf16[2,784,128]{2,1,0:T(8,128)(2,1)S(1)}, bf16[2,784,128]{2,1,0:T(8,128)(2,1)S(1)}, u32[]{:S(2)}, u32[]{:S(2)}) collective-permute-start(bf16[2,784,128]{2,1,0:T(8,128)(2,1)S(1)} %stack_qg.1.refs_0_), channel_id=1, source_target_pairs={{0,12},{1,13},{2,14},{3,15},{4,0},{5,1},{6,2},{7,3},{8,4},{9,5},{1... | collective-permute-start | bytes 1204232 | tf_op jit(solution)/shard_map/ppermute | solution.py:414
  25.7 0.8 collective-permute-start.19
  26.5 1.0 collective-permute-start.7
  27.4 6.7 %collective-permute-done.5.refs_2_.refs_3_.k_ref = bf16[4,784,128]{2,1,0:T(8,128)(2,1)S(1)} collective-permute-done((bf16[4,784,128]{2,1,0:T(8,128)(2,1)S(1)}, bf16[4,784,128]{2,1,0:T(8,128)(2,1)S(1)}, u32[]{:S(2)}, u32[]{:S(2)}) %collective-permute-start.5) | collective-permute-done | bytes 802848 | tf_op jit(solution)/shard_map/ppermute | solution.py:414
  34.1 1.5 %stats_first.1 = (f32[256,128]{1,0:T(8,128)S(1)}, f32[8,256]{1,0:T(8,128)S(1)}, bf16[256,128]{1,0:T(8,128)(2,1)S(1)}, bf16[1024,128]{1,0:T(8,128)(2,1)S(1)}) custom-call(bf16[2,784,128]{2,1,0:T(8,128)(2,1)S(1)} %stack_qg.1.refs_0_, bf16[4,784,128]{2,1,0:T(8,128)(2,1)S(1)} %stack_kv.1.refs_1_.refs_2_.k_ref, ...), custom_call_target="tpu_custom_call" | custom-call | flops 1207959552 | bytes 4194304 | tf_op jit(solution)/shard_map/stats_first/pallas_call | solution.py:31
  35.7 0.6 collective-permute-done.6.refs_1_.refs_0_.refs_2_
  36.2 2.7 %stats_near.1 = (f32[512,128]{1,0:T(8,128)S(1)}, f32[8,512]{1,0:T(8,128)S(1)}, bf16[512,128]{1,0:T(8,128)(2,1)S(1)}) custom-call(bf16[2,784,128]{2,1,0:T(8,128)(2,1)S(1)} %collective-permute-done.1.refs_0_.refs_1_, bf16[2,784,128]{2,1,0:T(8,128)(2,1)S(1)} %collective-permute-done.6.refs_1_.refs_0_.refs_2_, ...), custom_call_target="tpu_custom_call" | custom-call | flops 2415919104 | bytes 4194304 | tf_op jit(solution)/shard_map/stats_near/pallas_call | solution.py:31
  38.9 5.4 %collective-permute-done.7.refs_0_.refs_1_.refs_3_ = bf16[2,784,128]{2,1,0:T(8,128)(2,1)S(1)} collective-permute-done((bf16[2,784,128]{2,1,0:T(8,128)(2,1)S(1)}, bf16[2,784,128]{2,1,0:T(8,128)(2,1)S(1)}, u32[]{:S(2)}, u32[]{:S(2)}) %collective-permute-start.7) | collective-permute-done | bytes 401440 | tf_op jit(solution)/shard_map/ppermute | solution.py:414
  44.3 1.5 %stats_last.1 = (f32[256,128]{1,0:T(8,128)S(1)}, f32[8,256]{1,0:T(8,128)S(1)}, bf16[256,128]{1,0:T(8,128)(2,1)S(1)}) custom-call(bf16[2,784,128]{2,1,0:T(8,128)(2,1)S(1)} %collective-permute-done.7.refs_0_.refs_1_.refs_3_, bf16[4,784,128]{2,1,0:T(8,128)(2,1)S(1)} %stack_kv.1.refs_1_.refs_2_.k_ref, ...), custom_call_target="tpu_custom_call" | custom-call | flops 1207959552 | bytes 4194304 | tf_op jit(solution)/shard_map/stats_last/pallas_call | solution.py:31
  45.8 0.3 collective-permute-start.8
  46.0 3.6 %forward_near.1.later_ref.refs_5_ = f32[3,512,384]{2,1,0:T(8,128)S(1)} custom-call(bf16[2,784,128]{2,1,0:T(8,128)(2,1)S(1)} %stack_qg.1.refs_0_, bf16[2,784,128]{2,1,0:T(8,128)(2,1)S(1)} %collective-permute-done.1.refs_0_.refs_1_, bf16[4,784,128]{2,1,0:T(8,128)(2,1)S(1)} %stack_kv.1.refs_1_.refs_2_.k_ref, ...), custom_call_target="tpu_custom_call" | custom-call | flops 4831838208 | bytes 8388608 | tf_op jit(solution)/shard_map/forward_near/pallas_call | solution.py:31
  49.7 0.1 pair_rows.1.refs_0_
  49.8 2.9 %collective-permute-start.11 = (f32[8,1024]{1,0:T(8,128)S(1)}, f32[8,1024]{1,0:T(8,128)S(1)}, u32[]{:S(2)}, u32[]{:S(2)}) collective-permute-start(f32[8,1024]{1,0:T(8,128)S(1)} %pair_rows.1.refs_0_), channel_id=1, source_target_pairs={{0,8},{1,9},{2,10},{3,11},{4,12},{5,13},{6,14},{7,15},{8,0},{9,1},... | collective-permute-start | bytes 98312 | tf_op jit(solution)/shard_map/ppermute | solution.py:414
  52.7 1.1 %collective-permute-start.9 = (f32[8,1024]{1,0:T(8,128)S(1)}, f32[8,1024]{1,0:T(8,128)S(1)}, u32[]{:S(2)}, u32[]{:S(2)}) collective-permute-start(f32[8,1024]{1,0:T(8,128)S(1)} %pair_rows.1.refs_0_), channel_id=1, source_target_pairs={{0,4},{1,5},{2,6},{3,7},{4,8},{5,9},{6,10},{7,11},{8,12},{9,13},{1... | collective-permute-start | bytes 98312 | tf_op jit(solution)/shard_map/ppermute | solution.py:414
  53.9 3.6 %forward_far.1.refs_6_ = f32[3,512,384]{2,1,0:T(8,128)S(1)} custom-call(bf16[2,784,128]{2,1,0:T(8,128)(2,1)S(1)} %collective-permute-done.6.refs_1_.refs_0_.refs_2_, bf16[2,784,128]{2,1,0:T(8,128)(2,1)S(1)} %collective-permute-done.7.refs_0_.refs_1_.refs_3_, bf16[4,784,128]{2,1,0:T(8,128)(2,1)S(1)} %stack_kv.1.refs_1_.refs_2_.k_ref, ...), custom_call_target="tpu_custom_call" | custom-call | flops 4831838208 | bytes 8388608 | tf_op jit(solution)/shard_map/forward_far/pallas_call | solution.py:31
  57.5 1.7 %combine_rows.1 = (bf16[2,768,128]{2,1,0:T(8,128)(2,1)S(1)}, bf16[2,768,128]{2,1,0:T(8,128)(2,1)S(1)}, bf16[2,768,128]{2,1,0:T(8,128)(2,1)S(1)}, bf16[2,768,128]{2,1,0:T(8,128)(2,1)S(1)}, f32[8,1024]{1,0:T(8,128)S(1)}) custom-call(f32[8,1024]{1,0:T(8,128)S(1)} %pair_rows.1.refs_0_, f32[8,1024]{1,0:T(8,128)S(1)} %collective-permute-done.9.refs_1_, ...), custom_call_target="tpu_custom_call" | custom-call | flops 3932160 | bytes 6291456 | tf_op jit(solution)/shard_map/combine_rows/pallas_call | solution.py:31
  59.3 3.6 %backward_partner.1 = bf16[4,768,128]{2,1,0:T(8,128)(2,1)S(1)} custom-call(bf16[4,784,128]{2,1,0:T(8,128)(2,1)S(1)} %collective-permute-done.5.refs_2_.refs_3_.k_ref, bf16[2,784,128]{2,1,0:T(8,128)(2,1)S(1)} %stack_qg.1.refs_0_, bf16[2,784,128]{2,1,0:T(8,128)(2,1)S(1)} %collective-permute-done.1.refs_0_.refs_1_, ...), custom_call_target="tpu_custom_call" | custom-call | flops 4026531840 | bytes 8388608 | tf_op jit(solution)/shard_map/backward_partner/pallas_call | solution.py:31
  62.9 0.1 collective-permute-start.15
  63.0 0.4 collective-permute-start.12
  63.4 2.4 %collective-permute-start.13 = (bf16[2,768,128]{2,1,0:T(8,128)(2,1)S(1)}, bf16[2,768,128]{2,1,0:T(8,128)(2,1)S(1)}, u32[]{:S(2)}, u32[]{:S(2)}) collective-permute-start(bf16[2,768,128]{2,1,0:T(8,128)(2,1)S(1)} %get-tuple-element.42), channel_id=1, source_target_pairs={{0,4},{1,5},{2,6},{3,7},{4,8},{5,9},{6,10},{7,11},{8,12},{9,13},{1... | collective-permute-start | bytes 1179656 | tf_op jit(solution)/shard_map/ppermute | solution.py:414
  65.8 3.6 %backward_own.1.own_ref = bf16[4,768,128]{2,1,0:T(8,128)(2,1)S(1)} custom-call(bf16[4,784,128]{2,1,0:T(8,128)(2,1)S(1)} %stack_kv.1.refs_1_.refs_2_.k_ref, bf16[2,784,128]{2,1,0:T(8,128)(2,1)S(1)} %stack_qg.1.refs_0_, bf16[2,784,128]{2,1,0:T(8,128)(2,1)S(1)} %collective-permute-done.1.refs_0_.refs_1_, ...), custom_call_target="tpu_custom_call" | custom-call | flops 4026531840 | bytes 8388608 | tf_op jit(solution)/shard_map/backward_own/pallas_call | solution.py:31
  69.4 5.9 %collective-permute-done.15.got_ref = bf16[4,768,128]{2,1,0:T(8,128)(2,1)S(1)} collective-permute-done((bf16[4,768,128]{2,1,0:T(8,128)(2,1)S(1)}, bf16[4,768,128]{2,1,0:T(8,128)(2,1)S(1)}, u32[]{:S(2)}, u32[]{:S(2)}) %collective-permute-start.15) | collective-permute-done | bytes 786464 | tf_op jit(solution)/shard_map/ppermute | solution.py:414
  75.3 0.2 add_keys.1
  75.6 0.8 collective-permute-done.12.refs_1_
  76.4 0.6 collective-permute-start.21
  77.1 0.6 collective-permute-start.22
  77.7 0.1 sum_partner.1
  77.8 1.2 %collective-permute-start.16 = (bf16[768,128]{1,0:T(8,128)(2,1)S(1)}, bf16[768,128]{1,0:T(8,128)(2,1)S(1)}, u32[]{:S(2)}, u32[]{:S(2)}) collective-permute-start(bf16[768,128]{1,0:T(8,128)(2,1)S(1)} %get-tuple-element.46), channel_id=1, source_target_pairs={{0,66},{1,65},{2,64},{3,67},{4,70},{5,69},{6,68},{7,71},{8,74},{9,... | collective-permute-start | bytes 589832 | tf_op jit(solution)/shard_map/ppermute | solution.py:414
  79.1 1.4 %collective-permute-done.20.refs_1_ = bf16[768,128]{1,0:T(8,128)(2,1)S(1)} collective-permute-done((bf16[768,128]{1,0:T(8,128)(2,1)S(1)}, bf16[768,128]{1,0:T(8,128)(2,1)S(1)}, u32[]{:S(2)}, u32[]{:S(2)}) %collective-permute-start.20) | collective-permute-done | bytes 196640 | tf_op jit(solution)/shard_map/ppermute | solution.py:414
  80.4 8.5 %collective-permute-start.17 = (bf16[384,128]{1,0:T(8,128)(2,1)S(1)}, bf16[384,128]{1,0:T(8,128)(2,1)S(1)}, u32[]{:S(2)}, u32[]{:S(2)}) collective-permute-start(bf16[384,128]{1,0:T(8,128)(2,1)S(1)} %get-tuple-element.47), channel_id=1, source_target_pairs={{0,1},{1,0},{2,3},{3,2},{4,5},{5,4},{6,7},{7,6},{8,9},{9,8},{10,11... | collective-permute-start | bytes 294920 | tf_op jit(solution)/shard_map/ppermute | solution.py:496
  89.0 5.6 %collective-permute-start.18 = (bf16[384,128]{1,0:T(8,128)(2,1)S(1)}, bf16[384,128]{1,0:T(8,128)(2,1)S(1)}, u32[]{:S(2)}, u32[]{:S(2)}) collective-permute-start(bf16[384,128]{1,0:T(8,128)(2,1)S(1)} %get-tuple-element.48), channel_id=1, source_target_pairs={{0,67},{1,64},{2,65},{3,66},{4,71},{5,68},{6,69},{7,70},{8,75},{9,... | collective-permute-start | bytes 294920 | tf_op jit(solution)/shard_map/ppermute | solution.py:414
  94.5 0.8 sum_keys.1
  95.3 2.7 %collective-permute-done.18.refs_6_ = bf16[384,128]{1,0:T(8,128)(2,1)S(1)} collective-permute-done((bf16[384,128]{1,0:T(8,128)(2,1)S(1)}, bf16[384,128]{1,0:T(8,128)(2,1)S(1)}, u32[]{:S(2)}, u32[]{:S(2)}) %collective-permute-start.18) | collective-permute-done | bytes 98336 | tf_op jit(solution)/shard_map/ppermute | solution.py:414
  98.0 1.4 %finish_rows.1 = (bf16[128,1536]{1,0:T(8,128)(2,1)}, bf16[128,384]{1,0:T(8,128)(2,1)}) custom-call(bf16[2,768,128]{2,1,0:T(8,128)(2,1)S(1)} %get-tuple-element.40.refs_0_, bf16[2,768,128]{2,1,0:T(8,128)(2,1)S(1)} %collective-permute-done.12.refs_1_, bf16[2,768,128]{2,1,0:T(8,128)(2,1)S(1)} %collective-permute-done.13.refs_2_, ...), custom_call_target="tpu_custom_call" | custom-call | flops 301989888 | bytes 2359296 | tf_op jit(solution)/shard_map/finish_rows/pallas_call | solution.py:31
  (24 shorter events, 0.2 us)
Async XLA Ops:
  0.6 25.1 %copy-start = (bf16[384,1536]{1,0:T(8,128)(2,1)S(1)}, bf16[384,1536]{1,0:T(8,128)(2,1)}, u32[]{:S(2)}) copy-start(bf16[384,1536]{1,0:T(8,128)(2,1)} %refs_7_.1) | copy-start | bytes 3538948
  3.4 8.1 %collective-permute-start = (bf16[784,128]{1,0:T(8,128)(2,1)}, bf16[784,128]{1,0:T(8,128)(2,1)S(1)}, u32[]{:S(2)}, u32[]{:S(2)}) collective-permute-start(bf16[784,128]{1,0:T(8,128)(2,1)} %pack_qg.1.refs_0_), channel_id=1, source_target_pairs={{0,66},{1,65},{2,64},{3,67},{4,70},{5,69},{6,68},{7,71},{8,74},{9,... | collective-permute-start | bytes 602120 | tf_op jit(solution)/shard_map/ppermute | solution.py:414
  6.4 7.1 %collective-permute-start.2 = (bf16[784,128]{1,0:T(8,128)(2,1)}, bf16[784,128]{1,0:T(8,128)(2,1)S(1)}, u32[]{:S(2)}, u32[]{:S(2)}) collective-permute-start(bf16[784,128]{1,0:T(8,128)(2,1)} %pack_kv.1.refs_1_), channel_id=1, source_target_pairs={{0,16},{1,17},{2,18},{3,19},{4,20},{5,21},{6,22},{7,23},{8,24},{9,... | collective-permute-start | bytes 602120 | tf_op jit(solution)/shard_map/ppermute | solution.py:414
  8.1 5.8 %collective-permute-start.3 = (bf16[784,128]{1,0:T(8,128)(2,1)}, bf16[784,128]{1,0:T(8,128)(2,1)S(1)}, u32[]{:S(2)}, u32[]{:S(2)}) collective-permute-start(bf16[784,128]{1,0:T(8,128)(2,1)} %pack_kv.1.refs_1_), channel_id=1, source_target_pairs={{0,48},{1,49},{2,50},{3,51},{4,52},{5,53},{6,54},{7,55},{8,56},{9,... | collective-permute-start | bytes 602120 | tf_op jit(solution)/shard_map/ppermute | solution.py:414
  10.3 8.1 %collective-permute-start.4 = (bf16[784,128]{1,0:T(8,128)(2,1)}, bf16[784,128]{1,0:T(8,128)(2,1)S(1)}, u32[]{:S(2)}, u32[]{:S(2)}) collective-permute-start(bf16[784,128]{1,0:T(8,128)(2,1)} %pack_kv.1.refs_1_), channel_id=1, source_target_pairs={{0,32},{1,33},{2,34},{3,35},{4,36},{5,37},{6,38},{7,39},{8,40},{9,... | collective-permute-start | bytes 602120 | tf_op jit(solution)/shard_map/ppermute | solution.py:414
  11.5 0.9 copy-start.1
  18.4 0.9 copy-start.2
  20.4 13.7 %collective-permute-start.5 = (bf16[4,784,128]{2,1,0:T(8,128)(2,1)S(1)}, bf16[4,784,128]{2,1,0:T(8,128)(2,1)S(1)}, u32[]{:S(2)}, u32[]{:S(2)}) collective-permute-start(bf16[4,784,128]{2,1,0:T(8,128)(2,1)S(1)} %stack_kv.1.refs_1_.refs_2_.k_ref), channel_id=1, source_target_pairs={{0,64},{1,67},{2,66},{3,65},{4,68},{5,71},{6,70},{7,69},{8,72},{9,... | collective-permute-start | bytes 2408456 | tf_op jit(solution)/shard_map/ppermute | solution.py:414
  24.3 11.4 %collective-permute-start.1 = (bf16[2,784,128]{2,1,0:T(8,128)(2,1)S(1)}, bf16[2,784,128]{2,1,0:T(8,128)(2,1)S(1)}, u32[]{:S(2)}, u32[]{:S(2)}) collective-permute-start(bf16[2,784,128]{2,1,0:T(8,128)(2,1)S(1)} %stack_qg.1.refs_0_), channel_id=1, source_target_pairs={{0,4},{1,5},{2,6},{3,7},{4,8},{5,9},{6,10},{7,11},{8,12},{9,13},{1... | collective-permute-start | bytes 1204232 | tf_op jit(solution)/shard_map/ppermute | solution.py:414
  24.3 12.0 %collective-permute-start.6 = (bf16[2,784,128]{2,1,0:T(8,128)(2,1)S(1)}, bf16[2,784,128]{2,1,0:T(8,128)(2,1)S(1)}, u32[]{:S(2)}, u32[]{:S(2)}) collective-permute-start(bf16[2,784,128]{2,1,0:T(8,128)(2,1)S(1)} %stack_qg.1.refs_0_), channel_id=1, source_target_pairs={{0,12},{1,13},{2,14},{3,15},{4,0},{5,1},{6,2},{7,3},{8,4},{9,5},{1... | collective-permute-start | bytes 1204232 | tf_op jit(solution)/shard_map/ppermute | solution.py:414
  25.7 69.6 %collective-permute-start.19 = (bf16[384,1536]{1,0:T(8,128)(2,1)S(1)}, bf16[384,1536]{1,0:T(8,128)(2,1)S(1)}, u32[]{:S(2)}, u32[]{:S(2)}) collective-permute-start(bf16[384,1536]{1,0:T(8,128)(2,1)S(1)} %copy-done), channel_id=1, source_target_pairs={{0,1},{1,0},{2,3},{3,2},{4,5},{5,4},{6,7},{7,6},{8,9},{9,8},{10,11... | collective-permute-start | bytes 3538952 | tf_op jit(solution)/shard_map/ppermute | solution.py:449
  26.5 17.8 %collective-permute-start.7 = (bf16[2,784,128]{2,1,0:T(8,128)(2,1)S(1)}, bf16[2,784,128]{2,1,0:T(8,128)(2,1)S(1)}, u32[]{:S(2)}, u32[]{:S(2)}) collective-permute-start(bf16[2,784,128]{2,1,0:T(8,128)(2,1)S(1)} %stack_qg.1.refs_0_), channel_id=1, source_target_pairs={{0,8},{1,9},{2,10},{3,11},{4,12},{5,13},{6,14},{7,15},{8,0},{9,1},... | collective-permute-start | bytes 1204232 | tf_op jit(solution)/shard_map/ppermute | solution.py:414
  45.8 3.9 %collective-permute-start.8 = (f32[8,1024]{1,0:T(8,128)S(1)}, f32[8,1024]{1,0:T(8,128)S(1)}, u32[]{:S(2)}, u32[]{:S(2)}) collective-permute-start(f32[8,1024]{1,0:T(8,128)S(1)} %constant_dynamic-update-slice_fusion.refs_0_.refs_4_), channel_id=1, source_target_pairs={{0,66},{1,65},{2,64},{3,67},{4,70},{5,69},{6,68},{7,71},{8,74},{9,... | collective-permute-start | bytes 98312 | tf_op jit(solution)/shard_map/ppermute | solution.py:414
  49.8 7.7 %collective-permute-start.10 = (f32[8,1024]{1,0:T(8,128)S(1)}, f32[8,1024]{1,0:T(8,128)S(1)}, u32[]{:S(2)}, u32[]{:S(2)}) collective-permute-start(f32[8,1024]{1,0:T(8,128)S(1)} %pair_rows.1.refs_0_), channel_id=1, source_target_pairs={{0,12},{1,13},{2,14},{3,15},{4,0},{5,1},{6,2},{7,3},{8,4},{9,5},{1... | collective-permute-start | bytes 98312 | tf_op jit(solution)/shard_map/ppermute | solution.py:414
  49.8 7.7 %collective-permute-start.11 = (f32[8,1024]{1,0:T(8,128)S(1)}, f32[8,1024]{1,0:T(8,128)S(1)}, u32[]{:S(2)}, u32[]{:S(2)}) collective-permute-start(f32[8,1024]{1,0:T(8,128)S(1)} %pair_rows.1.refs_0_), channel_id=1, source_target_pairs={{0,8},{1,9},{2,10},{3,11},{4,12},{5,13},{6,14},{7,15},{8,0},{9,1},... | collective-permute-start | bytes 98312 | tf_op jit(solution)/shard_map/ppermute | solution.py:414
  52.7 4.8 %collective-permute-start.9 = (f32[8,1024]{1,0:T(8,128)S(1)}, f32[8,1024]{1,0:T(8,128)S(1)}, u32[]{:S(2)}, u32[]{:S(2)}) collective-permute-start(f32[8,1024]{1,0:T(8,128)S(1)} %pair_rows.1.refs_0_), channel_id=1, source_target_pairs={{0,4},{1,5},{2,6},{3,7},{4,8},{5,9},{6,10},{7,11},{8,12},{9,13},{1... | collective-permute-start | bytes 98312 | tf_op jit(solution)/shard_map/ppermute | solution.py:414
  62.9 12.4 %collective-permute-start.15 = (bf16[4,768,128]{2,1,0:T(8,128)(2,1)S(1)}, bf16[4,768,128]{2,1,0:T(8,128)(2,1)S(1)}, u32[]{:S(2)}, u32[]{:S(2)}) collective-permute-start(bf16[4,768,128]{2,1,0:T(8,128)(2,1)S(1)} %backward_partner.1), channel_id=1, source_target_pairs={{0,64},{1,67},{2,66},{3,65},{4,68},{5,71},{6,70},{7,69},{8,72},{9,... | collective-permute-start | bytes 2359304 | tf_op jit(solution)/shard_map/ppermute | solution.py:414
  63.0 13.4 %collective-permute-start.12 = (bf16[2,768,128]{2,1,0:T(8,128)(2,1)S(1)}, bf16[2,768,128]{2,1,0:T(8,128)(2,1)S(1)}, u32[]{:S(2)}, u32[]{:S(2)}) collective-permute-start(bf16[2,768,128]{2,1,0:T(8,128)(2,1)S(1)} %get-tuple-element.41), channel_id=1, source_target_pairs={{0,12},{1,13},{2,14},{3,15},{4,0},{5,1},{6,2},{7,3},{8,4},{9,5},{1... | collective-permute-start | bytes 1179656 | tf_op jit(solution)/shard_map/ppermute | solution.py:414
  63.4 13.7 %collective-permute-start.13 = (bf16[2,768,128]{2,1,0:T(8,128)(2,1)S(1)}, bf16[2,768,128]{2,1,0:T(8,128)(2,1)S(1)}, u32[]{:S(2)}, u32[]{:S(2)}) collective-permute-start(bf16[2,768,128]{2,1,0:T(8,128)(2,1)S(1)} %get-tuple-element.42), channel_id=1, source_target_pairs={{0,4},{1,5},{2,6},{3,7},{4,8},{5,9},{6,10},{7,11},{8,12},{9,13},{1... | collective-permute-start | bytes 1179656 | tf_op jit(solution)/shard_map/ppermute | solution.py:414
  65.8 11.9 %collective-permute-start.14 = (bf16[2,768,128]{2,1,0:T(8,128)(2,1)S(1)}, bf16[2,768,128]{2,1,0:T(8,128)(2,1)S(1)}, u32[]{:S(2)}, u32[]{:S(2)}) collective-permute-start(bf16[2,768,128]{2,1,0:T(8,128)(2,1)S(1)} %get-tuple-element.43), channel_id=1, source_target_pairs={{0,8},{1,9},{2,10},{3,11},{4,12},{5,13},{6,14},{7,15},{8,0},{9,1},... | collective-permute-start | bytes 1179656 | tf_op jit(solution)/shard_map/ppermute | solution.py:414
  75.5 4.9 %collective-permute-start.20 = (bf16[768,128]{1,0:T(8,128)(2,1)S(1)}, bf16[768,128]{1,0:T(8,128)(2,1)S(1)}, u32[]{:S(2)}, u32[]{:S(2)}) collective-permute-start(bf16[768,128]{1,0:T(8,128)(2,1)S(1)} %get-tuple-element.51), channel_id=1, source_target_pairs={{0,48},{1,49},{2,50},{3,51},{4,52},{5,53},{6,54},{7,55},{8,56},{9,... | collective-permute-start | bytes 589832 | tf_op jit(solution)/shard_map/ppermute | solution.py:414
  76.4 12.5 %collective-permute-start.21 = (bf16[768,128]{1,0:T(8,128)(2,1)S(1)}, bf16[768,128]{1,0:T(8,128)(2,1)S(1)}, u32[]{:S(2)}, u32[]{:S(2)}) collective-permute-start(bf16[768,128]{1,0:T(8,128)(2,1)S(1)} %get-tuple-element.52), channel_id=1, source_target_pairs={{0,16},{1,17},{2,18},{3,19},{4,20},{5,21},{6,22},{7,23},{8,24},{9,... | collective-permute-start | bytes 589832 | tf_op jit(solution)/shard_map/ppermute | solution.py:414
  77.1 17.4 %collective-permute-start.22 = (bf16[768,128]{1,0:T(8,128)(2,1)S(1)}, bf16[768,128]{1,0:T(8,128)(2,1)S(1)}, u32[]{:S(2)}, u32[]{:S(2)}) collective-permute-start(bf16[768,128]{1,0:T(8,128)(2,1)S(1)} %get-tuple-element.53), channel_id=1, source_target_pairs={{0,32},{1,33},{2,34},{3,35},{4,36},{5,37},{6,38},{7,39},{8,40},{9,... | collective-permute-start | bytes 589832 | tf_op jit(solution)/shard_map/ppermute | solution.py:414
  77.8 20.2 %collective-permute-start.16 = (bf16[768,128]{1,0:T(8,128)(2,1)S(1)}, bf16[768,128]{1,0:T(8,128)(2,1)S(1)}, u32[]{:S(2)}, u32[]{:S(2)}) collective-permute-start(bf16[768,128]{1,0:T(8,128)(2,1)S(1)} %get-tuple-element.46), channel_id=1, source_target_pairs={{0,66},{1,65},{2,64},{3,67},{4,70},{5,69},{6,68},{7,71},{8,74},{9,... | collective-permute-start | bytes 589832 | tf_op jit(solution)/shard_map/ppermute | solution.py:414
  80.4 14.9 %collective-permute-start.17 = (bf16[384,128]{1,0:T(8,128)(2,1)S(1)}, bf16[384,128]{1,0:T(8,128)(2,1)S(1)}, u32[]{:S(2)}, u32[]{:S(2)}) collective-permute-start(bf16[384,128]{1,0:T(8,128)(2,1)S(1)} %get-tuple-element.47), channel_id=1, source_target_pairs={{0,1},{1,0},{2,3},{3,2},{4,5},{5,4},{6,7},{7,6},{8,9},{9,8},{10,11... | collective-permute-start | bytes 294920 | tf_op jit(solution)/shard_map/ppermute | solution.py:496
  89.0 9.1 %collective-permute-start.18 = (bf16[384,128]{1,0:T(8,128)(2,1)S(1)}, bf16[384,128]{1,0:T(8,128)(2,1)S(1)}, u32[]{:S(2)}, u32[]{:S(2)}) collective-permute-start(bf16[384,128]{1,0:T(8,128)(2,1)S(1)} %get-tuple-element.48), channel_id=1, source_target_pairs={{0,67},{1,64},{2,65},{3,66},{4,71},{5,68},{6,69},{7,70},{8,75},{9,... | collective-permute-start | bytes 294920 | tf_op jit(solution)/shard_map/ppermute | solution.py:414

commit v3 on v2

v3 whole, which is shorter than its diff:
```python
import functools
import math

import jax
import jax.numpy as jnp
from jax import lax
from jax.experimental import pallas as pl
from jax.experimental.pallas import tpu as pltpu
from jax.sharding import PartitionSpec as P

HD = 128
TB = 128
HP = 3
PR = 2 * HP * TB
SR = 16
SCALE = 1.0 / math.sqrt(HD)
C2 = SCALE * math.log2(math.e)
FAR = 128.0
SEGS = 8
VMEM_BYTES = 12 * 1024 * 1024
ALL_VMEM = 63_000_000
F32 = jnp.float32
BF16 = jnp.bfloat16
WHOLE = pl.BlockSpec(memory_space=pltpu.VMEM)
ANYWHERE = pl.BlockSpec(memory_space=pl.ANY)


def call(
    kernel, name, out_shape, args, scratch=(), anywhere=0, vmem=VMEM_BYTES, flops=0, moved=0, exps=0
):
    return pl.pallas_call(
        kernel,
        out_shape=out_shape,
        in_specs=[ANYWHERE] * anywhere + [WHOLE] * (len(args) - anywhere),
        out_specs=jax.tree.map(lambda _: WHOLE, out_shape),
        scratch_shapes=list(scratch),
        compiler_params=pltpu.CompilerParams(vmem_limit_bytes=vmem),
        cost_estimate=pl.CostEstimate(flops=flops, bytes_accessed=moved, transcendentals=exps),
        name=name,
    )(*args)


def shape(dims, dtype):
    return jax.ShapeDtypeStruct(dims, dtype)


def dot_nn(a, b):
    return lax.dot_general(a, b, (((1,), (0,)), ((), ())), preferred_element_type=F32)


def dot_nt(a, b):
    return lax.dot_general(a, b, (((1,), (1,)), ((), ())), preferred_element_type=F32)


def write_block(first, second, seg_ref, out_ref):
    for h in range(HP):
        cols = slice(h * HD, (h + 1) * HD)
        out_ref[h * TB : (h + 1) * TB, :] = first[:, cols]
        out_ref[(HP + h) * TB : (HP + h + 1) * TB, :] = second[:, cols]
    out_ref[PR : PR + SR, :] = jnp.broadcast_to(seg_ref[...].astype(F32), (SR, TB)).astype(BF16)


def fetch(sources, held, sems):
    copies = [pltpu.make_async_copy(a, b, sems.at[i]) for i, (a, b) in enumerate(zip(sources, held))]
    for copy in copies:
        copy.start()
    for copy in copies:
        copy.wait()


def pack_kernel(*refs):
    sources, (kv_ref, qg_ref), (*held, sems) = refs[:6], refs[6:8], refs[8:]
    fetch(sources, held, sems)
    seg, key, value, query, grad, weight = held
    write_block(key[...], value[...], seg, kv_ref)
    write_block(query[...], dot_nt(grad[...], weight[...]).astype(BF16), seg, qg_ref)


def pack(*args):
    block = shape((PR + SR, HD), BF16)
    scratch = [pltpu.VMEM(a.shape, a.dtype) for a in args] + [pltpu.SemaphoreType.DMA((len(args),))]
    return call(pack_kernel, "pack", (block, block), args, scratch, len(args), ALL_VMEM)


def gate_kernel(source_ref, *refs):
    del source_ref, refs


def gate(array, *later):
    return pl.pallas_call(
        gate_kernel,
        out_shape=shape(array.shape, array.dtype),
        in_specs=[ANYWHERE] * (1 + len(later)),
        out_specs=ANYWHERE,
        input_output_aliases={0: 0},
        cost_estimate=pl.CostEstimate(flops=0, bytes_accessed=0, transcendentals=0),
        name="gate",
    )(array, *later)


def fill_marks(part_refs, mark_ref, for_keys):
    place = lax.broadcasted_iota(jnp.int32, (TB, TB), 0).astype(F32)
    start = 0
    for part_ref in part_refs:
        for b in range(part_ref.shape[0]):
            seg = part_ref[b, PR : PR + SR, :][0:1].astype(F32)
            if for_keys:
                marks = jnp.where((place != seg) & (place < SEGS), -FAR, 0.0)
            else:
                marks = jnp.where(place == seg, FAR, 0.0)
            mark_ref[start : start + TB, :] = jnp.transpose(marks).astype(BF16)
            start += TB


def head_rows(refs, slot):
    return jnp.concatenate(
        [
            ref[:, slot * TB : (slot + 1) * TB, :].reshape(ref.shape[0] * TB, HD)
            for ref in refs
        ],
        axis=0,
    )


STEP = 2
ROWS = STEP * TB


def merge(first, second):
    top = jnp.maximum(first[0], second[0])
    norm = top + jnp.log2(jnp.exp2(first[0] - top) + jnp.exp2(second[0] - top))
    delta = jnp.exp2(first[0] - norm) * first[1] + jnp.exp2(second[0] - norm) * second[1]
    return norm, delta


def chunk_rows(ref, slot):
    return ref[:, slot * TB : (slot + 1) * TB, :].reshape(ROWS, HD)


def stats_part(tasks, qmark, cols_ref, rows_ref):
    cols_ref[...] = jnp.zeros_like(cols_ref)
    for h in range(HP):
        for key_refs, kmarks, chunks in tasks:
            marks = jnp.concatenate([m[...] for m in kmarks], axis=0)
            k = jnp.concatenate([head_rows(key_refs, h), marks], axis=1)
            v = head_rows(key_refs, HP + h)
            for chunk, i in chunks:
                here = slice(i * ROWS, (i + 1) * ROWS)
                q, g = chunk_rows(chunk, h), chunk_rows(chunk, HP + h)
                scores = dot_nt(jnp.concatenate([q, qmark[here, :]], axis=1), k)
                top = jnp.max(scores, axis=1, keepdims=True)
                e = jnp.exp2((scores - top) * C2)
                cols_ref[here, 3 * h : 3 * h + 1] = top
                cols_ref[here, 3 * h + 1 : 3 * h + 2] = jnp.sum(e, axis=1, keepdims=True)
                cols_ref[here, 3 * h + 2 : 3 * h + 3] = jnp.sum(
                    e * dot_nt(g, v), axis=1, keepdims=True
                )
    found = jnp.transpose(cols_ref[...])
    rows_ref[...] = jnp.zeros_like(rows_ref)
    for h in range(HP):
        top, total, delta = (found[r : r + 1, :] for r in range(3 * h, 3 * h + 3))
        rows_ref[2 * h : 2 * h + 1, :] = top * C2 + jnp.log2(total)
        rows_ref[2 * h + 1 : 2 * h + 2, :] = delta / total


def early_stats_kernel(*refs):
    *chunks, key_ref, rows_ref, qmark, kmark, cols_ref = refs
    fill_marks(chunks, qmark, False)
    fill_marks((key_ref,), kmark, True)
    chunks = [(chunk, i) for i, chunk in enumerate(chunks)]
    stats_part([((key_ref,), (kmark,), chunks)], qmark, cols_ref, rows_ref)


def all_stats_kernel(early, count, *refs):
    chunks, refs = refs[:count], refs[count:]
    ko_ref, kx_ref, kmark_o, early_mark, before_ref, cols_ref, rows_ref, qmark, kmark_x = refs
    fill_marks((kx_ref,), kmark_x, True)
    late = [i for i in range(count) if i not in early]
    for j, i in enumerate(early):
        qmark[i * ROWS : (i + 1) * ROWS, :] = early_mark[j * ROWS : (j + 1) * ROWS, :]
    for i in late:
        fill_marks((chunks[i],), qmark.at[i * ROWS : (i + 1) * ROWS, :], False)
    tasks = [
        ((kx_ref,), (kmark_x,), [(chunks[i], i) for i in early]),
        ((ko_ref, kx_ref), (kmark_o, kmark_x), [(chunks[i], i) for i in late]),
    ]
    stats_part(tasks, qmark, cols_ref, rows_ref)
    for j, i in enumerate(early):
        then, here = slice(j * ROWS, (j + 1) * ROWS), slice(i * ROWS, (i + 1) * ROWS)
        for r in range(0, 2 * HP, 2):
            norm, delta = merge(
                (before_ref[r : r + 1, then], before_ref[r + 1 : r + 2, then]),
                (rows_ref[r : r + 1, here], rows_ref[r + 1 : r + 2, here]),
            )
            rows_ref[r : r + 1, here] = norm
            rows_ref[r + 1 : r + 2, here] = delta
    rows = rows_ref[...]
    rest = jnp.zeros((HD - rows.shape[0], rows.shape[1]), F32)
    cols_ref[...] = jnp.transpose(jnp.concatenate([rows, rest], axis=0))


def early_stats(chunks, key):
    n, m = len(chunks) * ROWS, key.shape[0] * TB
    out = (shape((8, n), F32), shape((n, HD), BF16), shape((m, HD), BF16))
    scratch = [pltpu.VMEM((n, HD), F32)]
    return call(early_stats_kernel, "stats_early", out, (*chunks, key), scratch)


def all_stats(early, chunks, *args):
    n, m = len(chunks) * ROWS, args[1].shape[0] * TB
    out = (shape((n, HD), F32), shape((8, n), F32), shape((n, HD), BF16), shape((m, HD), BF16))
    kernel = functools.partial(all_stats_kernel, early, len(chunks))
    return call(kernel, "stats_all", out, (*chunks, *args))


def forward_kernel(first, *refs):
    *chunks, ko_ref, kx_ref, kmark_o, kmark_x, qmark, norm_ref, out_ref = refs
    marks = jnp.concatenate([kmark_o[...], kmark_x[...]], axis=0)
    for h in range(HP):
        k = head_rows((ko_ref, kx_ref), h)
        v = head_rows((ko_ref, kx_ref), HP + h)
        k_marked = jnp.concatenate([k, marks], axis=1)
        vk = jnp.concatenate([v, k], axis=1)
        for i, chunk in enumerate(chunks):
            here = slice(i * ROWS, (i + 1) * ROWS)
            there = slice((first + i) * ROWS, (first + i + 1) * ROWS)
            q, g = chunk_rows(chunk, h), chunk_rows(chunk, HP + h)
            scores = dot_nt(jnp.concatenate([q, qmark[there, :]], axis=1), k_marked)
            p = jnp.exp2(scores * C2 - norm_ref[there, 2 * h : 2 * h + 1])
            mix = p * dot_nt(g, v)
            out_ref[h, here, : 2 * HD] = dot_nn(p.astype(BF16), vk)
            out_ref[h, here, 2 * HD :] = dot_nn(mix.astype(BF16), k)


def forward(name, first, chunks, *args):
    n, m = len(chunks) * ROWS, 2 * args[0].shape[0] * TB
    return call(
        functools.partial(forward_kernel, first), name, shape((HP, n, 3 * HD), F32),
        (*chunks, *args), flops=12 * n * m * 2 * HD * HP, moved=8 * 2**20, exps=n * m * HP,
    )


def pair_kernel(later_ref, *refs):
    del later_ref
    mine_ref, got_ref, out_ref = refs
    out_ref[...] = jnp.zeros_like(out_ref)
    for block in range(mine_ref.shape[1] // TB):
        mine = slice(block * TB, (block + 1) * TB)
        theirs = slice((block ^ 1) * TB, ((block ^ 1) + 1) * TB)
        for r in range(0, 2 * HP, 2):
            norm, delta = merge(
                (mine_ref[r : r + 1, mine], mine_ref[r + 1 : r + 2, mine]),
                (got_ref[r : r + 1, theirs], got_ref[r + 1 : r + 2, theirs]),
            )
            out_ref[r : r + 1, mine] = norm
            out_ref[r + 1 : r + 2, mine] = delta


def pair(later, mine, got):
    return call(pair_kernel, "pair_rows", shape(mine.shape, F32), (later, mine, got), anywhere=1)


def whole_kernel(steps, later_ref, *refs):
    del later_ref
    *members, stat_ref = refs
    stat_ref[...] = jnp.zeros_like(stat_ref)
    for i, mine in enumerate(steps):
        here = slice(i * ROWS, (i + 1) * ROWS)
        found = []
        for member, step in zip(members, steps):
            at = steps.index((mine - step) % len(steps)) * ROWS
            found.append(member[:, at : at + ROWS])
        for r in range(0, 2 * HP, 2):
            norm, delta = functools.reduce(merge, [(f[r : r + 1], f[r + 1 : r + 2]) for f in found])
            stat_ref[r : r + 1, here] = norm
            stat_ref[r + 1 : r + 2, here] = delta


def whole(steps, members, later):
    out = shape(members[0].shape, F32)
    return call(functools.partial(whole_kernel, steps), "whole_rows", out, (later, *members), anywhere=1)


def share_kernel(chunks, later_ref, stat_ref, rows_ref, *refs):
    del later_ref
    outs, sends, partners = refs[:2], refs[2 : 2 + chunks], refs[2 + chunks :]
    partners = [None] * (chunks - len(partners)) + list(partners)
    rows = []
    for r in range(0, 2 * HP, 2):
        rows.append(jnp.exp2(rows_ref[r : r + 1, :] - stat_ref[r : r + 1, :]))
        rows.append(stat_ref[r + 1 : r + 2, :])
    rows.append(jnp.zeros((TB - 2 * HP, chunks * ROWS), F32))
    cols = jnp.transpose(jnp.concatenate(rows, axis=0))
    for i, send_ref in enumerate(sends):
        here = slice(i * ROWS, (i + 1) * ROWS)
        out_ref, start = outs[i // (chunks // 2)], i % (chunks // 2) * ROWS
        there = slice(start, start + ROWS)
        for h in range(HP):
            share = cols[here, 2 * h : 2 * h + 1]
            delta = cols[here, 2 * h + 1 : 2 * h + 2]
            attn, plain, mixed = (out_ref[h, there, c * HD : (c + 1) * HD] for c in range(3))
            attn = (share * attn).astype(BF16)
            grad = (share * SCALE * (mixed - delta * plain)).astype(BF16)
            for slot, value in ((h, attn), (HP + h, grad)):
                there_rows = slice(slot * TB, (slot + 1) * TB)
                send_ref[0, there_rows, :] = value[:TB]
                if partners[i] is None:
                    send_ref[1, there_rows, :] = value[TB:]
                else:
                    partners[i][there_rows, :] = value[TB:]


def shares(chunks, far, later, *args):
    out = (shape((STEP, PR, HD), BF16),) * (chunks - far) + (shape((1, PR, HD), BF16),) * far
    out += (shape((PR, HD), BF16),) * far
    return call(
        functools.partial(share_kernel, chunks), "share_rows", out, (later, *args), anywhere=1,
        moved=4 * 2**20,
    )


def backward_kernel(count, k_ref, *refs):
    chunks, (kmark, qmark, stat_ref, send_ref) = refs[:count], refs[count:]
    marks = qmark[...]
    for h in range(HP):
        q = head_rows(chunks, h)
        g = head_rows(chunks, HP + h)
        q_marked = jnp.concatenate([q, marks], axis=1)
        norm, delta = (stat_ref[r : r + 1, :] for r in (2 * h, 2 * h + 1))

        for i in range(k_ref.shape[0] // STEP):
            here = slice(i * ROWS, (i + 1) * ROWS)
            these = slice(i * STEP, (i + 1) * STEP)
            k, v = (
                k_ref[these, slot * TB : (slot + 1) * TB, :].reshape(ROWS, HD)
                for slot in (h, HP + h)
            )
            scores = dot_nt(jnp.concatenate([k, kmark[here, :]], axis=1), q_marked)
            probs = jnp.exp2(scores * C2 - norm)
            change = probs * (dot_nt(v, g) - delta)
            grad_k = (dot_nn(change.astype(BF16), q) * SCALE).astype(BF16)
            grad_v = dot_nn(probs.astype(BF16), g).astype(BF16)
            send_ref[these, h * TB : (h + 1) * TB, :] = grad_k.reshape(STEP, TB, HD)
            send_ref[these, (HP + h) * TB : (HP + h + 1) * TB, :] = grad_v.reshape(STEP, TB, HD)


def backward(name, k, chunks, kmark, qmark, stat):
    n, m = len(chunks) * ROWS, k.shape[0] * TB
    args = (k, *chunks, kmark, qmark, stat)
    return call(
        functools.partial(backward_kernel, len(chunks)), name,
        shape((k.shape[0], PR, HD), BF16), args,
        flops=10 * n * m * 2 * HD * HP, moved=8 * 2**20, exps=n * m * HP,
    )


def partner_sum_kernel(later_ref, *refs):
    del later_ref
    refs[-1][...] = sum(ref[1].astype(F32) for ref in refs[:-1]).astype(BF16)


def partner_sum(parts, later):
    return call(
        partner_sum_kernel, "sum_partner", shape((PR, HD), BF16), (later, *parts), anywhere=1,
        moved=len(parts) * PR * HD * 2,
    )


def far_sum_kernel(later_ref, mine_ref, got_ref, out_ref):
    del later_ref
    out_ref[...] = (mine_ref[0].astype(F32) + got_ref[...].astype(F32)).astype(BF16)


def far_sum(mine, got, later):
    args = (later, mine, got)
    return call(far_sum_kernel, "sum_far", shape((PR, HD), BF16), args, anywhere=1)


def add_kernel(later_ref, own_ref, got_ref, *out_refs):
    del later_ref
    for j, out_ref in enumerate(out_refs):
        out_ref[...] = (own_ref[j].astype(F32) + got_ref[j].astype(F32)).astype(BF16)


def add(own, got, name, later):
    out = tuple(shape(own.shape[1:], BF16) for _ in range(own.shape[0]))
    args = (later, own, got)
    return call(add_kernel, name, out, args, anywhere=1, flops=own.size, moved=6 * own.size)


def sum_kernel(skip, *refs):
    parts, (first_ref, second_ref) = refs[skip:-2], refs[-2:]
    parts = [part[0] if len(part.shape) == 3 else part[...] for part in parts]
    total = sum(part.astype(F32) for part in parts).astype(BF16)
    for h in range(HP):
        cols = slice(h * HD, (h + 1) * HD)
        first_ref[:, cols] = total[h * TB : (h + 1) * TB, :]
        second_ref[:, cols] = total[(HP + h) * TB : (HP + h + 1) * TB, :]


def sum_parts(parts, name, later=()):
    out = shape((TB, HP * HD), BF16)
    size = sum(p.size for p in parts)
    kernel, args = functools.partial(sum_kernel, len(later)), (*later, *parts)
    return call(kernel, name, (out, out), args, anywhere=len(later), flops=size, moved=2 * size)


def project_kernel(own_ref, other_ref, own_weight, other_weight, out_ref, token_ref):
    token_ref[...] = jnp.zeros_like(token_ref)
    out_ref[...] = (
        dot_nn(own_ref[...], own_weight[...]) + dot_nn(other_ref[...], other_weight[...])
    ).astype(BF16)


def project(own, other, own_weight, other_weight):
    width = own_weight.shape[1]
    return call(
        project_kernel, "project", (shape((TB, width), BF16), shape((8, HD), F32)),
        (own, other, own_weight, other_weight),
        flops=4 * own.size * width, moved=4 * own_weight.size,
    )


class Places:
    def __init__(self, n_row, n_col):
        self.n_row, self.n_col = n_row, n_col
        self.ny, self.nz = n_col // 2, n_row // 2

    def of(self, index):
        row, col = divmod(index, self.n_col)
        low, z = divmod(row, self.nz)
        y, high = divmod(col, 2)
        return high, low, y, z

    def index(self, high, low, y, z):
        return (low * self.nz + z) * self.n_col + y * 2 + high

    def send(self, array, move):
        pairs = []
        for i in range(self.n_row * self.n_col):
            for core in range(2):
                target = self.index(*move(core, *self.of(i)))
                pairs.append((2 * i + core, 2 * target + core))
        return lax.ppermute(array, ("row", "col", "head"), pairs)

    def along_y(self, array, by):
        return self.send(array, lambda core, high, low, y, z: (high, low, (y + by) % self.ny, z))

    def along_z(self, array, by):
        return self.send(array, lambda core, high, low, y, z: (high, low, y, (z + by) % self.nz))

    def query_partner(self, array):
        return self.send(array, lambda core, high, low, y, z: (high ^ 1 ^ core, low ^ 1, y, z))

    def query_partner_along_y(self, array, by):
        return self.send(
            array,
            lambda core, high, low, y, z: (high ^ 1 ^ core, low ^ 1, (y + by) % self.ny, z),
        )

    def key_partner(self, array):
        return self.send(array, lambda core, high, low, y, z: (high ^ core, low ^ 1, y, z))


def shifts(n):
    return [0] + sorted(range(1, n), key=lambda d: min(d, n - d))


def on_device(places, query, key, value, segment_ids, out_weight, grad_output):
    swap = [(0, 1), (1, 0)]
    y_shifts, z_shifts = shifts(places.ny), shifts(places.nz)
    seg = segment_ids.reshape(1, TB)

    kv, qg = pack(seg, key, value, query, grad_output, out_weight)
    pair0 = jnp.stack([qg, places.query_partner(qg)])
    far = [d for d in y_shifts if 1 < d == places.ny - d]
    near = [d for d in y_shifts[1:] if d not in far]
    chunks = [pair0] + [places.along_y(pair0, d) for d in near]
    far_blocks = [places.along_y(qg, d) for d in far]
    far_partner_blocks = [places.query_partner_along_y(qg, d) for d in far]
    chunks += [jnp.stack(pair) for pair in zip(far_blocks, far_partner_blocks)]
    key_blocks = [places.along_z(kv, d) for d in z_shifts[1:]]
    key_blocks[-1] = gate(key_blocks[-1], pair0, *far_blocks, *far_partner_blocks)
    ko = jnp.stack([kv] + key_blocks)
    kx = places.key_partner(ko)
    other_weight = lax.ppermute(out_weight, "head", swap)

    count = len(chunks)
    early = [i for i in range(count) if not 1 <= i <= len(near)]
    early_rows, early_mark, kmark_o = early_stats([chunks[i] for i in early], ko)
    cols, rows, qmark, kmark_x = all_stats(early, chunks, ko, kx, kmark_o, early_mark, early_rows)
    got = places.query_partner(rows)
    halves = []
    for name, first in (("forward_near", 0), ("forward_far", count // 2)):
        if halves:
            pair_rows = pair(halves[0], rows, got)
            members = [pair_rows] + [places.along_y(pair_rows, d) for d in y_shifts[1:]]
        some = chunks[first : first + count // 2]
        halves.append(forward(name, first, some, ko, kx, kmark_o, kmark_x, qmark, cols))
    stat = whole(y_shifts, members, halves[1])
    key_partner = backward("backward_partner", kx, chunks, kmark_x, qmark, stat)
    key_got = places.key_partner(key_partner)

    made = shares(count, len(far), key_partner, stat, rows, *halves)
    sends, far_partners = made[:count], made[count:]
    row_parts = [sends[0]] + [places.along_y(part, -d) for part, d in zip(sends[1:], near)]
    far_parts = sends[len(row_parts) :]
    far_got = [places.query_partner(far_rows) for far_rows in far_partners]
    key_own = backward("backward_own", ko, chunks, kmark_o, qmark, stat)
    far_parts = [
        places.along_y(far_sum(part, got, key_own), -d)
        for part, got, d in zip(far_parts, far_got, far)
    ]

    key_parts = add(key_own, key_got, "add_keys", stat)
    key_parts = [key_parts[0]] + [
        places.along_z(part, -d) for part, d in zip(key_parts[1:], z_shifts[1:])
    ]
    row_got = places.query_partner(partner_sum(row_parts, key_parts[0]))
    attn, grad_queries = sum_parts(row_parts + far_parts + [row_got], "sum_rows")
    other_attn = lax.ppermute(attn, "head", swap)
    mixed_output, token = project(attn, other_attn, out_weight, other_weight)
    grad_keys, grad_values = sum_parts(key_parts, "sum_keys", (token,))
    return (mixed_output, grad_queries, grad_keys, grad_values)


def solution(mesh):
    tokens = P(("row", "col"))
    heads = P(("row", "col"), "head")
    whole = P(("row", "col"), None)
    places = Places(mesh.shape["row"], mesh.shape["col"])
    return jax.shard_map(
        functools.partial(on_device, places),
        mesh=mesh,
        in_specs=(heads, heads, heads, tokens, P("head", None), whole),
        out_specs=(whole, heads, heads, heads),
        check_vma=False,
    )
```

time: 99.6 us -> 88.7 us (0.89)
  the two profiles are of different devices: /device:TPU:25 before, /device:TPU:0 now
where the time goes in v3:
time: 88.7 us; the launch traced here: 88.4 us
  starting transfers between devices  38.1 us (43%)
  Pallas kernels  27.9 us (31%)
  waiting for transfers between devices  16.3 us (18%)
  other arithmetic  3.9 us (4%)
  local copies, waits for them, and re-layouts  1.38 us (2%)
    ppermute x22, starting transfers between devices, send(): return lax.ppermute(array, ('row', 'col', 'head'), pairs)  38.1 us
    pallas_call x16, Pallas kernels, call(): pl.pallas_call(kernel, out_shape=out_shape, in_specs=[ANYWHERE] * anywher...  27.9 us
    ppermute x22, waiting for transfers between devices, send(): return lax.ppermute(array, ('row', 'col', 'head'), pairs)  15 us
  transfers between devices with their start and end apart: 24, of which 9 were waited for; matrix products, arithmetic and copies ran while one was open for 3% of the time, Pallas kernels for 27%

profile of v3, /device:TPU:0, one launch (start us, length us, event | category | flops | bytes accessed | tf_op | source)
XLA Modules:
  0.0 88.4 jit_solution(12913680946422265587)
XLA Ops:
  0.6 2.9 %pack.1 = (bf16[784,128]{1,0:T(8,128)(2,1)}, bf16[784,128]{1,0:T(8,128)(2,1)}) custom-call(s32[1,128]{1,0:T(1,128)} %bitcast.17, bf16[128,384]{1,0:T(8,128)(2,1)} %refs_1_.1, bf16[128,384]{1,0:T(8,128)(2,1)} %refs_2_.1, bf16[128,384]{1,0:T(8,128)(2,1)} %refs_3_.1, bf16[128,1536]{1,0:T(8,128)(2,1)} %refs_4_.1, bf16[384,1536]{1,0:T(8,128)(2,1)} %own_weight.1), custom_call_target="tpu_custom_call" | custom-call | tf_op jit(solution)/shard_map/pack/pallas_call | solution.py:31
  3.5 2.9 %collective-permute-start.3 = (bf16[784,128]{1,0:T(8,128)(2,1)}, bf16[784,128]{1,0:T(8,128)(2,1)S(1)}, u32[]{:S(2)}, u32[]{:S(2)}) collective-permute-start(bf16[784,128]{1,0:T(8,128)(2,1)} %get-tuple-element.29), channel_id=1, source_target_pairs={{0,66},{1,65},{2,64},{3,67},{4,70},{5,69},{6,68},{7,71},{8,74},{9,... | collective-permute-start | bytes 602120 | tf_op jit(solution)/shard_map/ppermute | solution.py:444
  6.5 3.2 %collective-permute-start.4 = (bf16[784,128]{1,0:T(8,128)(2,1)}, bf16[784,128]{1,0:T(8,128)(2,1)S(1)}, u32[]{:S(2)}, u32[]{:S(2)}) collective-permute-start(bf16[784,128]{1,0:T(8,128)(2,1)} %get-tuple-element.29), channel_id=1, source_target_pairs={{0,8},{1,9},{2,10},{3,11},{4,12},{5,13},{6,14},{7,15},{8,0},{9,1},... | collective-permute-start | bytes 602120 | tf_op jit(solution)/shard_map/ppermute | solution.py:444
  9.7 0.2 collective-permute-start.5
  9.8 4.0 %collective-permute-start.2 = (bf16[784,128]{1,0:T(8,128)(2,1)}, bf16[784,128]{1,0:T(8,128)(2,1)S(1)}, u32[]{:S(2)}, u32[]{:S(2)}) collective-permute-start(bf16[784,128]{1,0:T(8,128)(2,1)} %get-tuple-element.28), channel_id=1, source_target_pairs={{0,32},{1,33},{2,34},{3,35},{4,36},{5,37},{6,38},{7,39},{8,40},{9,... | collective-permute-start | bytes 602120 | tf_op jit(solution)/shard_map/ppermute | solution.py:444
  13.8 1.0 %collective-permute-start = (bf16[784,128]{1,0:T(8,128)(2,1)}, bf16[784,128]{1,0:T(8,128)(2,1)S(1)}, u32[]{:S(2)}, u32[]{:S(2)}) collective-permute-start(bf16[784,128]{1,0:T(8,128)(2,1)} %get-tuple-element.28), channel_id=1, source_target_pairs={{0,16},{1,17},{2,18},{3,19},{4,20},{5,21},{6,22},{7,23},{8,24},{9,... | collective-permute-start | bytes 602120 | tf_op jit(solution)/shard_map/ppermute | solution.py:444
  14.8 2.2 %collective-permute-start.1 = (bf16[784,128]{1,0:T(8,128)(2,1)}, bf16[784,128]{1,0:T(8,128)(2,1)S(1)}, u32[]{:S(2)}, u32[]{:S(2)}) collective-permute-start(bf16[784,128]{1,0:T(8,128)(2,1)} %get-tuple-element.28), channel_id=1, source_target_pairs={{0,48},{1,49},{2,50},{3,51},{4,52},{5,53},{6,54},{7,55},{8,56},{9,... | collective-permute-start | bytes 602120 | tf_op jit(solution)/shard_map/ppermute | solution.py:444
  17.0 1.7 %pad_maximum_fusion.1.refs_0_ = bf16[2,784,128]{2,1,0:T(8,128)(2,1)} fusion(bf16[1,784,128]{2,1,0:T(8,128)(2,1)S(1)} %bitcast.16, bf16[1,784,128]{2,1,0:T(8,128)(2,1)} %bitcast.15), kind=kLoop, calls=%fused_computation.1 | loop fusion | flops 200704 | bytes 802816 | tf_op jit(solution)/shard_map/stack | solution.py:475
  18.8 0.4 collective-permute-done.5.refs_2_
  19.2 0.2 copy-done.3
  19.4 0.5 copy-done.4
  19.9 0.7 copy-done.2
  20.6 1.2 %collective-permute-done = bf16[784,128]{1,0:T(8,128)(2,1)S(1)} collective-permute-done((bf16[784,128]{1,0:T(8,128)(2,1)}, bf16[784,128]{1,0:T(8,128)(2,1)S(1)}, u32[]{:S(2)}, u32[]{:S(2)}) %collective-permute-start) | collective-permute-done | bytes 200736 | tf_op jit(solution)/shard_map/ppermute | solution.py:444
  21.8 0.2 collective-permute-done.1
  22.0 1.1 %pad_maximum_fusion.refs_2_.refs_4_.k_ref = bf16[4,784,128]{2,1,0:T(8,128)(2,1)S(1)} fusion(bf16[1,784,128]{2,1,0:T(8,128)(2,1)} %bitcast.9, bf16[1,784,128]{2,1,0:T(8,128)(2,1)S(1)} %bitcast.14, bf16[1,784,128]{2,1,0:T(8,128)(2,1)S(1)} %bitcast.13, bf16[1,784,128]{2,1,0:T(8,128)(2,1)} %bitcast.12), kind=kLoop, calls=%fused_computation | loop fusion | flops 1204224 | bytes 1605632 | tf_op jit(solution)/shard_map/stack | solution.py:484
  23.1 1.5 %collective-permute-start.6 = (bf16[4,784,128]{2,1,0:T(8,128)(2,1)S(1)}, bf16[4,784,128]{2,1,0:T(8,128)(2,1)S(1)}, u32[]{:S(2)}, u32[]{:S(2)}) collective-permute-start(bf16[4,784,128]{2,1,0:T(8,128)(2,1)S(1)} %pad_maximum_fusion.refs_2_.refs_4_.k_ref), channel_id=1, source_target_pairs={{0,64},{1,67},{2,66},{3,65},{4,68},{5,71},{6,70},{7,69},{8,72},{9,... | collective-permute-start | bytes 2408456 | tf_op jit(solution)/shard_map/ppermute | solution.py:444
  24.7 1.6 %collective-permute-start.7 = (bf16[2,784,128]{2,1,0:T(8,128)(2,1)S(1)}, bf16[2,784,128]{2,1,0:T(8,128)(2,1)S(1)}, u32[]{:S(2)}, u32[]{:S(2)}) collective-permute-start(bf16[2,784,128]{2,1,0:T(8,128)(2,1)S(1)} %copy-done), channel_id=1, source_target_pairs={{0,4},{1,5},{2,6},{3,7},{4,8},{5,9},{6,10},{7,11},{8,12},{9,13},{1... | collective-permute-start | bytes 1204232 | tf_op jit(solution)/shard_map/ppermute | solution.py:444
  26.3 1.7 %collective-permute-start.8 = (bf16[2,784,128]{2,1,0:T(8,128)(2,1)S(1)}, bf16[2,784,128]{2,1,0:T(8,128)(2,1)S(1)}, u32[]{:S(2)}, u32[]{:S(2)}) collective-permute-start(bf16[2,784,128]{2,1,0:T(8,128)(2,1)S(1)} %copy-done), channel_id=1, source_target_pairs={{0,12},{1,13},{2,14},{3,15},{4,0},{5,1},{6,2},{7,3},{8,4},{9,5},{1... | collective-permute-start | bytes 1204232 | tf_op jit(solution)/shard_map/ppermute | solution.py:444
  27.9 1.1 %pad_maximum_fusion.2.refs_1_.refs_3_ = bf16[2,784,128]{2,1,0:T(8,128)(2,1)S(1)} fusion(bf16[1,784,128]{2,1,0:T(8,128)(2,1)} %bitcast.11, bf16[1,784,128]{2,1,0:T(8,128)(2,1)} %bitcast.10), kind=kLoop, calls=%fused_computation.2 | loop fusion | flops 200704 | bytes 802816 | tf_op jit(solution)/shard_map/stack | solution.py:481
  29.0 1.7 %stats_early.1 = (f32[8,512]{1,0:T(8,128)S(1)}, bf16[512,128]{1,0:T(8,128)(2,1)S(1)}, bf16[512,128]{1,0:T(8,128)(2,1)S(1)}) custom-call(bf16[2,784,128]{2,1,0:T(8,128)(2,1)S(1)} %copy-done, bf16[2,784,128]{2,1,0:T(8,128)(2,1)S(1)} %pad_maximum_fusion.2.refs_1_.refs_3_, bf16[4,784,128]{2,1,0:T(8,128)(2,1)S(1)} %pad_maximum_fusion.refs_2_.refs_4_.k_ref), custom_call_target="tpu_custom_call" | custom-call | tf_op jit(solution)/shard_map/stats_early/pallas_call | solution.py:31
  30.7 5.5 %collective-permute-done.7.refs_1_ = bf16[2,784,128]{2,1,0:T(8,128)(2,1)S(1)} collective-permute-done((bf16[2,784,128]{2,1,0:T(8,128)(2,1)S(1)}, bf16[2,784,128]{2,1,0:T(8,128)(2,1)S(1)}, u32[]{:S(2)}, u32[]{:S(2)}) %collective-permute-start.7) | collective-permute-done | bytes 401440 | tf_op jit(solution)/shard_map/ppermute | solution.py:444
  36.3 4.2 %stats_all.1 = (f32[1024,128]{1,0:T(8,128)S(1)}, f32[8,1024]{1,0:T(8,128)S(1)}, bf16[1024,128]{1,0:T(8,128)(2,1)S(1)}, bf16[512,128]{1,0:T(8,128)(2,1)S(1)}) custom-call(bf16[2,784,128]{2,1,0:T(8,128)(2,1)S(1)} %copy-done, bf16[2,784,128]{2,1,0:T(8,128)(2,1)S(1)} %collective-permute-done.7.refs_1_, ...), custom_call_target="tpu_custom_call" | custom-call | tf_op jit(solution)/shard_map/stats_all/pallas_call | solution.py:31
  40.5 2.1 %collective-permute-start.9 = (f32[8,1024]{1,0:T(8,128)S(1)}, f32[8,1024]{1,0:T(8,128)S(1)}, u32[]{:S(2)}, u32[]{:S(2)}) collective-permute-start(f32[8,1024]{1,0:T(8,128)S(1)} %get-tuple-element.36.refs_0_.rows_ref), channel_id=1, source_target_pairs={{0,66},{1,65},{2,64},{3,67},{4,70},{5,69},{6,68},{7,71},{8,74},{9,... | collective-permute-start | bytes 98312 | tf_op jit(solution)/shard_map/ppermute | solution.py:444
  42.6 3.5 %forward_near.1.later_ref.refs_0_ = f32[3,512,384]{2,1,0:T(8,128)S(1)} custom-call(bf16[2,784,128]{2,1,0:T(8,128)(2,1)S(1)} %copy-done, bf16[2,784,128]{2,1,0:T(8,128)(2,1)S(1)} %collective-permute-done.7.refs_1_, bf16[4,784,128]{2,1,0:T(8,128)(2,1)S(1)} %pad_maximum_fusion.refs_2_.refs_4_.k_ref, ...), custom_call_target="tpu_custom_call" | custom-call | flops 4831838208 | bytes 8388608 | tf_op jit(solution)/shard_map/forward_near/pallas_call | solution.py:31
  46.2 1.6 %collective-permute-start.10 = (f32[8,1024]{1,0:T(8,128)S(1)}, f32[8,1024]{1,0:T(8,128)S(1)}, u32[]{:S(2)}, u32[]{:S(2)}) collective-permute-start(f32[8,1024]{1,0:T(8,128)S(1)} %pair_rows.1.refs_0_), channel_id=1, source_target_pairs={{0,4},{1,5},{2,6},{3,7},{4,8},{5,9},{6,10},{7,11},{8,12},{9,13},{1... | collective-permute-start | bytes 98312 | tf_op jit(solution)/shard_map/ppermute | solution.py:444
  47.9 1.7 %collective-permute-start.11 = (f32[8,1024]{1,0:T(8,128)S(1)}, f32[8,1024]{1,0:T(8,128)S(1)}, u32[]{:S(2)}, u32[]{:S(2)}) collective-permute-start(f32[8,1024]{1,0:T(8,128)S(1)} %pair_rows.1.refs_0_), channel_id=1, source_target_pairs={{0,12},{1,13},{2,14},{3,15},{4,0},{5,1},{6,2},{7,3},{8,4},{9,5},{1... | collective-permute-start | bytes 98312 | tf_op jit(solution)/shard_map/ppermute | solution.py:444
  49.5 2.0 %collective-permute-start.12 = (f32[8,1024]{1,0:T(8,128)S(1)}, f32[8,1024]{1,0:T(8,128)S(1)}, u32[]{:S(2)}, u32[]{:S(2)}) collective-permute-start(f32[8,1024]{1,0:T(8,128)S(1)} %pair_rows.1.refs_0_), channel_id=1, source_target_pairs={{0,8},{1,9},{2,10},{3,11},{4,12},{5,13},{6,14},{7,15},{8,0},{9,1},... | collective-permute-start | bytes 98312 | tf_op jit(solution)/shard_map/ppermute | solution.py:444
  51.5 3.5 %forward_far.1.later_ref.refs_1_ = f32[3,512,384]{2,1,0:T(8,128)S(1)} custom-call(bf16[2,784,128]{2,1,0:T(8,128)(2,1)S(1)} %collective-permute-done.8.refs_2_.refs_0_, bf16[2,784,128]{2,1,0:T(8,128)(2,1)S(1)} %pad_maximum_fusion.2.refs_1_.refs_3_, bf16[4,784,128]{2,1,0:T(8,128)(2,1)S(1)} %pad_maximum_fusion.refs_2_.refs_4_.k_ref, ...), custom_call_target="tpu_custom_call" | custom-call | flops 4831838208 | bytes 8388608 | tf_op jit(solution)/shard_map/forward_far/pallas_call | solution.py:31
  55.2 3.6 %backward_partner.1.later_ref = bf16[4,768,128]{2,1,0:T(8,128)(2,1)S(1)} custom-call(bf16[4,784,128]{2,1,0:T(8,128)(2,1)S(1)} %collective-permute-done.6.refs_5_.refs_3_.k_ref, bf16[2,784,128]{2,1,0:T(8,128)(2,1)S(1)} %copy-done, bf16[2,784,128]{2,1,0:T(8,128)(2,1)S(1)} %collective-permute-done.7.refs_1_, ...), custom_call_target="tpu_custom_call" | custom-call | flops 4026531840 | bytes 8388608 | tf_op jit(solution)/shard_map/backward_partner/pallas_call | solution.py:31
  58.8 0.5 collective-permute-start.17
  59.3 1.5 %share_rows.1 = (bf16[2,768,128]{2,1,0:T(8,128)(2,1)S(1)}, bf16[2,768,128]{2,1,0:T(8,128)(2,1)S(1)}, bf16[2,768,128]{2,1,0:T(8,128)(2,1)S(1)}, bf16[1,768,128]{2,1,0:T(8,128)(2,1)S(1)}, bf16[768,128]{1,0:T(8,128)(2,1)S(1)}) custom-call(bf16[4,768,128]{2,1,0:T(8,128)(2,1)S(1)} %backward_partner.1.later_ref, ...), custom_call_target="tpu_custom_call" | custom-call | bytes 4194304 | tf_op jit(solution)/shard_map/share_rows/pallas_call | solution.py:31
  60.8 1.8 %collective-permute-start.13 = (bf16[2,768,128]{2,1,0:T(8,128)(2,1)S(1)}, bf16[2,768,128]{2,1,0:T(8,128)(2,1)S(1)}, u32[]{:S(2)}, u32[]{:S(2)}) collective-permute-start(bf16[2,768,128]{2,1,0:T(8,128)(2,1)S(1)} %get-tuple-element.38), channel_id=1, source_target_pairs={{0,12},{1,13},{2,14},{3,15},{4,0},{5,1},{6,2},{7,3},{8,4},{9,5},{1... | collective-permute-start | bytes 1179656 | tf_op jit(solution)/shard_map/ppermute | solution.py:444
  62.6 0.3 collective-permute-start.14
  62.9 1.4 %collective-permute-start.15 = (bf16[768,128]{1,0:T(8,128)(2,1)S(1)}, bf16[768,128]{1,0:T(8,128)(2,1)S(1)}, u32[]{:S(2)}, u32[]{:S(2)}) collective-permute-start(bf16[768,128]{1,0:T(8,128)(2,1)S(1)} %get-tuple-element.41), channel_id=1, source_target_pairs={{0,66},{1,65},{2,64},{3,67},{4,70},{5,69},{6,68},{7,71},{8,74},{9,... | collective-permute-start | bytes 589832 | tf_op jit(solution)/shard_map/ppermute | solution.py:444
  64.3 3.6 %backward_own.1.later_ref.own_ref = bf16[4,768,128]{2,1,0:T(8,128)(2,1)S(1)} custom-call(bf16[4,784,128]{2,1,0:T(8,128)(2,1)S(1)} %pad_maximum_fusion.refs_2_.refs_4_.k_ref, bf16[2,784,128]{2,1,0:T(8,128)(2,1)S(1)} %copy-done, bf16[2,784,128]{2,1,0:T(8,128)(2,1)S(1)} %collective-permute-done.7.refs_1_, ...), custom_call_target="tpu_custom_call" | custom-call | flops 4026531840 | bytes 8388608 | tf_op jit(solution)/shard_map/backward_own/pallas_call | solution.py:31
  67.9 1.9 %collective-permute-done.15.got_ref = bf16[768,128]{1,0:T(8,128)(2,1)S(1)} collective-permute-done((bf16[768,128]{1,0:T(8,128)(2,1)S(1)}, bf16[768,128]{1,0:T(8,128)(2,1)S(1)}, u32[]{:S(2)}, u32[]{:S(2)}) %collective-permute-start.15) | collective-permute-done | bytes 196640 | tf_op jit(solution)/shard_map/ppermute | solution.py:444
  69.9 1.9 %collective-permute-start.16 = (bf16[768,128]{1,0:T(8,128)(2,1)S(1)}, bf16[768,128]{1,0:T(8,128)(2,1)S(1)}, u32[]{:S(2)}, u32[]{:S(2)}) collective-permute-start(bf16[768,128]{1,0:T(8,128)(2,1)S(1)} %sum_far.1), channel_id=1, source_target_pairs={{0,8},{1,9},{2,10},{3,11},{4,12},{5,13},{6,14},{7,15},{8,0},{9,1},... | collective-permute-start | bytes 589832 | tf_op jit(solution)/shard_map/ppermute | solution.py:444
  71.8 2.5 %collective-permute-done.17.got_ref = bf16[4,768,128]{2,1,0:T(8,128)(2,1)S(1)} collective-permute-done((bf16[4,768,128]{2,1,0:T(8,128)(2,1)S(1)}, bf16[4,768,128]{2,1,0:T(8,128)(2,1)S(1)}, u32[]{:S(2)}, u32[]{:S(2)}) %collective-permute-start.17) | collective-permute-done | bytes 786464 | tf_op jit(solution)/shard_map/ppermute | solution.py:444
  74.3 0.2 add_keys.1
  74.6 0.7 collective-permute-start.18
  75.3 3.4 %collective-permute-start.21 = (bf16[768,128]{1,0:T(8,128)(2,1)S(1)}, bf16[768,128]{1,0:T(8,128)(2,1)S(1)}, u32[]{:S(2)}, u32[]{:S(2)}) collective-permute-start(bf16[768,128]{1,0:T(8,128)(2,1)S(1)} %get-tuple-element.47), channel_id=1, source_target_pairs={{0,48},{1,49},{2,50},{3,51},{4,52},{5,53},{6,54},{7,55},{8,56},{9,... | collective-permute-start | bytes 589832 | tf_op jit(solution)/shard_map/ppermute | solution.py:444
  78.7 2.4 %collective-permute-start.23 = (bf16[768,128]{1,0:T(8,128)(2,1)S(1)}, bf16[768,128]{1,0:T(8,128)(2,1)S(1)}, u32[]{:S(2)}, u32[]{:S(2)}) collective-permute-start(bf16[768,128]{1,0:T(8,128)(2,1)S(1)} %get-tuple-element.49), channel_id=1, source_target_pairs={{0,32},{1,33},{2,34},{3,35},{4,36},{5,37},{6,38},{7,39},{8,40},{9,... | collective-permute-start | bytes 589832 | tf_op jit(solution)/shard_map/ppermute | solution.py:444
  81.1 0.5 collective-permute-done.18.refs_4_
  81.6 0.7 sum_rows.1
  82.3 1.3 %collective-permute-done.19.other_ref = bf16[128,384]{1,0:T(8,128)(2,1)S(1)} collective-permute-done((bf16[128,384]{1,0:T(8,128)(2,1)S(1)}, bf16[128,384]{1,0:T(8,128)(2,1)S(1)}, u32[]{:S(2)}, u32[]{:S(2)}) %collective-permute-start.19) | collective-permute-done | bytes 98336 | tf_op jit(solution)/shard_map/ppermute | solution.py:521
  83.6 1.3 %project.1 = (bf16[128,1536]{1,0:T(8,128)(2,1)}, f32[8,128]{1,0:T(8,128)S(1)}) custom-call(bf16[128,384]{1,0:T(8,128)(2,1)S(1)} %get-tuple-element.43.own_ref, bf16[128,384]{1,0:T(8,128)(2,1)S(1)} %collective-permute-done.19.other_ref, bf16[384,1536]{1,0:T(8,128)(2,1)S(1)} %copy-done.1, bf16[384,1536]{1,0:T(8,128)(2,1)S(1)} %collective-permute-done.20.other_weight), custom_call_target="tpu_custom_call" | custom-call | flops 301989888 | bytes 2359296 | tf_op jit(solution)/shard_map/project/pallas_call | solution.py:31
  84.9 2.8 %collective-permute-done.22.refs_3_ = bf16[768,128]{1,0:T(8,128)(2,1)S(1)} collective-permute-done((bf16[768,128]{1,0:T(8,128)(2,1)S(1)}, bf16[768,128]{1,0:T(8,128)(2,1)S(1)}, u32[]{:S(2)}, u32[]{:S(2)}) %collective-permute-start.22) | collective-permute-done | bytes 196640 | tf_op jit(solution)/shard_map/ppermute | solution.py:444
  87.7 0.8 sum_keys.1
  (30 shorter events, 0.4 us)
Async XLA Ops:
  0.6 27.3 %copy-start.1 = (bf16[384,1536]{1,0:T(8,128)(2,1)S(1)}, bf16[384,1536]{1,0:T(8,128)(2,1)}, u32[]{:S(2)}) copy-start(bf16[384,1536]{1,0:T(8,128)(2,1)} %own_weight.1) | copy-start | bytes 3538948
  3.5 11.3 %collective-permute-start.3 = (bf16[784,128]{1,0:T(8,128)(2,1)}, bf16[784,128]{1,0:T(8,128)(2,1)S(1)}, u32[]{:S(2)}, u32[]{:S(2)}) collective-permute-start(bf16[784,128]{1,0:T(8,128)(2,1)} %get-tuple-element.29), channel_id=1, source_target_pairs={{0,66},{1,65},{2,64},{3,67},{4,70},{5,69},{6,68},{7,71},{8,74},{9,... | collective-permute-start | bytes 602120 | tf_op jit(solution)/shard_map/ppermute | solution.py:444
  6.5 12.3 %collective-permute-start.4 = (bf16[784,128]{1,0:T(8,128)(2,1)}, bf16[784,128]{1,0:T(8,128)(2,1)S(1)}, u32[]{:S(2)}, u32[]{:S(2)}) collective-permute-start(bf16[784,128]{1,0:T(8,128)(2,1)} %get-tuple-element.29), channel_id=1, source_target_pairs={{0,8},{1,9},{2,10},{3,11},{4,12},{5,13},{6,14},{7,15},{8,0},{9,1},... | collective-permute-start | bytes 602120 | tf_op jit(solution)/shard_map/ppermute | solution.py:444
  9.7 9.5 %collective-permute-start.5 = (bf16[784,128]{1,0:T(8,128)(2,1)}, bf16[784,128]{1,0:T(8,128)(2,1)S(1)}, u32[]{:S(2)}, u32[]{:S(2)}) collective-permute-start(bf16[784,128]{1,0:T(8,128)(2,1)} %get-tuple-element.29), channel_id=1, source_target_pairs={{0,74},{1,73},{2,72},{3,75},{4,78},{5,77},{6,76},{7,79},{8,66},{9,... | collective-permute-start | bytes 602120 | tf_op jit(solution)/shard_map/ppermute | solution.py:444
  9.8 9.4 %collective-permute-start.2 = (bf16[784,128]{1,0:T(8,128)(2,1)}, bf16[784,128]{1,0:T(8,128)(2,1)S(1)}, u32[]{:S(2)}, u32[]{:S(2)}) collective-permute-start(bf16[784,128]{1,0:T(8,128)(2,1)} %get-tuple-element.28), channel_id=1, source_target_pairs={{0,32},{1,33},{2,34},{3,35},{4,36},{5,37},{6,38},{7,39},{8,40},{9,... | collective-permute-start | bytes 602120 | tf_op jit(solution)/shard_map/ppermute | solution.py:444
  13.8 8.0 %collective-permute-start = (bf16[784,128]{1,0:T(8,128)(2,1)}, bf16[784,128]{1,0:T(8,128)(2,1)S(1)}, u32[]{:S(2)}, u32[]{:S(2)}) collective-permute-start(bf16[784,128]{1,0:T(8,128)(2,1)} %get-tuple-element.28), channel_id=1, source_target_pairs={{0,16},{1,17},{2,18},{3,19},{4,20},{5,21},{6,22},{7,23},{8,24},{9,... | collective-permute-start | bytes 602120 | tf_op jit(solution)/shard_map/ppermute | solution.py:444
  14.8 7.2 %collective-permute-start.1 = (bf16[784,128]{1,0:T(8,128)(2,1)}, bf16[784,128]{1,0:T(8,128)(2,1)S(1)}, u32[]{:S(2)}, u32[]{:S(2)}) collective-permute-start(bf16[784,128]{1,0:T(8,128)(2,1)} %get-tuple-element.28), channel_id=1, source_target_pairs={{0,48},{1,49},{2,50},{3,51},{4,52},{5,53},{6,54},{7,55},{8,56},{9,... | collective-permute-start | bytes 602120 | tf_op jit(solution)/shard_map/ppermute | solution.py:444
  18.7 5.9 %copy-start = (bf16[2,784,128]{2,1,0:T(8,128)(2,1)S(1)}, bf16[2,784,128]{2,1,0:T(8,128)(2,1)}, u32[]{:S(2)}) copy-start(bf16[2,784,128]{2,1,0:T(8,128)(2,1)} %pad_maximum_fusion.1.refs_0_) | copy-start | bytes 1204228
  18.7 0.7 copy-start.3
  19.2 0.7 copy-start.4
  19.9 0.7 copy-start.2
  23.1 13.1 %collective-permute-start.6 = (bf16[4,784,128]{2,1,0:T(8,128)(2,1)S(1)}, bf16[4,784,128]{2,1,0:T(8,128)(2,1)S(1)}, u32[]{:S(2)}, u32[]{:S(2)}) collective-permute-start(bf16[4,784,128]{2,1,0:T(8,128)(2,1)S(1)} %pad_maximum_fusion.refs_2_.refs_4_.k_ref), channel_id=1, source_target_pairs={{0,64},{1,67},{2,66},{3,65},{4,68},{5,71},{6,70},{7,69},{8,72},{9,... | collective-permute-start | bytes 2408456 | tf_op jit(solution)/shard_map/ppermute | solution.py:444
  24.7 11.6 %collective-permute-start.7 = (bf16[2,784,128]{2,1,0:T(8,128)(2,1)S(1)}, bf16[2,784,128]{2,1,0:T(8,128)(2,1)S(1)}, u32[]{:S(2)}, u32[]{:S(2)}) collective-permute-start(bf16[2,784,128]{2,1,0:T(8,128)(2,1)S(1)} %copy-done), channel_id=1, source_target_pairs={{0,4},{1,5},{2,6},{3,7},{4,8},{5,9},{6,10},{7,11},{8,12},{9,13},{1... | collective-permute-start | bytes 1204232 | tf_op jit(solution)/shard_map/ppermute | solution.py:444
  26.3 10.0 %collective-permute-start.8 = (bf16[2,784,128]{2,1,0:T(8,128)(2,1)S(1)}, bf16[2,784,128]{2,1,0:T(8,128)(2,1)S(1)}, u32[]{:S(2)}, u32[]{:S(2)}) collective-permute-start(bf16[2,784,128]{2,1,0:T(8,128)(2,1)S(1)} %copy-done), channel_id=1, source_target_pairs={{0,12},{1,13},{2,14},{3,15},{4,0},{5,1},{6,2},{7,3},{8,4},{9,5},{1... | collective-permute-start | bytes 1204232 | tf_op jit(solution)/shard_map/ppermute | solution.py:444
  27.9 54.4 %collective-permute-start.20 = (bf16[384,1536]{1,0:T(8,128)(2,1)S(1)}, bf16[384,1536]{1,0:T(8,128)(2,1)S(1)}, u32[]{:S(2)}, u32[]{:S(2)}) collective-permute-start(bf16[384,1536]{1,0:T(8,128)(2,1)S(1)} %copy-done.1), channel_id=1, source_target_pairs={{0,1},{1,0},{2,3},{3,2},{4,5},{5,4},{6,7},{7,6},{8,9},{9,8},{10,11... | collective-permute-start | bytes 3538952 | tf_op jit(solution)/shard_map/ppermute | solution.py:486
  40.5 5.6 %collective-permute-start.9 = (f32[8,1024]{1,0:T(8,128)S(1)}, f32[8,1024]{1,0:T(8,128)S(1)}, u32[]{:S(2)}, u32[]{:S(2)}) collective-permute-start(f32[8,1024]{1,0:T(8,128)S(1)} %get-tuple-element.36.refs_0_.rows_ref), channel_id=1, source_target_pairs={{0,66},{1,65},{2,64},{3,67},{4,70},{5,69},{6,68},{7,71},{8,74},{9,... | collective-permute-start | bytes 98312 | tf_op jit(solution)/shard_map/ppermute | solution.py:444
  46.2 8.8 %collective-permute-start.10 = (f32[8,1024]{1,0:T(8,128)S(1)}, f32[8,1024]{1,0:T(8,128)S(1)}, u32[]{:S(2)}, u32[]{:S(2)}) collective-permute-start(f32[8,1024]{1,0:T(8,128)S(1)} %pair_rows.1.refs_0_), channel_id=1, source_target_pairs={{0,4},{1,5},{2,6},{3,7},{4,8},{5,9},{6,10},{7,11},{8,12},{9,13},{1... | collective-permute-start | bytes 98312 | tf_op jit(solution)/shard_map/ppermute | solution.py:444
  47.9 7.2 %collective-permute-start.11 = (f32[8,1024]{1,0:T(8,128)S(1)}, f32[8,1024]{1,0:T(8,128)S(1)}, u32[]{:S(2)}, u32[]{:S(2)}) collective-permute-start(f32[8,1024]{1,0:T(8,128)S(1)} %pair_rows.1.refs_0_), channel_id=1, source_target_pairs={{0,12},{1,13},{2,14},{3,15},{4,0},{5,1},{6,2},{7,3},{8,4},{9,5},{1... | collective-permute-start | bytes 98312 | tf_op jit(solution)/shard_map/ppermute | solution.py:444
  49.5 5.5 %collective-permute-start.12 = (f32[8,1024]{1,0:T(8,128)S(1)}, f32[8,1024]{1,0:T(8,128)S(1)}, u32[]{:S(2)}, u32[]{:S(2)}) collective-permute-start(f32[8,1024]{1,0:T(8,128)S(1)} %pair_rows.1.refs_0_), channel_id=1, source_target_pairs={{0,8},{1,9},{2,10},{3,11},{4,12},{5,13},{6,14},{7,15},{8,0},{9,1},... | collective-permute-start | bytes 98312 | tf_op jit(solution)/shard_map/ppermute | solution.py:444
  58.8 15.5 %collective-permute-start.17 = (bf16[4,768,128]{2,1,0:T(8,128)(2,1)S(1)}, bf16[4,768,128]{2,1,0:T(8,128)(2,1)S(1)}, u32[]{:S(2)}, u32[]{:S(2)}) collective-permute-start(bf16[4,768,128]{2,1,0:T(8,128)(2,1)S(1)} %backward_partner.1.later_ref), channel_id=1, source_target_pairs={{0,64},{1,67},{2,66},{3,65},{4,68},{5,71},{6,70},{7,69},{8,72},{9,... | collective-permute-start | bytes 2359304 | tf_op jit(solution)/shard_map/ppermute | solution.py:444
  60.8 13.7 %collective-permute-start.13 = (bf16[2,768,128]{2,1,0:T(8,128)(2,1)S(1)}, bf16[2,768,128]{2,1,0:T(8,128)(2,1)S(1)}, u32[]{:S(2)}, u32[]{:S(2)}) collective-permute-start(bf16[2,768,128]{2,1,0:T(8,128)(2,1)S(1)} %get-tuple-element.38), channel_id=1, source_target_pairs={{0,12},{1,13},{2,14},{3,15},{4,0},{5,1},{6,2},{7,3},{8,4},{9,5},{1... | collective-permute-start | bytes 1179656 | tf_op jit(solution)/shard_map/ppermute | solution.py:444
  62.6 11.9 %collective-permute-start.14 = (bf16[2,768,128]{2,1,0:T(8,128)(2,1)S(1)}, bf16[2,768,128]{2,1,0:T(8,128)(2,1)S(1)}, u32[]{:S(2)}, u32[]{:S(2)}) collective-permute-start(bf16[2,768,128]{2,1,0:T(8,128)(2,1)S(1)} %get-tuple-element.39), channel_id=1, source_target_pairs={{0,4},{1,5},{2,6},{3,7},{4,8},{5,9},{6,10},{7,11},{8,12},{9,13},{1... | collective-permute-start | bytes 1179656 | tf_op jit(solution)/shard_map/ppermute | solution.py:444
  62.9 6.9 %collective-permute-start.15 = (bf16[768,128]{1,0:T(8,128)(2,1)S(1)}, bf16[768,128]{1,0:T(8,128)(2,1)S(1)}, u32[]{:S(2)}, u32[]{:S(2)}) collective-permute-start(bf16[768,128]{1,0:T(8,128)(2,1)S(1)} %get-tuple-element.41), channel_id=1, source_target_pairs={{0,66},{1,65},{2,64},{3,67},{4,70},{5,69},{6,68},{7,71},{8,74},{9,... | collective-permute-start | bytes 589832 | tf_op jit(solution)/shard_map/ppermute | solution.py:444
  69.9 8.8 %collective-permute-start.16 = (bf16[768,128]{1,0:T(8,128)(2,1)S(1)}, bf16[768,128]{1,0:T(8,128)(2,1)S(1)}, u32[]{:S(2)}, u32[]{:S(2)}) collective-permute-start(bf16[768,128]{1,0:T(8,128)(2,1)S(1)} %sum_far.1), channel_id=1, source_target_pairs={{0,8},{1,9},{2,10},{3,11},{4,12},{5,13},{6,14},{7,15},{8,0},{9,1},... | collective-permute-start | bytes 589832 | tf_op jit(solution)/shard_map/ppermute | solution.py:444
  74.6 7.0 %collective-permute-start.18 = (bf16[768,128]{1,0:T(8,128)(2,1)S(1)}, bf16[768,128]{1,0:T(8,128)(2,1)S(1)}, u32[]{:S(2)}, u32[]{:S(2)}) collective-permute-start(bf16[768,128]{1,0:T(8,128)(2,1)S(1)} %sum_partner.1), channel_id=1, source_target_pairs={{0,66},{1,65},{2,64},{3,67},{4,70},{5,69},{6,68},{7,71},{8,74},{9,... | collective-permute-start | bytes 589832 | tf_op jit(solution)/shard_map/ppermute | solution.py:444
  75.3 9.6 %collective-permute-start.21 = (bf16[768,128]{1,0:T(8,128)(2,1)S(1)}, bf16[768,128]{1,0:T(8,128)(2,1)S(1)}, u32[]{:S(2)}, u32[]{:S(2)}) collective-permute-start(bf16[768,128]{1,0:T(8,128)(2,1)S(1)} %get-tuple-element.47), channel_id=1, source_target_pairs={{0,48},{1,49},{2,50},{3,51},{4,52},{5,53},{6,54},{7,55},{8,56},{9,... | collective-permute-start | bytes 589832 | tf_op jit(solution)/shard_map/ppermute | solution.py:444
  78.7 9.0 %collective-permute-start.22 = (bf16[768,128]{1,0:T(8,128)(2,1)S(1)}, bf16[768,128]{1,0:T(8,128)(2,1)S(1)}, u32[]{:S(2)}, u32[]{:S(2)}) collective-permute-start(bf16[768,128]{1,0:T(8,128)(2,1)S(1)} %get-tuple-element.48), channel_id=1, source_target_pairs={{0,16},{1,17},{2,18},{3,19},{4,20},{5,21},{6,22},{7,23},{8,24},{9,... | collective-permute-start | bytes 589832 | tf_op jit(solution)/shard_map/ppermute | solution.py:444
  78.7 9.0 %collective-permute-start.23 = (bf16[768,128]{1,0:T(8,128)(2,1)S(1)}, bf16[768,128]{1,0:T(8,128)(2,1)S(1)}, u32[]{:S(2)}, u32[]{:S(2)}) collective-permute-start(bf16[768,128]{1,0:T(8,128)(2,1)S(1)} %get-tuple-element.49), channel_id=1, source_target_pairs={{0,32},{1,33},{2,34},{3,35},{4,36},{5,37},{6,38},{7,39},{8,40},{9,... | collective-permute-start | bytes 589832 | tf_op jit(solution)/shard_map/ppermute | solution.py:444
  82.3 1.3 %collective-permute-start.19 = (bf16[128,384]{1,0:T(8,128)(2,1)S(1)}, bf16[128,384]{1,0:T(8,128)(2,1)S(1)}, u32[]{:S(2)}, u32[]{:S(2)}) collective-permute-start(bf16[128,384]{1,0:T(8,128)(2,1)S(1)} %get-tuple-element.43.own_ref), channel_id=1, source_target_pairs={{0,1},{1,0},{2,3},{3,2},{4,5},{5,4},{6,7},{7,6},{8,9},{9,8},{10,11... | collective-permute-start | bytes 294920 | tf_op jit(solution)/shard_map/ppermute | solution.py:521

commit v4 on v3

--- a/solution.py
+++ b/solution.py
@@ -80,22 +80,6 @@
     block = shape((PR + SR, HD), BF16)
     scratch = [pltpu.VMEM(a.shape, a.dtype) for a in args] + [pltpu.SemaphoreType.DMA((len(args),))]
     return call(pack_kernel, "pack", (block, block), args, scratch, len(args), ALL_VMEM)
-
-
-def gate_kernel(source_ref, *refs):
-    del source_ref, refs
-
-
-def gate(array, *later):
-    return pl.pallas_call(
-        gate_kernel,
-        out_shape=shape(array.shape, array.dtype),
-        in_specs=[ANYWHERE] * (1 + len(later)),
-        out_specs=ANYWHERE,
-        input_output_aliases={0: 0},
-        cost_estimate=pl.CostEstimate(flops=0, bytes_accessed=0, transcendentals=0),
-        name="gate",
-    )(array, *later)
 
 
 def fill_marks(part_refs, mark_ref, for_keys):
@@ -480,7 +464,9 @@
     far_partner_blocks = [places.query_partner_along_y(qg, d) for d in far]
     chunks += [jnp.stack(pair) for pair in zip(far_blocks, far_partner_blocks)]
     key_blocks = [places.along_z(kv, d) for d in z_shifts[1:]]
-    key_blocks[-1] = gate(key_blocks[-1], pair0, *far_blocks, *far_partner_blocks)
+    (kv, *key_blocks), *_ = lax.optimization_barrier(
+        ((kv, *key_blocks), pair0, *far_blocks, *far_partner_blocks)
+    )
     ko = jnp.stack([kv] + key_blocks)
     kx = places.key_partner(ko)
     other_weight = lax.ppermute(out_weight, "head", swap)

time: 88.7 us -> 87.4 us (0.985)
  waiting for transfers between devices: 16.3 us -> 20.3 us
  starting transfers between devices: 38.1 us -> 36.1 us
  other arithmetic: 3.9 us -> 2.03 us
  local copies, waits for them, and re-layouts: 1.38 us -> 0.01 us
    ppermute x22, waiting for transfers between devices: 15 us -> 19 us  [send(): return lax.ppermute(array, ('row', 'col', 'head'), pairs)]
    ppermute x22, starting transfers between devices: 38.1 us -> 36.1 us  [send(): return lax.ppermute(array, ('row', 'col', 'head'), pairs)]
    unnamed x10 -> x2, local copies, waits for them, and re-layouts: 1.38 us -> 0.01 us
    another operation x1, other arithmetic: 1.06 us -> 0.04 us  [on_device(): chunks += [jnp.stack(pair) for pair in zip(far_blocks, far_partner_blocks)]]
  transfers between devices with their start and end apart: 24 -> 24, of which waited for: 9 -> 12; matrix products, arithmetic and copies ran while one was open for 3% -> 1% of each run, Pallas kernels for 27% -> 28%
where the time goes in v4:
time: 87.4 us; the launch traced here: 87.2 us
  starting transfers between devices  36.1 us (41%)
  Pallas kernels  28 us (32%)
  waiting for transfers between devices  20.3 us (23%)
  other arithmetic  2.03 us (2%)
    ppermute x22, starting transfers between devices, send(): return lax.ppermute(array, ('row', 'col', 'head'), pairs)  36.1 us
    pallas_call x16, Pallas kernels, call(): pl.pallas_call(kernel, out_shape=out_shape, in_specs=[ANYWHERE] * anywher...  28 us
    ppermute x22, waiting for transfers between devices, send(): return lax.ppermute(array, ('row', 'col', 'head'), pairs)  19 us
  transfers between devices with their start and end apart: 24, of which 12 were waited for; matrix products, arithmetic and copies ran while one was open for 1% of the time, Pallas kernels for 28%

profile of v4, /device:TPU:0, one launch (start us, length us, event | category | flops | bytes accessed | tf_op | source)
XLA Modules:
  0.0 87.2 jit_solution(12532159514930150255)
XLA Ops:
  0.6 2.9 %pack.1 = (bf16[784,128]{1,0:T(8,128)(2,1)}, bf16[784,128]{1,0:T(8,128)(2,1)}) custom-call(s32[1,128]{1,0:T(1,128)} %bitcast.17, bf16[128,384]{1,0:T(8,128)(2,1)} %refs_1_.1, bf16[128,384]{1,0:T(8,128)(2,1)} %refs_2_.1, bf16[128,384]{1,0:T(8,128)(2,1)} %refs_3_.1, bf16[128,1536]{1,0:T(8,128)(2,1)} %refs_4_.1, bf16[384,1536]{1,0:T(8,128)(2,1)} %own_weight.1), custom_call_target="tpu_custom_call" | custom-call | tf_op jit(solution)/shard_map/pack/pallas_call | solution.py:31
  3.5 2.9 %collective-permute-start.3 = (bf16[784,128]{1,0:T(8,128)(2,1)}, bf16[784,128]{1,0:T(8,128)(2,1)S(1)}, u32[]{:S(2)}, u32[]{:S(2)}) collective-permute-start(bf16[784,128]{1,0:T(8,128)(2,1)} %get-tuple-element.33), channel_id=1, source_target_pairs={{0,66},{1,65},{2,64},{3,67},{4,70},{5,69},{6,68},{7,71},{8,74},{9,... | collective-permute-start | bytes 602120 | tf_op jit(solution)/shard_map/ppermute | solution.py:428
  6.5 3.2 %collective-permute-start.4 = (bf16[784,128]{1,0:T(8,128)(2,1)}, bf16[784,128]{1,0:T(8,128)(2,1)S(1)}, u32[]{:S(2)}, u32[]{:S(2)}) collective-permute-start(bf16[784,128]{1,0:T(8,128)(2,1)} %get-tuple-element.33), channel_id=1, source_target_pairs={{0,8},{1,9},{2,10},{3,11},{4,12},{5,13},{6,14},{7,15},{8,0},{9,1},... | collective-permute-start | bytes 602120 | tf_op jit(solution)/shard_map/ppermute | solution.py:428
  9.7 0.2 collective-permute-start.5
  9.8 2.0 %collective-permute-start = (bf16[784,128]{1,0:T(8,128)(2,1)}, bf16[784,128]{1,0:T(8,128)(2,1)S(1)}, u32[]{:S(2)}, u32[]{:S(2)}) collective-permute-start(bf16[784,128]{1,0:T(8,128)(2,1)} %get-tuple-element.34), channel_id=1, source_target_pairs={{0,16},{1,17},{2,18},{3,19},{4,20},{5,21},{6,22},{7,23},{8,24},{9,... | collective-permute-start | bytes 602120 | tf_op jit(solution)/shard_map/ppermute | solution.py:428
  11.8 2.1 %collective-permute-start.1 = (bf16[784,128]{1,0:T(8,128)(2,1)}, bf16[784,128]{1,0:T(8,128)(2,1)S(1)}, u32[]{:S(2)}, u32[]{:S(2)}) collective-permute-start(bf16[784,128]{1,0:T(8,128)(2,1)} %get-tuple-element.34), channel_id=1, source_target_pairs={{0,48},{1,49},{2,50},{3,51},{4,52},{5,53},{6,54},{7,55},{8,56},{9,... | collective-permute-start | bytes 602120 | tf_op jit(solution)/shard_map/ppermute | solution.py:428
  13.9 1.9 %collective-permute-start.2 = (bf16[784,128]{1,0:T(8,128)(2,1)}, bf16[784,128]{1,0:T(8,128)(2,1)S(1)}, u32[]{:S(2)}, u32[]{:S(2)}) collective-permute-start(bf16[784,128]{1,0:T(8,128)(2,1)} %get-tuple-element.34), channel_id=1, source_target_pairs={{0,32},{1,33},{2,34},{3,35},{4,36},{5,37},{6,38},{7,39},{8,40},{9,... | collective-permute-start | bytes 602120 | tf_op jit(solution)/shard_map/ppermute | solution.py:428
  15.8 1.0 %pad_maximum_fusion.1.refs_0_ = bf16[2,784,128]{2,1,0:T(8,128)(2,1)S(1)} fusion(bf16[1,784,128]{2,1,0:T(8,128)(2,1)S(1)} %bitcast.16, bf16[1,784,128]{2,1,0:T(8,128)(2,1)} %bitcast.15), kind=kLoop, calls=%fused_computation.1 | loop fusion | flops 200704 | bytes 802816 | tf_op jit(solution)/shard_map/stack | solution.py:459
  16.8 0.2 collective-permute-done.4
  17.0 2.2 %collective-permute-done.5 = bf16[784,128]{1,0:T(8,128)(2,1)S(1)} collective-permute-done((bf16[784,128]{1,0:T(8,128)(2,1)}, bf16[784,128]{1,0:T(8,128)(2,1)S(1)}, u32[]{:S(2)}, u32[]{:S(2)}) %collective-permute-start.5) | collective-permute-done | bytes 200736 | tf_op jit(solution)/shard_map/ppermute | solution.py:428
  19.2 0.8 collective-permute-done
  20.0 0.8 collective-permute-done.1
  20.8 1.8 %collective-permute-done.2 = bf16[784,128]{1,0:T(8,128)(2,1)S(1)} collective-permute-done((bf16[784,128]{1,0:T(8,128)(2,1)}, bf16[784,128]{1,0:T(8,128)(2,1)S(1)}, u32[]{:S(2)}, u32[]{:S(2)}) %collective-permute-start.2) | collective-permute-done | bytes 200736 | tf_op jit(solution)/shard_map/ppermute | solution.py:428
  22.6 1.0 %pad_maximum_fusion.refs_2_.refs_4_.k_ref = bf16[4,784,128]{2,1,0:T(8,128)(2,1)S(1)} fusion(bf16[1,784,128]{2,1,0:T(8,128)(2,1)S(1)} %bitcast.12, bf16[1,784,128]{2,1,0:T(8,128)(2,1)S(1)} %bitcast.11, bf16[1,784,128]{2,1,0:T(8,128)(2,1)S(1)} %bitcast.10, bf16[1,784,128]{2,1,0:T(8,128)(2,1)} %bitcast.9), kind=kLoop, calls=%fused_computation | loop fusion | flops 1204224 | bytes 1605632 | tf_op jit(solution)/shard_map/stack | solution.py:470
  23.6 1.5 %collective-permute-start.6 = (bf16[4,784,128]{2,1,0:T(8,128)(2,1)S(1)}, bf16[4,784,128]{2,1,0:T(8,128)(2,1)S(1)}, u32[]{:S(2)}, u32[]{:S(2)}) collective-permute-start(bf16[4,784,128]{2,1,0:T(8,128)(2,1)S(1)} %pad_maximum_fusion.refs_2_.refs_4_.k_ref), channel_id=1, source_target_pairs={{0,64},{1,67},{2,66},{3,65},{4,68},{5,71},{6,70},{7,69},{8,72},{9,... | collective-permute-start | bytes 2408456 | tf_op jit(solution)/shard_map/ppermute | solution.py:428
  25.2 1.6 %collective-permute-start.7 = (bf16[2,784,128]{2,1,0:T(8,128)(2,1)S(1)}, bf16[2,784,128]{2,1,0:T(8,128)(2,1)S(1)}, u32[]{:S(2)}, u32[]{:S(2)}) collective-permute-start(bf16[2,784,128]{2,1,0:T(8,128)(2,1)S(1)} %pad_maximum_fusion.1.refs_0_), channel_id=1, source_target_pairs={{0,4},{1,5},{2,6},{3,7},{4,8},{5,9},{6,10},{7,11},{8,12},{9,13},{1... | collective-permute-start | bytes 1204232 | tf_op jit(solution)/shard_map/ppermute | solution.py:428
  26.7 1.7 %collective-permute-start.8 = (bf16[2,784,128]{2,1,0:T(8,128)(2,1)S(1)}, bf16[2,784,128]{2,1,0:T(8,128)(2,1)S(1)}, u32[]{:S(2)}, u32[]{:S(2)}) collective-permute-start(bf16[2,784,128]{2,1,0:T(8,128)(2,1)S(1)} %pad_maximum_fusion.1.refs_0_), channel_id=1, source_target_pairs={{0,12},{1,13},{2,14},{3,15},{4,0},{5,1},{6,2},{7,3},{8,4},{9,5},{1... | collective-permute-start | bytes 1204232 | tf_op jit(solution)/shard_map/ppermute | solution.py:428
  28.5 1.7 %stats_early.1 = (f32[8,512]{1,0:T(8,128)S(1)}, bf16[512,128]{1,0:T(8,128)(2,1)S(1)}, bf16[512,128]{1,0:T(8,128)(2,1)S(1)}) custom-call(bf16[2,784,128]{2,1,0:T(8,128)(2,1)S(1)} %pad_maximum_fusion.1.refs_0_, bf16[2,784,128]{2,1,0:T(8,128)(2,1)S(1)} %pad_maximum_fusion.2.refs_1_.refs_3_, bf16[4,784,128]{2,1,0:T(8,128)(2,1)S(1)} %pad_maximum_fusion.refs_2_.refs_4_.k_ref), custom_call_target="tpu_custom_call" | custom-call | tf_op jit(solution)/shard_map/stats_early/pallas_call | solution.py:31
  30.2 5.1 %collective-permute-done.7.refs_1_ = bf16[2,784,128]{2,1,0:T(8,128)(2,1)S(1)} collective-permute-done((bf16[2,784,128]{2,1,0:T(8,128)(2,1)S(1)}, bf16[2,784,128]{2,1,0:T(8,128)(2,1)S(1)}, u32[]{:S(2)}, u32[]{:S(2)}) %collective-permute-start.7) | collective-permute-done | bytes 401440 | tf_op jit(solution)/shard_map/ppermute | solution.py:428
  35.3 0.6 collective-permute-done.6.refs_5_.refs_3_.k_ref
  35.9 4.2 %stats_all.1 = (f32[1024,128]{1,0:T(8,128)S(1)}, f32[8,1024]{1,0:T(8,128)S(1)}, bf16[1024,128]{1,0:T(8,128)(2,1)S(1)}, bf16[512,128]{1,0:T(8,128)(2,1)S(1)}) custom-call(bf16[2,784,128]{2,1,0:T(8,128)(2,1)S(1)} %pad_maximum_fusion.1.refs_0_, bf16[2,784,128]{2,1,0:T(8,128)(2,1)S(1)} %collective-permute-done.7.refs_1_, ...), custom_call_target="tpu_custom_call" | custom-call | tf_op jit(solution)/shard_map/stats_all/pallas_call | solution.py:31
  40.1 3.0 %collective-permute-start.9 = (f32[8,1024]{1,0:T(8,128)S(1)}, f32[8,1024]{1,0:T(8,128)S(1)}, u32[]{:S(2)}, u32[]{:S(2)}) collective-permute-start(f32[8,1024]{1,0:T(8,128)S(1)} %get-tuple-element.44.refs_0_.rows_ref), channel_id=1, source_target_pairs={{0,66},{1,65},{2,64},{3,67},{4,70},{5,69},{6,68},{7,71},{8,74},{9,... | collective-permute-start | bytes 98312 | tf_op jit(solution)/shard_map/ppermute | solution.py:428
  43.2 3.5 %forward_near.1.later_ref.refs_0_ = f32[3,512,384]{2,1,0:T(8,128)S(1)} custom-call(bf16[2,784,128]{2,1,0:T(8,128)(2,1)S(1)} %pad_maximum_fusion.1.refs_0_, bf16[2,784,128]{2,1,0:T(8,128)(2,1)S(1)} %collective-permute-done.7.refs_1_, bf16[4,784,128]{2,1,0:T(8,128)(2,1)S(1)} %pad_maximum_fusion.refs_2_.refs_4_.k_ref, ...), custom_call_target="tpu_custom_call" | custom-call | flops 4831838208 | bytes 8388608 | tf_op jit(solution)/shard_map/forward_near/pallas_call | solution.py:31
  46.8 1.6 %collective-permute-start.10 = (f32[8,1024]{1,0:T(8,128)S(1)}, f32[8,1024]{1,0:T(8,128)S(1)}, u32[]{:S(2)}, u32[]{:S(2)}) collective-permute-start(f32[8,1024]{1,0:T(8,128)S(1)} %pair_rows.1.refs_0_), channel_id=1, source_target_pairs={{0,4},{1,5},{2,6},{3,7},{4,8},{5,9},{6,10},{7,11},{8,12},{9,13},{1... | collective-permute-start | bytes 98312 | tf_op jit(solution)/shard_map/ppermute | solution.py:428
  48.4 1.7 %collective-permute-start.11 = (f32[8,1024]{1,0:T(8,128)S(1)}, f32[8,1024]{1,0:T(8,128)S(1)}, u32[]{:S(2)}, u32[]{:S(2)}) collective-permute-start(f32[8,1024]{1,0:T(8,128)S(1)} %pair_rows.1.refs_0_), channel_id=1, source_target_pairs={{0,12},{1,13},{2,14},{3,15},{4,0},{5,1},{6,2},{7,3},{8,4},{9,5},{1... | collective-permute-start | bytes 98312 | tf_op jit(solution)/shard_map/ppermute | solution.py:428
  50.1 2.0 %collective-permute-start.12 = (f32[8,1024]{1,0:T(8,128)S(1)}, f32[8,1024]{1,0:T(8,128)S(1)}, u32[]{:S(2)}, u32[]{:S(2)}) collective-permute-start(f32[8,1024]{1,0:T(8,128)S(1)} %pair_rows.1.refs_0_), channel_id=1, source_target_pairs={{0,8},{1,9},{2,10},{3,11},{4,12},{5,13},{6,14},{7,15},{8,0},{9,1},... | collective-permute-start | bytes 98312 | tf_op jit(solution)/shard_map/ppermute | solution.py:428
  52.1 3.5 %forward_far.1.later_ref.refs_1_ = f32[3,512,384]{2,1,0:T(8,128)S(1)} custom-call(bf16[2,784,128]{2,1,0:T(8,128)(2,1)S(1)} %collective-permute-done.8.refs_2_.refs_0_, bf16[2,784,128]{2,1,0:T(8,128)(2,1)S(1)} %pad_maximum_fusion.2.refs_1_.refs_3_, bf16[4,784,128]{2,1,0:T(8,128)(2,1)S(1)} %pad_maximum_fusion.refs_2_.refs_4_.k_ref, ...), custom_call_target="tpu_custom_call" | custom-call | flops 4831838208 | bytes 8388608 | tf_op jit(solution)/shard_map/forward_far/pallas_call | solution.py:31
  55.7 3.6 %backward_partner.1.later_ref = bf16[4,768,128]{2,1,0:T(8,128)(2,1)S(1)} custom-call(bf16[4,784,128]{2,1,0:T(8,128)(2,1)S(1)} %collective-permute-done.6.refs_5_.refs_3_.k_ref, bf16[2,784,128]{2,1,0:T(8,128)(2,1)S(1)} %pad_maximum_fusion.1.refs_0_, bf16[2,784,128]{2,1,0:T(8,128)(2,1)S(1)} %collective-permute-done.7.refs_1_, ...), custom_call_target="tpu_custom_call" | custom-call | flops 4026531840 | bytes 8388608 | tf_op jit(solution)/shard_map/backward_partner/pallas_call | solution.py:31
  59.3 0.5 collective-permute-start.17
  59.9 1.5 %share_rows.1 = (bf16[2,768,128]{2,1,0:T(8,128)(2,1)S(1)}, bf16[2,768,128]{2,1,0:T(8,128)(2,1)S(1)}, bf16[2,768,128]{2,1,0:T(8,128)(2,1)S(1)}, bf16[1,768,128]{2,1,0:T(8,128)(2,1)S(1)}, bf16[768,128]{1,0:T(8,128)(2,1)S(1)}) custom-call(bf16[4,768,128]{2,1,0:T(8,128)(2,1)S(1)} %backward_partner.1.later_ref, ...), custom_call_target="tpu_custom_call" | custom-call | bytes 4194304 | tf_op jit(solution)/shard_map/share_rows/pallas_call | solution.py:31
  61.4 1.8 %collective-permute-start.13 = (bf16[2,768,128]{2,1,0:T(8,128)(2,1)S(1)}, bf16[2,768,128]{2,1,0:T(8,128)(2,1)S(1)}, u32[]{:S(2)}, u32[]{:S(2)}) collective-permute-start(bf16[2,768,128]{2,1,0:T(8,128)(2,1)S(1)} %get-tuple-element.46), channel_id=1, source_target_pairs={{0,12},{1,13},{2,14},{3,15},{4,0},{5,1},{6,2},{7,3},{8,4},{9,5},{1... | collective-permute-start | bytes 1179656 | tf_op jit(solution)/shard_map/ppermute | solution.py:428
  63.1 0.3 collective-permute-start.14
  63.5 1.4 %collective-permute-start.15 = (bf16[768,128]{1,0:T(8,128)(2,1)S(1)}, bf16[768,128]{1,0:T(8,128)(2,1)S(1)}, u32[]{:S(2)}, u32[]{:S(2)}) collective-permute-start(bf16[768,128]{1,0:T(8,128)(2,1)S(1)} %get-tuple-element.49), channel_id=1, source_target_pairs={{0,66},{1,65},{2,64},{3,67},{4,70},{5,69},{6,68},{7,71},{8,74},{9,... | collective-permute-start | bytes 589832 | tf_op jit(solution)/shard_map/ppermute | solution.py:428
  64.9 3.6 %backward_own.1.later_ref.own_ref = bf16[4,768,128]{2,1,0:T(8,128)(2,1)S(1)} custom-call(bf16[4,784,128]{2,1,0:T(8,128)(2,1)S(1)} %pad_maximum_fusion.refs_2_.refs_4_.k_ref, bf16[2,784,128]{2,1,0:T(8,128)(2,1)S(1)} %pad_maximum_fusion.1.refs_0_, bf16[2,784,128]{2,1,0:T(8,128)(2,1)S(1)} %collective-permute-done.7.refs_1_, ...), custom_call_target="tpu_custom_call" | custom-call | flops 4026531840 | bytes 8388608 | tf_op jit(solution)/shard_map/backward_own/pallas_call | solution.py:31
  68.5 1.8 %collective-permute-done.15.got_ref = bf16[768,128]{1,0:T(8,128)(2,1)S(1)} collective-permute-done((bf16[768,128]{1,0:T(8,128)(2,1)S(1)}, bf16[768,128]{1,0:T(8,128)(2,1)S(1)}, u32[]{:S(2)}, u32[]{:S(2)}) %collective-permute-start.15) | collective-permute-done | bytes 196640 | tf_op jit(solution)/shard_map/ppermute | solution.py:428
  70.4 1.9 %collective-permute-start.16 = (bf16[768,128]{1,0:T(8,128)(2,1)S(1)}, bf16[768,128]{1,0:T(8,128)(2,1)S(1)}, u32[]{:S(2)}, u32[]{:S(2)}) collective-permute-start(bf16[768,128]{1,0:T(8,128)(2,1)S(1)} %sum_far.1), channel_id=1, source_target_pairs={{0,8},{1,9},{2,10},{3,11},{4,12},{5,13},{6,14},{7,15},{8,0},{9,1},... | collective-permute-start | bytes 589832 | tf_op jit(solution)/shard_map/ppermute | solution.py:428
  72.4 2.2 %collective-permute-done.17.got_ref = bf16[4,768,128]{2,1,0:T(8,128)(2,1)S(1)} collective-permute-done((bf16[4,768,128]{2,1,0:T(8,128)(2,1)S(1)}, bf16[4,768,128]{2,1,0:T(8,128)(2,1)S(1)}, u32[]{:S(2)}, u32[]{:S(2)}) %collective-permute-start.17) | collective-permute-done | bytes 786464 | tf_op jit(solution)/shard_map/ppermute | solution.py:428
  74.6 0.2 add_keys.1
  74.9 1.1 %collective-permute-start.18 = (bf16[768,128]{1,0:T(8,128)(2,1)S(1)}, bf16[768,128]{1,0:T(8,128)(2,1)S(1)}, u32[]{:S(2)}, u32[]{:S(2)}) collective-permute-start(bf16[768,128]{1,0:T(8,128)(2,1)S(1)} %sum_partner.1), channel_id=1, source_target_pairs={{0,66},{1,65},{2,64},{3,67},{4,70},{5,69},{6,68},{7,71},{8,74},{9,... | collective-permute-start | bytes 589832 | tf_op jit(solution)/shard_map/ppermute | solution.py:428
  75.9 1.5 %collective-permute-start.21 = (bf16[768,128]{1,0:T(8,128)(2,1)S(1)}, bf16[768,128]{1,0:T(8,128)(2,1)S(1)}, u32[]{:S(2)}, u32[]{:S(2)}) collective-permute-start(bf16[768,128]{1,0:T(8,128)(2,1)S(1)} %get-tuple-element.55), channel_id=1, source_target_pairs={{0,48},{1,49},{2,50},{3,51},{4,52},{5,53},{6,54},{7,55},{8,56},{9,... | collective-permute-start | bytes 589832 | tf_op jit(solution)/shard_map/ppermute | solution.py:428
  77.4 0.5 collective-permute-start.22
  77.9 1.7 %collective-permute-start.23 = (bf16[768,128]{1,0:T(8,128)(2,1)S(1)}, bf16[768,128]{1,0:T(8,128)(2,1)S(1)}, u32[]{:S(2)}, u32[]{:S(2)}) collective-permute-start(bf16[768,128]{1,0:T(8,128)(2,1)S(1)} %get-tuple-element.57), channel_id=1, source_target_pairs={{0,32},{1,33},{2,34},{3,35},{4,36},{5,37},{6,38},{7,39},{8,40},{9,... | collective-permute-start | bytes 589832 | tf_op jit(solution)/shard_map/ppermute | solution.py:428
  79.6 2.2 %collective-permute-done.18.refs_4_ = bf16[768,128]{1,0:T(8,128)(2,1)S(1)} collective-permute-done((bf16[768,128]{1,0:T(8,128)(2,1)S(1)}, bf16[768,128]{1,0:T(8,128)(2,1)S(1)}, u32[]{:S(2)}, u32[]{:S(2)}) %collective-permute-start.18) | collective-permute-done | bytes 196640 | tf_op jit(solution)/shard_map/ppermute | solution.py:428
  81.8 0.7 sum_rows.1
  82.5 1.3 %collective-permute-done.19.other_ref = bf16[128,384]{1,0:T(8,128)(2,1)S(1)} collective-permute-done((bf16[128,384]{1,0:T(8,128)(2,1)S(1)}, bf16[128,384]{1,0:T(8,128)(2,1)S(1)}, u32[]{:S(2)}, u32[]{:S(2)}) %collective-permute-start.19) | collective-permute-done | bytes 98336 | tf_op jit(solution)/shard_map/ppermute | solution.py:507
  83.8 1.3 %project.1 = (bf16[128,1536]{1,0:T(8,128)(2,1)}, f32[8,128]{1,0:T(8,128)S(1)}) custom-call(bf16[128,384]{1,0:T(8,128)(2,1)S(1)} %get-tuple-element.51.own_ref, bf16[128,384]{1,0:T(8,128)(2,1)S(1)} %collective-permute-done.19.other_ref, bf16[384,1536]{1,0:T(8,128)(2,1)S(1)} %copy-done, bf16[384,1536]{1,0:T(8,128)(2,1)S(1)} %collective-permute-done.20.other_weight), custom_call_target="tpu_custom_call" | custom-call | flops 301989888 | bytes 2359296 | tf_op jit(solution)/shard_map/project/pallas_call | solution.py:31
  85.2 1.2 %collective-permute-done.22.refs_3_ = bf16[768,128]{1,0:T(8,128)(2,1)S(1)} collective-permute-done((bf16[768,128]{1,0:T(8,128)(2,1)S(1)}, bf16[768,128]{1,0:T(8,128)(2,1)S(1)}, u32[]{:S(2)}, u32[]{:S(2)}) %collective-permute-start.22) | collective-permute-done | bytes 196640 | tf_op jit(solution)/shard_map/ppermute | solution.py:428
  86.4 0.8 sum_keys.1
  (21 shorter events, 0.4 us)
Async XLA Ops:
  0.6 27.8 %copy-start = (bf16[384,1536]{1,0:T(8,128)(2,1)S(1)}, bf16[384,1536]{1,0:T(8,128)(2,1)}, u32[]{:S(2)}) copy-start(bf16[384,1536]{1,0:T(8,128)(2,1)} %own_weight.1) | copy-start | bytes 3538948
  3.5 10.4 %collective-permute-start.3 = (bf16[784,128]{1,0:T(8,128)(2,1)}, bf16[784,128]{1,0:T(8,128)(2,1)S(1)}, u32[]{:S(2)}, u32[]{:S(2)}) collective-permute-start(bf16[784,128]{1,0:T(8,128)(2,1)} %get-tuple-element.33), channel_id=1, source_target_pairs={{0,66},{1,65},{2,64},{3,67},{4,70},{5,69},{6,68},{7,71},{8,74},{9,... | collective-permute-start | bytes 602120 | tf_op jit(solution)/shard_map/ppermute | solution.py:428
  6.5 10.5 %collective-permute-start.4 = (bf16[784,128]{1,0:T(8,128)(2,1)}, bf16[784,128]{1,0:T(8,128)(2,1)S(1)}, u32[]{:S(2)}, u32[]{:S(2)}) collective-permute-start(bf16[784,128]{1,0:T(8,128)(2,1)} %get-tuple-element.33), channel_id=1, source_target_pairs={{0,8},{1,9},{2,10},{3,11},{4,12},{5,13},{6,14},{7,15},{8,0},{9,1},... | collective-permute-start | bytes 602120 | tf_op jit(solution)/shard_map/ppermute | solution.py:428
  9.7 9.5 %collective-permute-start.5 = (bf16[784,128]{1,0:T(8,128)(2,1)}, bf16[784,128]{1,0:T(8,128)(2,1)S(1)}, u32[]{:S(2)}, u32[]{:S(2)}) collective-permute-start(bf16[784,128]{1,0:T(8,128)(2,1)} %get-tuple-element.33), channel_id=1, source_target_pairs={{0,74},{1,73},{2,72},{3,75},{4,78},{5,77},{6,76},{7,79},{8,66},{9,... | collective-permute-start | bytes 602120 | tf_op jit(solution)/shard_map/ppermute | solution.py:428
  9.8 10.2 %collective-permute-start = (bf16[784,128]{1,0:T(8,128)(2,1)}, bf16[784,128]{1,0:T(8,128)(2,1)S(1)}, u32[]{:S(2)}, u32[]{:S(2)}) collective-permute-start(bf16[784,128]{1,0:T(8,128)(2,1)} %get-tuple-element.34), channel_id=1, source_target_pairs={{0,16},{1,17},{2,18},{3,19},{4,20},{5,21},{6,22},{7,23},{8,24},{9,... | collective-permute-start | bytes 602120 | tf_op jit(solution)/shard_map/ppermute | solution.py:428
  11.8 9.0 %collective-permute-start.1 = (bf16[784,128]{1,0:T(8,128)(2,1)}, bf16[784,128]{1,0:T(8,128)(2,1)S(1)}, u32[]{:S(2)}, u32[]{:S(2)}) collective-permute-start(bf16[784,128]{1,0:T(8,128)(2,1)} %get-tuple-element.34), channel_id=1, source_target_pairs={{0,48},{1,49},{2,50},{3,51},{4,52},{5,53},{6,54},{7,55},{8,56},{9,... | collective-permute-start | bytes 602120 | tf_op jit(solution)/shard_map/ppermute | solution.py:428
  13.9 8.7 %collective-permute-start.2 = (bf16[784,128]{1,0:T(8,128)(2,1)}, bf16[784,128]{1,0:T(8,128)(2,1)S(1)}, u32[]{:S(2)}, u32[]{:S(2)}) collective-permute-start(bf16[784,128]{1,0:T(8,128)(2,1)} %get-tuple-element.34), channel_id=1, source_target_pairs={{0,32},{1,33},{2,34},{3,35},{4,36},{5,37},{6,38},{7,39},{8,40},{9,... | collective-permute-start | bytes 602120 | tf_op jit(solution)/shard_map/ppermute | solution.py:428
  23.6 12.2 %collective-permute-start.6 = (bf16[4,784,128]{2,1,0:T(8,128)(2,1)S(1)}, bf16[4,784,128]{2,1,0:T(8,128)(2,1)S(1)}, u32[]{:S(2)}, u32[]{:S(2)}) collective-permute-start(bf16[4,784,128]{2,1,0:T(8,128)(2,1)S(1)} %pad_maximum_fusion.refs_2_.refs_4_.k_ref), channel_id=1, source_target_pairs={{0,64},{1,67},{2,66},{3,65},{4,68},{5,71},{6,70},{7,69},{8,72},{9,... | collective-permute-start | bytes 2408456 | tf_op jit(solution)/shard_map/ppermute | solution.py:428
  25.2 10.1 %collective-permute-start.7 = (bf16[2,784,128]{2,1,0:T(8,128)(2,1)S(1)}, bf16[2,784,128]{2,1,0:T(8,128)(2,1)S(1)}, u32[]{:S(2)}, u32[]{:S(2)}) collective-permute-start(bf16[2,784,128]{2,1,0:T(8,128)(2,1)S(1)} %pad_maximum_fusion.1.refs_0_), channel_id=1, source_target_pairs={{0,4},{1,5},{2,6},{3,7},{4,8},{5,9},{6,10},{7,11},{8,12},{9,13},{1... | collective-permute-start | bytes 1204232 | tf_op jit(solution)/shard_map/ppermute | solution.py:428
  26.7 8.6 %collective-permute-start.8 = (bf16[2,784,128]{2,1,0:T(8,128)(2,1)S(1)}, bf16[2,784,128]{2,1,0:T(8,128)(2,1)S(1)}, u32[]{:S(2)}, u32[]{:S(2)}) collective-permute-start(bf16[2,784,128]{2,1,0:T(8,128)(2,1)S(1)} %pad_maximum_fusion.1.refs_0_), channel_id=1, source_target_pairs={{0,12},{1,13},{2,14},{3,15},{4,0},{5,1},{6,2},{7,3},{8,4},{9,5},{1... | collective-permute-start | bytes 1204232 | tf_op jit(solution)/shard_map/ppermute | solution.py:428
  28.4 54.1 %collective-permute-start.20 = (bf16[384,1536]{1,0:T(8,128)(2,1)S(1)}, bf16[384,1536]{1,0:T(8,128)(2,1)S(1)}, u32[]{:S(2)}, u32[]{:S(2)}) collective-permute-start(bf16[384,1536]{1,0:T(8,128)(2,1)S(1)} %copy-done), channel_id=1, source_target_pairs={{0,1},{1,0},{2,3},{3,2},{4,5},{5,4},{6,7},{7,6},{8,9},{9,8},{10,11... | collective-permute-start | bytes 3538952 | tf_op jit(solution)/shard_map/ppermute | solution.py:472
  40.1 6.5 %collective-permute-start.9 = (f32[8,1024]{1,0:T(8,128)S(1)}, f32[8,1024]{1,0:T(8,128)S(1)}, u32[]{:S(2)}, u32[]{:S(2)}) collective-permute-start(f32[8,1024]{1,0:T(8,128)S(1)} %get-tuple-element.44.refs_0_.rows_ref), channel_id=1, source_target_pairs={{0,66},{1,65},{2,64},{3,67},{4,70},{5,69},{6,68},{7,71},{8,74},{9,... | collective-permute-start | bytes 98312 | tf_op jit(solution)/shard_map/ppermute | solution.py:428
  46.8 8.8 %collective-permute-start.10 = (f32[8,1024]{1,0:T(8,128)S(1)}, f32[8,1024]{1,0:T(8,128)S(1)}, u32[]{:S(2)}, u32[]{:S(2)}) collective-permute-start(f32[8,1024]{1,0:T(8,128)S(1)} %pair_rows.1.refs_0_), channel_id=1, source_target_pairs={{0,4},{1,5},{2,6},{3,7},{4,8},{5,9},{6,10},{7,11},{8,12},{9,13},{1... | collective-permute-start | bytes 98312 | tf_op jit(solution)/shard_map/ppermute | solution.py:428
  48.4 7.2 %collective-permute-start.11 = (f32[8,1024]{1,0:T(8,128)S(1)}, f32[8,1024]{1,0:T(8,128)S(1)}, u32[]{:S(2)}, u32[]{:S(2)}) collective-permute-start(f32[8,1024]{1,0:T(8,128)S(1)} %pair_rows.1.refs_0_), channel_id=1, source_target_pairs={{0,12},{1,13},{2,14},{3,15},{4,0},{5,1},{6,2},{7,3},{8,4},{9,5},{1... | collective-permute-start | bytes 98312 | tf_op jit(solution)/shard_map/ppermute | solution.py:428
  50.1 5.5 %collective-permute-start.12 = (f32[8,1024]{1,0:T(8,128)S(1)}, f32[8,1024]{1,0:T(8,128)S(1)}, u32[]{:S(2)}, u32[]{:S(2)}) collective-permute-start(f32[8,1024]{1,0:T(8,128)S(1)} %pair_rows.1.refs_0_), channel_id=1, source_target_pairs={{0,8},{1,9},{2,10},{3,11},{4,12},{5,13},{6,14},{7,15},{8,0},{9,1},... | collective-permute-start | bytes 98312 | tf_op jit(solution)/shard_map/ppermute | solution.py:428
  59.3 15.2 %collective-permute-start.17 = (bf16[4,768,128]{2,1,0:T(8,128)(2,1)S(1)}, bf16[4,768,128]{2,1,0:T(8,128)(2,1)S(1)}, u32[]{:S(2)}, u32[]{:S(2)}) collective-permute-start(bf16[4,768,128]{2,1,0:T(8,128)(2,1)S(1)} %backward_partner.1.later_ref), channel_id=1, source_target_pairs={{0,64},{1,67},{2,66},{3,65},{4,68},{5,71},{6,70},{7,69},{8,72},{9,... | collective-permute-start | bytes 2359304 | tf_op jit(solution)/shard_map/ppermute | solution.py:428
  61.4 13.4 %collective-permute-start.13 = (bf16[2,768,128]{2,1,0:T(8,128)(2,1)S(1)}, bf16[2,768,128]{2,1,0:T(8,128)(2,1)S(1)}, u32[]{:S(2)}, u32[]{:S(2)}) collective-permute-start(bf16[2,768,128]{2,1,0:T(8,128)(2,1)S(1)} %get-tuple-element.46), channel_id=1, source_target_pairs={{0,12},{1,13},{2,14},{3,15},{4,0},{5,1},{6,2},{7,3},{8,4},{9,5},{1... | collective-permute-start | bytes 1179656 | tf_op jit(solution)/shard_map/ppermute | solution.py:428
  63.1 11.6 %collective-permute-start.14 = (bf16[2,768,128]{2,1,0:T(8,128)(2,1)S(1)}, bf16[2,768,128]{2,1,0:T(8,128)(2,1)S(1)}, u32[]{:S(2)}, u32[]{:S(2)}) collective-permute-start(bf16[2,768,128]{2,1,0:T(8,128)(2,1)S(1)} %get-tuple-element.47), channel_id=1, source_target_pairs={{0,4},{1,5},{2,6},{3,7},{4,8},{5,9},{6,10},{7,11},{8,12},{9,13},{1... | collective-permute-start | bytes 1179656 | tf_op jit(solution)/shard_map/ppermute | solution.py:428
  63.5 6.9 %collective-permute-start.15 = (bf16[768,128]{1,0:T(8,128)(2,1)S(1)}, bf16[768,128]{1,0:T(8,128)(2,1)S(1)}, u32[]{:S(2)}, u32[]{:S(2)}) collective-permute-start(bf16[768,128]{1,0:T(8,128)(2,1)S(1)} %get-tuple-element.49), channel_id=1, source_target_pairs={{0,66},{1,65},{2,64},{3,67},{4,70},{5,69},{6,68},{7,71},{8,74},{9,... | collective-permute-start | bytes 589832 | tf_op jit(solution)/shard_map/ppermute | solution.py:428
  70.4 7.5 %collective-permute-start.16 = (bf16[768,128]{1,0:T(8,128)(2,1)S(1)}, bf16[768,128]{1,0:T(8,128)(2,1)S(1)}, u32[]{:S(2)}, u32[]{:S(2)}) collective-permute-start(bf16[768,128]{1,0:T(8,128)(2,1)S(1)} %sum_far.1), channel_id=1, source_target_pairs={{0,8},{1,9},{2,10},{3,11},{4,12},{5,13},{6,14},{7,15},{8,0},{9,1},... | collective-permute-start | bytes 589832 | tf_op jit(solution)/shard_map/ppermute | solution.py:428
  74.9 7.0 %collective-permute-start.18 = (bf16[768,128]{1,0:T(8,128)(2,1)S(1)}, bf16[768,128]{1,0:T(8,128)(2,1)S(1)}, u32[]{:S(2)}, u32[]{:S(2)}) collective-permute-start(bf16[768,128]{1,0:T(8,128)(2,1)S(1)} %sum_partner.1), channel_id=1, source_target_pairs={{0,66},{1,65},{2,64},{3,67},{4,70},{5,69},{6,68},{7,71},{8,74},{9,... | collective-permute-start | bytes 589832 | tf_op jit(solution)/shard_map/ppermute | solution.py:428
  75.9 9.3 %collective-permute-start.21 = (bf16[768,128]{1,0:T(8,128)(2,1)S(1)}, bf16[768,128]{1,0:T(8,128)(2,1)S(1)}, u32[]{:S(2)}, u32[]{:S(2)}) collective-permute-start(bf16[768,128]{1,0:T(8,128)(2,1)S(1)} %get-tuple-element.55), channel_id=1, source_target_pairs={{0,48},{1,49},{2,50},{3,51},{4,52},{5,53},{6,54},{7,55},{8,56},{9,... | collective-permute-start | bytes 589832 | tf_op jit(solution)/shard_map/ppermute | solution.py:428
  77.4 9.0 %collective-permute-start.22 = (bf16[768,128]{1,0:T(8,128)(2,1)S(1)}, bf16[768,128]{1,0:T(8,128)(2,1)S(1)}, u32[]{:S(2)}, u32[]{:S(2)}) collective-permute-start(bf16[768,128]{1,0:T(8,128)(2,1)S(1)} %get-tuple-element.56), channel_id=1, source_target_pairs={{0,16},{1,17},{2,18},{3,19},{4,20},{5,21},{6,22},{7,23},{8,24},{9,... | collective-permute-start | bytes 589832 | tf_op jit(solution)/shard_map/ppermute | solution.py:428
  77.9 8.5 %collective-permute-start.23 = (bf16[768,128]{1,0:T(8,128)(2,1)S(1)}, bf16[768,128]{1,0:T(8,128)(2,1)S(1)}, u32[]{:S(2)}, u32[]{:S(2)}) collective-permute-start(bf16[768,128]{1,0:T(8,128)(2,1)S(1)} %get-tuple-element.57), channel_id=1, source_target_pairs={{0,32},{1,33},{2,34},{3,35},{4,36},{5,37},{6,38},{7,39},{8,40},{9,... | collective-permute-start | bytes 589832 | tf_op jit(solution)/shard_map/ppermute | solution.py:428
  82.5 1.3 %collective-permute-start.19 = (bf16[128,384]{1,0:T(8,128)(2,1)S(1)}, bf16[128,384]{1,0:T(8,128)(2,1)S(1)}, u32[]{:S(2)}, u32[]{:S(2)}) collective-permute-start(bf16[128,384]{1,0:T(8,128)(2,1)S(1)} %get-tuple-element.51.own_ref), channel_id=1, source_target_pairs={{0,1},{1,0},{2,3},{3,2},{4,5},{5,4},{6,7},{7,6},{8,9},{9,8},{10,11... | collective-permute-start | bytes 294920 | tf_op jit(solution)/shard_map/ppermute | solution.py:507

commit v5 on v4

--- a/solution.py
+++ b/solution.py
@@ -147,12 +147,19 @@
         rows_ref[2 * h + 1 : 2 * h + 2, :] = delta / total
 
 
+def rows_to_cols(rows_ref, cols_ref):
+    rows = rows_ref[...]
+    rest = jnp.zeros((HD - rows.shape[0], rows.shape[1]), F32)
+    cols_ref[...] = jnp.transpose(jnp.concatenate([rows, rest], axis=0))
+
+
 def early_stats_kernel(*refs):
-    *chunks, key_ref, rows_ref, qmark, kmark, cols_ref = refs
+    *chunks, key_ref, cols_ref, rows_ref, qmark, kmark = refs
     fill_marks(chunks, qmark, False)
     fill_marks((key_ref,), kmark, True)
     chunks = [(chunk, i) for i, chunk in enumerate(chunks)]
     stats_part([((key_ref,), (kmark,), chunks)], qmark, cols_ref, rows_ref)
+    rows_to_cols(rows_ref, cols_ref)
 
 
 def all_stats_kernel(early, count, *refs):
@@ -178,16 +185,13 @@
             )
             rows_ref[r : r + 1, here] = norm
             rows_ref[r + 1 : r + 2, here] = delta
-    rows = rows_ref[...]
-    rest = jnp.zeros((HD - rows.shape[0], rows.shape[1]), F32)
-    cols_ref[...] = jnp.transpose(jnp.concatenate([rows, rest], axis=0))
+    rows_to_cols(rows_ref, cols_ref)
 
 
 def early_stats(chunks, key):
     n, m = len(chunks) * ROWS, key.shape[0] * TB
-    out = (shape((8, n), F32), shape((n, HD), BF16), shape((m, HD), BF16))
-    scratch = [pltpu.VMEM((n, HD), F32)]
-    return call(early_stats_kernel, "stats_early", out, (*chunks, key), scratch)
+    out = (shape((n, HD), F32), shape((8, n), F32), shape((n, HD), BF16), shape((m, HD), BF16))
+    return call(early_stats_kernel, "stats_early", out, (*chunks, key))
 
 
 def all_stats(early, chunks, *args):
@@ -197,30 +201,32 @@
     return call(kernel, "stats_all", out, (*chunks, *args))
 
 
-def forward_kernel(first, *refs):
-    *chunks, ko_ref, kx_ref, kmark_o, kmark_x, qmark, norm_ref, out_ref = refs
-    marks = jnp.concatenate([kmark_o[...], kmark_x[...]], axis=0)
+def forward_kernel(first, skips, parts, *refs):
+    count = len(skips)
+    chunks, keys, refs = refs[:count], refs[count : count + parts], refs[count + parts :]
+    kmarks, (qmark, norm_ref, out_ref) = refs[:parts], refs[parts:]
+    marks = jnp.concatenate([m[...] for m in kmarks], axis=0)
     for h in range(HP):
-        k = head_rows((ko_ref, kx_ref), h)
-        v = head_rows((ko_ref, kx_ref), HP + h)
+        k = head_rows(keys, h)
+        v = head_rows(keys, HP + h)
         k_marked = jnp.concatenate([k, marks], axis=1)
         vk = jnp.concatenate([v, k], axis=1)
-        for i, chunk in enumerate(chunks):
+        for i, (chunk, skip) in enumerate(zip(chunks, skips)):
             here = slice(i * ROWS, (i + 1) * ROWS)
             there = slice((first + i) * ROWS, (first + i + 1) * ROWS)
             q, g = chunk_rows(chunk, h), chunk_rows(chunk, HP + h)
-            scores = dot_nt(jnp.concatenate([q, qmark[there, :]], axis=1), k_marked)
+            scores = dot_nt(jnp.concatenate([q, qmark[there, :]], axis=1), k_marked[skip:])
             p = jnp.exp2(scores * C2 - norm_ref[there, 2 * h : 2 * h + 1])
-            mix = p * dot_nt(g, v)
-            out_ref[h, here, : 2 * HD] = dot_nn(p.astype(BF16), vk)
-            out_ref[h, here, 2 * HD :] = dot_nn(mix.astype(BF16), k)
-
-
-def forward(name, first, chunks, *args):
-    n, m = len(chunks) * ROWS, 2 * args[0].shape[0] * TB
+            mix = p * dot_nt(g, v[skip:])
+            out_ref[h, here, : 2 * HD] = dot_nn(p.astype(BF16), vk[skip:])
+            out_ref[h, here, 2 * HD :] = dot_nn(mix.astype(BF16), k[skip:])
+
+
+def forward(name, first, skips, chunks, keys, kmarks, qmark, cols, flops=0):
+    n = len(chunks) * ROWS
     return call(
-        functools.partial(forward_kernel, first), name, shape((HP, n, 3 * HD), F32),
-        (*chunks, *args), flops=12 * n * m * 2 * HD * HP, moved=8 * 2**20, exps=n * m * HP,
+        functools.partial(forward_kernel, first, skips, len(keys)), name,
+        shape((HP, n, 3 * HD), F32), (*chunks, *keys, *kmarks, qmark, cols), flops=flops,
     )
 
 
@@ -265,26 +271,38 @@
     return call(functools.partial(whole_kernel, steps), "whole_rows", out, (later, *members), anywhere=1)
 
 
-def share_kernel(chunks, later_ref, stat_ref, rows_ref, *refs):
+def share_kernel(chunks, early, later_ref, stat_ref, rows_ref, early_rows, *refs):
     del later_ref
-    outs, sends, partners = refs[:2], refs[2 : 2 + chunks], refs[2 + chunks :]
+    outs, early_out, sends, partners = refs[:2], refs[2], refs[3 : 3 + chunks], refs[3 + chunks :]
     partners = [None] * (chunks - len(partners)) + list(partners)
     rows = []
     for r in range(0, 2 * HP, 2):
         rows.append(jnp.exp2(rows_ref[r : r + 1, :] - stat_ref[r : r + 1, :]))
         rows.append(stat_ref[r + 1 : r + 2, :])
-    rows.append(jnp.zeros((TB - 2 * HP, chunks * ROWS), F32))
+        parts = [jnp.zeros((1, ROWS), F32)] * chunks
+        for j, i in enumerate(early):
+            then, here = slice(j * ROWS, (j + 1) * ROWS), slice(i * ROWS, (i + 1) * ROWS)
+            parts[i] = jnp.exp2(early_rows[r : r + 1, then] - stat_ref[r : r + 1, here])
+        rows.append(jnp.concatenate(parts, axis=1))
+    rows.append(jnp.zeros((TB - 3 * HP, chunks * ROWS), F32))
     cols = jnp.transpose(jnp.concatenate(rows, axis=0))
     for i, send_ref in enumerate(sends):
         here = slice(i * ROWS, (i + 1) * ROWS)
         out_ref, start = outs[i // (chunks // 2)], i % (chunks // 2) * ROWS
         there = slice(start, start + ROWS)
         for h in range(HP):
-            share = cols[here, 2 * h : 2 * h + 1]
-            delta = cols[here, 2 * h + 1 : 2 * h + 2]
-            attn, plain, mixed = (out_ref[h, there, c * HD : (c + 1) * HD] for c in range(3))
-            attn = (share * attn).astype(BF16)
-            grad = (share * SCALE * (mixed - delta * plain)).astype(BF16)
+            share, delta, early_share = (cols[here, 3 * h + c : 3 * h + c + 1] for c in range(3))
+            attn, plain, mixed = (
+                share * out_ref[h, there, c * HD : (c + 1) * HD] for c in range(3)
+            )
+            if i in early:
+                then = slice(early.index(i) * ROWS, (early.index(i) + 1) * ROWS)
+                more = [
+                    early_share * early_out[h, then, c * HD : (c + 1) * HD] for c in range(3)
+                ]
+                attn, plain, mixed = attn + more[0], plain + more[1], mixed + more[2]
+            attn = attn.astype(BF16)
+            grad = (SCALE * (mixed - delta * plain)).astype(BF16)
             for slot, value in ((h, attn), (HP + h, grad)):
                 there_rows = slice(slot * TB, (slot + 1) * TB)
                 send_ref[0, there_rows, :] = value[:TB]
@@ -294,12 +312,12 @@
                     partners[i][there_rows, :] = value[TB:]
 
 
-def shares(chunks, far, later, *args):
+def shares(chunks, far, early, later, *args):
     out = (shape((STEP, PR, HD), BF16),) * (chunks - far) + (shape((1, PR, HD), BF16),) * far
     out += (shape((PR, HD), BF16),) * far
     return call(
-        functools.partial(share_kernel, chunks), "share_rows", out, (later, *args), anywhere=1,
-        moved=4 * 2**20,
+        functools.partial(share_kernel, chunks, early), "share_rows", out, (later, *args),
+        anywhere=1, moved=4 * 2**20,
     )
 
 
@@ -473,7 +491,12 @@
 
     count = len(chunks)
     early = [i for i in range(count) if not 1 <= i <= len(near)]
-    early_rows, early_mark, kmark_o = early_stats([chunks[i] for i in early], ko)
+    some = [chunks[i] for i in early]
+    early_cols, early_rows, early_mark, kmark_o = early_stats(some, ko)
+    early_out = forward(
+        "forward_early", 0, [0] * len(early), some, [ko], [kmark_o], early_mark, early_cols
+    )
+    early_rows, _ = lax.optimization_barrier((early_rows, early_out))
     cols, rows, qmark, kmark_x = all_stats(early, chunks, ko, kx, kmark_o, early_mark, early_rows)
     got = places.query_partner(rows)
     halves = []
@@ -482,12 +505,14 @@
             pair_rows = pair(halves[0], rows, got)
             members = [pair_rows] + [places.along_y(pair_rows, d) for d in y_shifts[1:]]
         some = chunks[first : first + count // 2]
-        halves.append(forward(name, first, some, ko, kx, kmark_o, kmark_x, qmark, cols))
+        skips = [ko.shape[0] * TB * (first + i in early) for i in range(len(some))]
+        keys, kmarks = (ko, kx), (kmark_o, kmark_x)
+        halves.append(forward(name, first, skips, some, keys, kmarks, qmark, cols, 3 * 10**9))
     stat = whole(y_shifts, members, halves[1])
     key_partner = backward("backward_partner", kx, chunks, kmark_x, qmark, stat)
     key_got = places.key_partner(key_partner)
 
-    made = shares(count, len(far), key_partner, stat, rows, *halves)
+    made = shares(count, len(far), early, key_partner, stat, rows, early_rows, *halves, early_out)
     sends, far_partners = made[:count], made[count:]
     row_parts = [sends[0]] + [places.along_y(part, -d) for part, d in zip(sends[1:], near)]
     far_parts = sends[len(row_parts) :]

time: 87.4 us -> 87.1 us (level)
  waiting for transfers between devices: 20.3 us -> 17.9 us
  starting transfers between devices: 36.1 us -> 37.7 us
    ppermute x22, waiting for transfers between devices: 19 us -> 16.6 us  [send(): return lax.ppermute(array, ('row', 'col', 'head'), pairs)]
    ppermute x22, starting transfers between devices: 36.1 us -> 37.7 us  [send(): return lax.ppermute(array, ('row', 'col', 'head'), pairs)]
    pallas_call x16 -> x17, Pallas kernels: 28 us -> 28.5 us  [call(): pl.pallas_call(kernel, out_shape=out_shape, in_specs=[ANYWHERE] * anywher...]
  transfers between devices with their start and end apart: 24 -> 24, of which waited for: 12 -> 14; matrix products, arithmetic and copies ran while one was open for 1% -> 1% of each run, Pallas kernels for 28% -> 29%
where the time goes in v5:
time: 87.1 us; the launch traced here: 86.9 us
  starting transfers between devices  37.7 us (43%)
  Pallas kernels  28.5 us (33%)
  waiting for transfers between devices  17.9 us (21%)
  other arithmetic  2.03 us (2%)
    ppermute x22, starting transfers between devices, send(): return lax.ppermute(array, ('row', 'col', 'head'), pairs)  37.7 us
    pallas_call x17, Pallas kernels, call(): pl.pallas_call(kernel, out_shape=out_shape, in_specs=[ANYWHERE] * anywher...  28.5 us
    ppermute x22, waiting for transfers between devices, send(): return lax.ppermute(array, ('row', 'col', 'head'), pairs)  16.6 us
  transfers between devices with their start and end apart: 24, of which 14 were waited for; matrix products, arithmetic and copies ran while one was open for 1% of the time, Pallas kernels for 29%

profile of v5, /device:TPU:0, one launch (start us, length us, event | category | flops | bytes accessed | tf_op | source)
XLA Modules:
  0.0 86.9 jit_solution(13970529121054314396)
XLA Ops:
  0.6 2.9 %pack.1 = (bf16[784,128]{1,0:T(8,128)(2,1)}, bf16[784,128]{1,0:T(8,128)(2,1)}) custom-call(s32[1,128]{1,0:T(1,128)} %bitcast.17, bf16[128,384]{1,0:T(8,128)(2,1)} %refs_1_.1, bf16[128,384]{1,0:T(8,128)(2,1)} %refs_2_.1, bf16[128,384]{1,0:T(8,128)(2,1)} %refs_3_.1, bf16[128,1536]{1,0:T(8,128)(2,1)} %refs_4_.1, bf16[384,1536]{1,0:T(8,128)(2,1)} %own_weight.1), custom_call_target="tpu_custom_call" | custom-call | tf_op jit(solution)/shard_map/pack/pallas_call | solution.py:31
  3.5 2.9 %collective-permute-start.3 = (bf16[784,128]{1,0:T(8,128)(2,1)}, bf16[784,128]{1,0:T(8,128)(2,1)S(1)}, u32[]{:S(2)}, u32[]{:S(2)}) collective-permute-start(bf16[784,128]{1,0:T(8,128)(2,1)} %get-tuple-element.35), channel_id=1, source_target_pairs={{0,66},{1,65},{2,64},{3,67},{4,70},{5,69},{6,68},{7,71},{8,74},{9,... | collective-permute-start | bytes 602120 | tf_op jit(solution)/shard_map/ppermute | solution.py:446
  6.5 3.2 %collective-permute-start.4 = (bf16[784,128]{1,0:T(8,128)(2,1)}, bf16[784,128]{1,0:T(8,128)(2,1)S(1)}, u32[]{:S(2)}, u32[]{:S(2)}) collective-permute-start(bf16[784,128]{1,0:T(8,128)(2,1)} %get-tuple-element.35), channel_id=1, source_target_pairs={{0,8},{1,9},{2,10},{3,11},{4,12},{5,13},{6,14},{7,15},{8,0},{9,1},... | collective-permute-start | bytes 602120 | tf_op jit(solution)/shard_map/ppermute | solution.py:446
  9.8 2.0 %collective-permute-start = (bf16[784,128]{1,0:T(8,128)(2,1)}, bf16[784,128]{1,0:T(8,128)(2,1)S(1)}, u32[]{:S(2)}, u32[]{:S(2)}) collective-permute-start(bf16[784,128]{1,0:T(8,128)(2,1)} %get-tuple-element.36), channel_id=1, source_target_pairs={{0,16},{1,17},{2,18},{3,19},{4,20},{5,21},{6,22},{7,23},{8,24},{9,... | collective-permute-start | bytes 602120 | tf_op jit(solution)/shard_map/ppermute | solution.py:446
  11.8 2.1 %collective-permute-start.1 = (bf16[784,128]{1,0:T(8,128)(2,1)}, bf16[784,128]{1,0:T(8,128)(2,1)S(1)}, u32[]{:S(2)}, u32[]{:S(2)}) collective-permute-start(bf16[784,128]{1,0:T(8,128)(2,1)} %get-tuple-element.36), channel_id=1, source_target_pairs={{0,48},{1,49},{2,50},{3,51},{4,52},{5,53},{6,54},{7,55},{8,56},{9,... | collective-permute-start | bytes 602120 | tf_op jit(solution)/shard_map/ppermute | solution.py:446
  13.9 1.9 %collective-permute-start.2 = (bf16[784,128]{1,0:T(8,128)(2,1)}, bf16[784,128]{1,0:T(8,128)(2,1)S(1)}, u32[]{:S(2)}, u32[]{:S(2)}) collective-permute-start(bf16[784,128]{1,0:T(8,128)(2,1)} %get-tuple-element.36), channel_id=1, source_target_pairs={{0,32},{1,33},{2,34},{3,35},{4,36},{5,37},{6,38},{7,39},{8,40},{9,... | collective-permute-start | bytes 602120 | tf_op jit(solution)/shard_map/ppermute | solution.py:446
  15.8 1.0 %pad_maximum_fusion.1.refs_0_ = bf16[2,784,128]{2,1,0:T(8,128)(2,1)S(1)} fusion(bf16[1,784,128]{2,1,0:T(8,128)(2,1)S(1)} %bitcast.16, bf16[1,784,128]{2,1,0:T(8,128)(2,1)} %bitcast.15), kind=kLoop, calls=%fused_computation.1 | loop fusion | flops 200704 | bytes 802816 | tf_op jit(solution)/shard_map/stack | solution.py:477
  17.0 2.2 %collective-permute-done.5 = bf16[784,128]{1,0:T(8,128)(2,1)S(1)} collective-permute-done((bf16[784,128]{1,0:T(8,128)(2,1)}, bf16[784,128]{1,0:T(8,128)(2,1)S(1)}, u32[]{:S(2)}, u32[]{:S(2)}) %collective-permute-start.5) | collective-permute-done | bytes 200736 | tf_op jit(solution)/shard_map/ppermute | solution.py:446
  19.2 0.8 collective-permute-done
  20.0 0.8 collective-permute-done.1
  20.8 1.8 %collective-permute-done.2 = bf16[784,128]{1,0:T(8,128)(2,1)S(1)} collective-permute-done((bf16[784,128]{1,0:T(8,128)(2,1)}, bf16[784,128]{1,0:T(8,128)(2,1)S(1)}, u32[]{:S(2)}, u32[]{:S(2)}) %collective-permute-start.2) | collective-permute-done | bytes 200736 | tf_op jit(solution)/shard_map/ppermute | solution.py:446
  22.6 1.0 %pad_maximum_fusion.refs_2_.refs_4_.k_ref = bf16[4,784,128]{2,1,0:T(8,128)(2,1)S(1)} fusion(bf16[1,784,128]{2,1,0:T(8,128)(2,1)S(1)} %bitcast.12, bf16[1,784,128]{2,1,0:T(8,128)(2,1)S(1)} %bitcast.11, bf16[1,784,128]{2,1,0:T(8,128)(2,1)S(1)} %bitcast.10, bf16[1,784,128]{2,1,0:T(8,128)(2,1)} %bitcast.9), kind=kLoop, calls=%fused_computation | loop fusion | flops 1204224 | bytes 1605632 | tf_op jit(solution)/shard_map/stack | solution.py:488
  23.6 1.5 %collective-permute-start.6 = (bf16[4,784,128]{2,1,0:T(8,128)(2,1)S(1)}, bf16[4,784,128]{2,1,0:T(8,128)(2,1)S(1)}, u32[]{:S(2)}, u32[]{:S(2)}) collective-permute-start(bf16[4,784,128]{2,1,0:T(8,128)(2,1)S(1)} %pad_maximum_fusion.refs_2_.refs_4_.k_ref), channel_id=1, source_target_pairs={{0,64},{1,67},{2,66},{3,65},{4,68},{5,71},{6,70},{7,69},{8,72},{9,... | collective-permute-start | bytes 2408456 | tf_op jit(solution)/shard_map/ppermute | solution.py:446
  25.2 1.6 %collective-permute-start.7 = (bf16[2,784,128]{2,1,0:T(8,128)(2,1)S(1)}, bf16[2,784,128]{2,1,0:T(8,128)(2,1)S(1)}, u32[]{:S(2)}, u32[]{:S(2)}) collective-permute-start(bf16[2,784,128]{2,1,0:T(8,128)(2,1)S(1)} %pad_maximum_fusion.1.refs_0_), channel_id=1, source_target_pairs={{0,4},{1,5},{2,6},{3,7},{4,8},{5,9},{6,10},{7,11},{8,12},{9,13},{1... | collective-permute-start | bytes 1204232 | tf_op jit(solution)/shard_map/ppermute | solution.py:446
  26.7 1.7 %collective-permute-start.8 = (bf16[2,784,128]{2,1,0:T(8,128)(2,1)S(1)}, bf16[2,784,128]{2,1,0:T(8,128)(2,1)S(1)}, u32[]{:S(2)}, u32[]{:S(2)}) collective-permute-start(bf16[2,784,128]{2,1,0:T(8,128)(2,1)S(1)} %pad_maximum_fusion.1.refs_0_), channel_id=1, source_target_pairs={{0,12},{1,13},{2,14},{3,15},{4,0},{5,1},{6,2},{7,3},{8,4},{9,5},{1... | collective-permute-start | bytes 1204232 | tf_op jit(solution)/shard_map/ppermute | solution.py:446
  28.5 1.9 %stats_early.1 = (f32[512,128]{1,0:T(8,128)S(1)}, f32[8,512]{1,0:T(8,128)S(1)}, bf16[512,128]{1,0:T(8,128)(2,1)S(1)}, bf16[512,128]{1,0:T(8,128)(2,1)S(1)}) custom-call(bf16[2,784,128]{2,1,0:T(8,128)(2,1)S(1)} %pad_maximum_fusion.1.refs_0_, bf16[2,784,128]{2,1,0:T(8,128)(2,1)S(1)} %pad_maximum_fusion.2.refs_1_.refs_3_, ...), custom_call_target="tpu_custom_call" | custom-call | tf_op jit(solution)/shard_map/stats_early/pallas_call | solution.py:31
  30.3 1.9 %forward_early.1.refs_2_ = f32[3,512,384]{2,1,0:T(8,128)S(1)} custom-call(bf16[2,784,128]{2,1,0:T(8,128)(2,1)S(1)} %pad_maximum_fusion.1.refs_0_, bf16[2,784,128]{2,1,0:T(8,128)(2,1)S(1)} %pad_maximum_fusion.2.refs_1_.refs_3_, bf16[4,784,128]{2,1,0:T(8,128)(2,1)S(1)} %pad_maximum_fusion.refs_2_.refs_4_.k_ref, ...), custom_call_target="tpu_custom_call" | custom-call | tf_op jit(solution)/shard_map/forward_early/pallas_call | solution.py:31
  32.2 3.0 %collective-permute-done.7.refs_1_ = bf16[2,784,128]{2,1,0:T(8,128)(2,1)S(1)} collective-permute-done((bf16[2,784,128]{2,1,0:T(8,128)(2,1)S(1)}, bf16[2,784,128]{2,1,0:T(8,128)(2,1)S(1)}, u32[]{:S(2)}, u32[]{:S(2)}) %collective-permute-start.7) | collective-permute-done | bytes 401440 | tf_op jit(solution)/shard_map/ppermute | solution.py:446
  35.3 0.6 collective-permute-done.6.refs_5_.refs_3_.k_ref
  35.9 4.3 %stats_all.1 = (f32[1024,128]{1,0:T(8,128)S(1)}, f32[8,1024]{1,0:T(8,128)S(1)}, bf16[1024,128]{1,0:T(8,128)(2,1)S(1)}, bf16[512,128]{1,0:T(8,128)(2,1)S(1)}) custom-call(bf16[2,784,128]{2,1,0:T(8,128)(2,1)S(1)} %pad_maximum_fusion.1.refs_0_, bf16[2,784,128]{2,1,0:T(8,128)(2,1)S(1)} %collective-permute-done.7.refs_1_, ...), custom_call_target="tpu_custom_call" | custom-call | tf_op jit(solution)/shard_map/stats_all/pallas_call | solution.py:31
  40.2 3.0 %collective-permute-start.9 = (f32[8,1024]{1,0:T(8,128)S(1)}, f32[8,1024]{1,0:T(8,128)S(1)}, u32[]{:S(2)}, u32[]{:S(2)}) collective-permute-start(f32[8,1024]{1,0:T(8,128)S(1)} %get-tuple-element.48.refs_0_.rows_ref), channel_id=1, source_target_pairs={{0,66},{1,65},{2,64},{3,67},{4,70},{5,69},{6,68},{7,71},{8,74},{9,... | collective-permute-start | bytes 98312 | tf_op jit(solution)/shard_map/ppermute | solution.py:446
  43.2 2.8 %forward_near.1.later_ref.refs_0_ = f32[3,512,384]{2,1,0:T(8,128)S(1)} custom-call(bf16[2,784,128]{2,1,0:T(8,128)(2,1)S(1)} %pad_maximum_fusion.1.refs_0_, bf16[2,784,128]{2,1,0:T(8,128)(2,1)S(1)} %collective-permute-done.7.refs_1_, bf16[4,784,128]{2,1,0:T(8,128)(2,1)S(1)} %pad_maximum_fusion.refs_2_.refs_4_.k_ref, ...), custom_call_target="tpu_custom_call" | custom-call | flops 3000000000 | tf_op jit(solution)/shard_map/forward_near/pallas_call | solution.py:31
  46.1 1.6 %collective-permute-start.10 = (f32[8,1024]{1,0:T(8,128)S(1)}, f32[8,1024]{1,0:T(8,128)S(1)}, u32[]{:S(2)}, u32[]{:S(2)}) collective-permute-start(f32[8,1024]{1,0:T(8,128)S(1)} %pair_rows.1.refs_0_), channel_id=1, source_target_pairs={{0,4},{1,5},{2,6},{3,7},{4,8},{5,9},{6,10},{7,11},{8,12},{9,13},{1... | collective-permute-start | bytes 98312 | tf_op jit(solution)/shard_map/ppermute | solution.py:446
  47.7 1.7 %collective-permute-start.11 = (f32[8,1024]{1,0:T(8,128)S(1)}, f32[8,1024]{1,0:T(8,128)S(1)}, u32[]{:S(2)}, u32[]{:S(2)}) collective-permute-start(f32[8,1024]{1,0:T(8,128)S(1)} %pair_rows.1.refs_0_), channel_id=1, source_target_pairs={{0,12},{1,13},{2,14},{3,15},{4,0},{5,1},{6,2},{7,3},{8,4},{9,5},{1... | collective-permute-start | bytes 98312 | tf_op jit(solution)/shard_map/ppermute | solution.py:446
  49.4 2.0 %collective-permute-start.12 = (f32[8,1024]{1,0:T(8,128)S(1)}, f32[8,1024]{1,0:T(8,128)S(1)}, u32[]{:S(2)}, u32[]{:S(2)}) collective-permute-start(f32[8,1024]{1,0:T(8,128)S(1)} %pair_rows.1.refs_0_), channel_id=1, source_target_pairs={{0,8},{1,9},{2,10},{3,11},{4,12},{5,13},{6,14},{7,15},{8,0},{9,1},... | collective-permute-start | bytes 98312 | tf_op jit(solution)/shard_map/ppermute | solution.py:446
  51.4 2.8 %forward_far.1.later_ref.refs_1_ = f32[3,512,384]{2,1,0:T(8,128)S(1)} custom-call(bf16[2,784,128]{2,1,0:T(8,128)(2,1)S(1)} %collective-permute-done.8.refs_2_.refs_0_, bf16[2,784,128]{2,1,0:T(8,128)(2,1)S(1)} %pad_maximum_fusion.2.refs_1_.refs_3_, bf16[4,784,128]{2,1,0:T(8,128)(2,1)S(1)} %pad_maximum_fusion.refs_2_.refs_4_.k_ref, ...), custom_call_target="tpu_custom_call" | custom-call | flops 3000000000 | tf_op jit(solution)/shard_map/forward_far/pallas_call | solution.py:31
  54.2 0.6 collective-permute-done.12.refs_3_
  54.9 3.6 %backward_partner.1.later_ref = bf16[4,768,128]{2,1,0:T(8,128)(2,1)S(1)} custom-call(bf16[4,784,128]{2,1,0:T(8,128)(2,1)S(1)} %collective-permute-done.6.refs_5_.refs_3_.k_ref, bf16[2,784,128]{2,1,0:T(8,128)(2,1)S(1)} %pad_maximum_fusion.1.refs_0_, bf16[2,784,128]{2,1,0:T(8,128)(2,1)S(1)} %collective-permute-done.7.refs_1_, ...), custom_call_target="tpu_custom_call" | custom-call | flops 4026531840 | bytes 8388608 | tf_op jit(solution)/shard_map/backward_partner/pallas_call | solution.py:31
  58.5 0.3 collective-permute-start.17
  58.8 1.4 %share_rows.1 = (bf16[2,768,128]{2,1,0:T(8,128)(2,1)S(1)}, bf16[2,768,128]{2,1,0:T(8,128)(2,1)S(1)}, bf16[2,768,128]{2,1,0:T(8,128)(2,1)S(1)}, bf16[1,768,128]{2,1,0:T(8,128)(2,1)S(1)}, bf16[768,128]{1,0:T(8,128)(2,1)S(1)}) custom-call(bf16[4,768,128]{2,1,0:T(8,128)(2,1)S(1)} %backward_partner.1.later_ref, ...), custom_call_target="tpu_custom_call" | custom-call | bytes 4194304 | tf_op jit(solution)/shard_map/share_rows/pallas_call | solution.py:31
  60.3 2.1 %collective-permute-start.13 = (bf16[2,768,128]{2,1,0:T(8,128)(2,1)S(1)}, bf16[2,768,128]{2,1,0:T(8,128)(2,1)S(1)}, u32[]{:S(2)}, u32[]{:S(2)}) collective-permute-start(bf16[2,768,128]{2,1,0:T(8,128)(2,1)S(1)} %get-tuple-element.50), channel_id=1, source_target_pairs={{0,12},{1,13},{2,14},{3,15},{4,0},{5,1},{6,2},{7,3},{8,4},{9,5},{1... | collective-permute-start | bytes 1179656 | tf_op jit(solution)/shard_map/ppermute | solution.py:446
  62.3 0.2 collective-permute-start.14
  62.6 2.2 %collective-permute-start.15 = (bf16[768,128]{1,0:T(8,128)(2,1)S(1)}, bf16[768,128]{1,0:T(8,128)(2,1)S(1)}, u32[]{:S(2)}, u32[]{:S(2)}) collective-permute-start(bf16[768,128]{1,0:T(8,128)(2,1)S(1)} %get-tuple-element.53), channel_id=1, source_target_pairs={{0,66},{1,65},{2,64},{3,67},{4,70},{5,69},{6,68},{7,71},{8,74},{9,... | collective-permute-start | bytes 589832 | tf_op jit(solution)/shard_map/ppermute | solution.py:446
  64.7 3.6 %backward_own.1.later_ref.own_ref = bf16[4,768,128]{2,1,0:T(8,128)(2,1)S(1)} custom-call(bf16[4,784,128]{2,1,0:T(8,128)(2,1)S(1)} %pad_maximum_fusion.refs_2_.refs_4_.k_ref, bf16[2,784,128]{2,1,0:T(8,128)(2,1)S(1)} %pad_maximum_fusion.1.refs_0_, bf16[2,784,128]{2,1,0:T(8,128)(2,1)S(1)} %collective-permute-done.7.refs_1_, ...), custom_call_target="tpu_custom_call" | custom-call | flops 4026531840 | bytes 8388608 | tf_op jit(solution)/shard_map/backward_own/pallas_call | solution.py:31
  68.4 1.1 %collective-permute-done.15.got_ref = bf16[768,128]{1,0:T(8,128)(2,1)S(1)} collective-permute-done((bf16[768,128]{1,0:T(8,128)(2,1)S(1)}, bf16[768,128]{1,0:T(8,128)(2,1)S(1)}, u32[]{:S(2)}, u32[]{:S(2)}) %collective-permute-start.15) | collective-permute-done | bytes 196640 | tf_op jit(solution)/shard_map/ppermute | solution.py:446
  69.5 2.0 %collective-permute-start.16 = (bf16[768,128]{1,0:T(8,128)(2,1)S(1)}, bf16[768,128]{1,0:T(8,128)(2,1)S(1)}, u32[]{:S(2)}, u32[]{:S(2)}) collective-permute-start(bf16[768,128]{1,0:T(8,128)(2,1)S(1)} %sum_far.1), channel_id=1, source_target_pairs={{0,8},{1,9},{2,10},{3,11},{4,12},{5,13},{6,14},{7,15},{8,0},{9,1},... | collective-permute-start | bytes 589832 | tf_op jit(solution)/shard_map/ppermute | solution.py:446
  71.5 1.5 %collective-permute-done.17.got_ref = bf16[4,768,128]{2,1,0:T(8,128)(2,1)S(1)} collective-permute-done((bf16[4,768,128]{2,1,0:T(8,128)(2,1)S(1)}, bf16[4,768,128]{2,1,0:T(8,128)(2,1)S(1)}, u32[]{:S(2)}, u32[]{:S(2)}) %collective-permute-start.17) | collective-permute-done | bytes 786464 | tf_op jit(solution)/shard_map/ppermute | solution.py:446
  73.2 0.2 collective-permute-done.14.refs_2_
  73.5 1.9 %collective-permute-start.18 = (bf16[768,128]{1,0:T(8,128)(2,1)S(1)}, bf16[768,128]{1,0:T(8,128)(2,1)S(1)}, u32[]{:S(2)}, u32[]{:S(2)}) collective-permute-start(bf16[768,128]{1,0:T(8,128)(2,1)S(1)} %sum_partner.1), channel_id=1, source_target_pairs={{0,66},{1,65},{2,64},{3,67},{4,70},{5,69},{6,68},{7,71},{8,74},{9,... | collective-permute-start | bytes 589832 | tf_op jit(solution)/shard_map/ppermute | solution.py:446
  75.4 1.7 %collective-permute-start.21 = (bf16[768,128]{1,0:T(8,128)(2,1)S(1)}, bf16[768,128]{1,0:T(8,128)(2,1)S(1)}, u32[]{:S(2)}, u32[]{:S(2)}) collective-permute-start(bf16[768,128]{1,0:T(8,128)(2,1)S(1)} %get-tuple-element.59), channel_id=1, source_target_pairs={{0,48},{1,49},{2,50},{3,51},{4,52},{5,53},{6,54},{7,55},{8,56},{9,... | collective-permute-start | bytes 589832 | tf_op jit(solution)/shard_map/ppermute | solution.py:446
  77.2 0.3 collective-permute-start.22
  77.4 1.6 %collective-permute-start.23 = (bf16[768,128]{1,0:T(8,128)(2,1)S(1)}, bf16[768,128]{1,0:T(8,128)(2,1)S(1)}, u32[]{:S(2)}, u32[]{:S(2)}) collective-permute-start(bf16[768,128]{1,0:T(8,128)(2,1)S(1)} %get-tuple-element.61), channel_id=1, source_target_pairs={{0,32},{1,33},{2,34},{3,35},{4,36},{5,37},{6,38},{7,39},{8,40},{9,... | collective-permute-start | bytes 589832 | tf_op jit(solution)/shard_map/ppermute | solution.py:446
  79.1 1.4 %collective-permute-done.18.refs_4_ = bf16[768,128]{1,0:T(8,128)(2,1)S(1)} collective-permute-done((bf16[768,128]{1,0:T(8,128)(2,1)S(1)}, bf16[768,128]{1,0:T(8,128)(2,1)S(1)}, u32[]{:S(2)}, u32[]{:S(2)}) %collective-permute-start.18) | collective-permute-done | bytes 196640 | tf_op jit(solution)/shard_map/ppermute | solution.py:446
  80.5 0.7 sum_rows.1
  81.2 1.3 %collective-permute-done.19.other_ref = bf16[128,384]{1,0:T(8,128)(2,1)S(1)} collective-permute-done((bf16[128,384]{1,0:T(8,128)(2,1)S(1)}, bf16[128,384]{1,0:T(8,128)(2,1)S(1)}, u32[]{:S(2)}, u32[]{:S(2)}) %collective-permute-start.19) | collective-permute-done | bytes 98336 | tf_op jit(solution)/shard_map/ppermute | solution.py:532
  82.5 1.3 %project.1 = (bf16[128,1536]{1,0:T(8,128)(2,1)}, f32[8,128]{1,0:T(8,128)S(1)}) custom-call(bf16[128,384]{1,0:T(8,128)(2,1)S(1)} %get-tuple-element.55.own_ref, bf16[128,384]{1,0:T(8,128)(2,1)S(1)} %collective-permute-done.19.other_ref, bf16[384,1536]{1,0:T(8,128)(2,1)S(1)} %copy-done, bf16[384,1536]{1,0:T(8,128)(2,1)S(1)} %collective-permute-done.20.other_weight), custom_call_target="tpu_custom_call" | custom-call | flops 301989888 | bytes 2359296 | tf_op jit(solution)/shard_map/project/pallas_call | solution.py:31
  83.8 2.3 %collective-permute-done.22.refs_3_ = bf16[768,128]{1,0:T(8,128)(2,1)S(1)} collective-permute-done((bf16[768,128]{1,0:T(8,128)(2,1)S(1)}, bf16[768,128]{1,0:T(8,128)(2,1)S(1)}, u32[]{:S(2)}, u32[]{:S(2)}) %collective-permute-start.22) | collective-permute-done | bytes 196640 | tf_op jit(solution)/shard_map/ppermute | solution.py:446
  86.1 0.8 sum_keys.1
  (22 shorter events, 0.9 us)
Async XLA Ops:
  0.6 27.8 %copy-start = (bf16[384,1536]{1,0:T(8,128)(2,1)S(1)}, bf16[384,1536]{1,0:T(8,128)(2,1)}, u32[]{:S(2)}) copy-start(bf16[384,1536]{1,0:T(8,128)(2,1)} %own_weight.1) | copy-start | bytes 3538948
  3.5 10.4 %collective-permute-start.3 = (bf16[784,128]{1,0:T(8,128)(2,1)}, bf16[784,128]{1,0:T(8,128)(2,1)S(1)}, u32[]{:S(2)}, u32[]{:S(2)}) collective-permute-start(bf16[784,128]{1,0:T(8,128)(2,1)} %get-tuple-element.35), channel_id=1, source_target_pairs={{0,66},{1,65},{2,64},{3,67},{4,70},{5,69},{6,68},{7,71},{8,74},{9,... | collective-permute-start | bytes 602120 | tf_op jit(solution)/shard_map/ppermute | solution.py:446
  6.5 10.5 %collective-permute-start.4 = (bf16[784,128]{1,0:T(8,128)(2,1)}, bf16[784,128]{1,0:T(8,128)(2,1)S(1)}, u32[]{:S(2)}, u32[]{:S(2)}) collective-permute-start(bf16[784,128]{1,0:T(8,128)(2,1)} %get-tuple-element.35), channel_id=1, source_target_pairs={{0,8},{1,9},{2,10},{3,11},{4,12},{5,13},{6,14},{7,15},{8,0},{9,1},... | collective-permute-start | bytes 602120 | tf_op jit(solution)/shard_map/ppermute | solution.py:446
  9.7 9.5 %collective-permute-start.5 = (bf16[784,128]{1,0:T(8,128)(2,1)}, bf16[784,128]{1,0:T(8,128)(2,1)S(1)}, u32[]{:S(2)}, u32[]{:S(2)}) collective-permute-start(bf16[784,128]{1,0:T(8,128)(2,1)} %get-tuple-element.35), channel_id=1, source_target_pairs={{0,74},{1,73},{2,72},{3,75},{4,78},{5,77},{6,76},{7,79},{8,66},{9,... | collective-permute-start | bytes 602120 | tf_op jit(solution)/shard_map/ppermute | solution.py:446
  9.8 10.2 %collective-permute-start = (bf16[784,128]{1,0:T(8,128)(2,1)}, bf16[784,128]{1,0:T(8,128)(2,1)S(1)}, u32[]{:S(2)}, u32[]{:S(2)}) collective-permute-start(bf16[784,128]{1,0:T(8,128)(2,1)} %get-tuple-element.36), channel_id=1, source_target_pairs={{0,16},{1,17},{2,18},{3,19},{4,20},{5,21},{6,22},{7,23},{8,24},{9,... | collective-permute-start | bytes 602120 | tf_op jit(solution)/shard_map/ppermute | solution.py:446
  11.8 9.0 %collective-permute-start.1 = (bf16[784,128]{1,0:T(8,128)(2,1)}, bf16[784,128]{1,0:T(8,128)(2,1)S(1)}, u32[]{:S(2)}, u32[]{:S(2)}) collective-permute-start(bf16[784,128]{1,0:T(8,128)(2,1)} %get-tuple-element.36), channel_id=1, source_target_pairs={{0,48},{1,49},{2,50},{3,51},{4,52},{5,53},{6,54},{7,55},{8,56},{9,... | collective-permute-start | bytes 602120 | tf_op jit(solution)/shard_map/ppermute | solution.py:446
  13.9 8.7 %collective-permute-start.2 = (bf16[784,128]{1,0:T(8,128)(2,1)}, bf16[784,128]{1,0:T(8,128)(2,1)S(1)}, u32[]{:S(2)}, u32[]{:S(2)}) collective-permute-start(bf16[784,128]{1,0:T(8,128)(2,1)} %get-tuple-element.36), channel_id=1, source_target_pairs={{0,32},{1,33},{2,34},{3,35},{4,36},{5,37},{6,38},{7,39},{8,40},{9,... | collective-permute-start | bytes 602120 | tf_op jit(solution)/shard_map/ppermute | solution.py:446
  23.6 12.2 %collective-permute-start.6 = (bf16[4,784,128]{2,1,0:T(8,128)(2,1)S(1)}, bf16[4,784,128]{2,1,0:T(8,128)(2,1)S(1)}, u32[]{:S(2)}, u32[]{:S(2)}) collective-permute-start(bf16[4,784,128]{2,1,0:T(8,128)(2,1)S(1)} %pad_maximum_fusion.refs_2_.refs_4_.k_ref), channel_id=1, source_target_pairs={{0,64},{1,67},{2,66},{3,65},{4,68},{5,71},{6,70},{7,69},{8,72},{9,... | collective-permute-start | bytes 2408456 | tf_op jit(solution)/shard_map/ppermute | solution.py:446
  25.2 10.1 %collective-permute-start.7 = (bf16[2,784,128]{2,1,0:T(8,128)(2,1)S(1)}, bf16[2,784,128]{2,1,0:T(8,128)(2,1)S(1)}, u32[]{:S(2)}, u32[]{:S(2)}) collective-permute-start(bf16[2,784,128]{2,1,0:T(8,128)(2,1)S(1)} %pad_maximum_fusion.1.refs_0_), channel_id=1, source_target_pairs={{0,4},{1,5},{2,6},{3,7},{4,8},{5,9},{6,10},{7,11},{8,12},{9,13},{1... | collective-permute-start | bytes 1204232 | tf_op jit(solution)/shard_map/ppermute | solution.py:446
  26.7 8.6 %collective-permute-start.8 = (bf16[2,784,128]{2,1,0:T(8,128)(2,1)S(1)}, bf16[2,784,128]{2,1,0:T(8,128)(2,1)S(1)}, u32[]{:S(2)}, u32[]{:S(2)}) collective-permute-start(bf16[2,784,128]{2,1,0:T(8,128)(2,1)S(1)} %pad_maximum_fusion.1.refs_0_), channel_id=1, source_target_pairs={{0,12},{1,13},{2,14},{3,15},{4,0},{5,1},{6,2},{7,3},{8,4},{9,5},{1... | collective-permute-start | bytes 1204232 | tf_op jit(solution)/shard_map/ppermute | solution.py:446
  28.4 52.8 %collective-permute-start.20 = (bf16[384,1536]{1,0:T(8,128)(2,1)S(1)}, bf16[384,1536]{1,0:T(8,128)(2,1)S(1)}, u32[]{:S(2)}, u32[]{:S(2)}) collective-permute-start(bf16[384,1536]{1,0:T(8,128)(2,1)S(1)} %copy-done), channel_id=1, source_target_pairs={{0,1},{1,0},{2,3},{3,2},{4,5},{5,4},{6,7},{7,6},{8,9},{9,8},{10,11... | collective-permute-start | bytes 3538952 | tf_op jit(solution)/shard_map/ppermute | solution.py:490
  40.2 5.8 %collective-permute-start.9 = (f32[8,1024]{1,0:T(8,128)S(1)}, f32[8,1024]{1,0:T(8,128)S(1)}, u32[]{:S(2)}, u32[]{:S(2)}) collective-permute-start(f32[8,1024]{1,0:T(8,128)S(1)} %get-tuple-element.48.refs_0_.rows_ref), channel_id=1, source_target_pairs={{0,66},{1,65},{2,64},{3,67},{4,70},{5,69},{6,68},{7,71},{8,74},{9,... | collective-permute-start | bytes 98312 | tf_op jit(solution)/shard_map/ppermute | solution.py:446
  46.1 8.1 %collective-permute-start.10 = (f32[8,1024]{1,0:T(8,128)S(1)}, f32[8,1024]{1,0:T(8,128)S(1)}, u32[]{:S(2)}, u32[]{:S(2)}) collective-permute-start(f32[8,1024]{1,0:T(8,128)S(1)} %pair_rows.1.refs_0_), channel_id=1, source_target_pairs={{0,4},{1,5},{2,6},{3,7},{4,8},{5,9},{6,10},{7,11},{8,12},{9,13},{1... | collective-permute-start | bytes 98312 | tf_op jit(solution)/shard_map/ppermute | solution.py:446
  47.7 6.4 %collective-permute-start.11 = (f32[8,1024]{1,0:T(8,128)S(1)}, f32[8,1024]{1,0:T(8,128)S(1)}, u32[]{:S(2)}, u32[]{:S(2)}) collective-permute-start(f32[8,1024]{1,0:T(8,128)S(1)} %pair_rows.1.refs_0_), channel_id=1, source_target_pairs={{0,12},{1,13},{2,14},{3,15},{4,0},{5,1},{6,2},{7,3},{8,4},{9,5},{1... | collective-permute-start | bytes 98312 | tf_op jit(solution)/shard_map/ppermute | solution.py:446
  49.4 5.4 %collective-permute-start.12 = (f32[8,1024]{1,0:T(8,128)S(1)}, f32[8,1024]{1,0:T(8,128)S(1)}, u32[]{:S(2)}, u32[]{:S(2)}) collective-permute-start(f32[8,1024]{1,0:T(8,128)S(1)} %pair_rows.1.refs_0_), channel_id=1, source_target_pairs={{0,8},{1,9},{2,10},{3,11},{4,12},{5,13},{6,14},{7,15},{8,0},{9,1},... | collective-permute-start | bytes 98312 | tf_op jit(solution)/shard_map/ppermute | solution.py:446
  58.5 14.5 %collective-permute-start.17 = (bf16[4,768,128]{2,1,0:T(8,128)(2,1)S(1)}, bf16[4,768,128]{2,1,0:T(8,128)(2,1)S(1)}, u32[]{:S(2)}, u32[]{:S(2)}) collective-permute-start(bf16[4,768,128]{2,1,0:T(8,128)(2,1)S(1)} %backward_partner.1.later_ref), channel_id=1, source_target_pairs={{0,64},{1,67},{2,66},{3,65},{4,68},{5,71},{6,70},{7,69},{8,72},{9,... | collective-permute-start | bytes 2359304 | tf_op jit(solution)/shard_map/ppermute | solution.py:446
  60.3 13.0 %collective-permute-start.13 = (bf16[2,768,128]{2,1,0:T(8,128)(2,1)S(1)}, bf16[2,768,128]{2,1,0:T(8,128)(2,1)S(1)}, u32[]{:S(2)}, u32[]{:S(2)}) collective-permute-start(bf16[2,768,128]{2,1,0:T(8,128)(2,1)S(1)} %get-tuple-element.50), channel_id=1, source_target_pairs={{0,12},{1,13},{2,14},{3,15},{4,0},{5,1},{6,2},{7,3},{8,4},{9,5},{1... | collective-permute-start | bytes 1179656 | tf_op jit(solution)/shard_map/ppermute | solution.py:446
  62.3 11.1 %collective-permute-start.14 = (bf16[2,768,128]{2,1,0:T(8,128)(2,1)S(1)}, bf16[2,768,128]{2,1,0:T(8,128)(2,1)S(1)}, u32[]{:S(2)}, u32[]{:S(2)}) collective-permute-start(bf16[2,768,128]{2,1,0:T(8,128)(2,1)S(1)} %get-tuple-element.51), channel_id=1, source_target_pairs={{0,4},{1,5},{2,6},{3,7},{4,8},{5,9},{6,10},{7,11},{8,12},{9,13},{1... | collective-permute-start | bytes 1179656 | tf_op jit(solution)/shard_map/ppermute | solution.py:446
  62.6 6.9 %collective-permute-start.15 = (bf16[768,128]{1,0:T(8,128)(2,1)S(1)}, bf16[768,128]{1,0:T(8,128)(2,1)S(1)}, u32[]{:S(2)}, u32[]{:S(2)}) collective-permute-start(bf16[768,128]{1,0:T(8,128)(2,1)S(1)} %get-tuple-element.53), channel_id=1, source_target_pairs={{0,66},{1,65},{2,64},{3,67},{4,70},{5,69},{6,68},{7,71},{8,74},{9,... | collective-permute-start | bytes 589832 | tf_op jit(solution)/shard_map/ppermute | solution.py:446
  69.5 7.9 %collective-permute-start.16 = (bf16[768,128]{1,0:T(8,128)(2,1)S(1)}, bf16[768,128]{1,0:T(8,128)(2,1)S(1)}, u32[]{:S(2)}, u32[]{:S(2)}) collective-permute-start(bf16[768,128]{1,0:T(8,128)(2,1)S(1)} %sum_far.1), channel_id=1, source_target_pairs={{0,8},{1,9},{2,10},{3,11},{4,12},{5,13},{6,14},{7,15},{8,0},{9,1},... | collective-permute-start | bytes 589832 | tf_op jit(solution)/shard_map/ppermute | solution.py:446
  73.5 7.0 %collective-permute-start.18 = (bf16[768,128]{1,0:T(8,128)(2,1)S(1)}, bf16[768,128]{1,0:T(8,128)(2,1)S(1)}, u32[]{:S(2)}, u32[]{:S(2)}) collective-permute-start(bf16[768,128]{1,0:T(8,128)(2,1)S(1)} %sum_partner.1), channel_id=1, source_target_pairs={{0,66},{1,65},{2,64},{3,67},{4,70},{5,69},{6,68},{7,71},{8,74},{9,... | collective-permute-start | bytes 589832 | tf_op jit(solution)/shard_map/ppermute | solution.py:446
  75.4 8.4 %collective-permute-start.21 = (bf16[768,128]{1,0:T(8,128)(2,1)S(1)}, bf16[768,128]{1,0:T(8,128)(2,1)S(1)}, u32[]{:S(2)}, u32[]{:S(2)}) collective-permute-start(bf16[768,128]{1,0:T(8,128)(2,1)S(1)} %get-tuple-element.59), channel_id=1, source_target_pairs={{0,48},{1,49},{2,50},{3,51},{4,52},{5,53},{6,54},{7,55},{8,56},{9,... | collective-permute-start | bytes 589832 | tf_op jit(solution)/shard_map/ppermute | solution.py:446
  77.2 9.0 %collective-permute-start.22 = (bf16[768,128]{1,0:T(8,128)(2,1)S(1)}, bf16[768,128]{1,0:T(8,128)(2,1)S(1)}, u32[]{:S(2)}, u32[]{:S(2)}) collective-permute-start(bf16[768,128]{1,0:T(8,128)(2,1)S(1)} %get-tuple-element.60), channel_id=1, source_target_pairs={{0,16},{1,17},{2,18},{3,19},{4,20},{5,21},{6,22},{7,23},{8,24},{9,... | collective-permute-start | bytes 589832 | tf_op jit(solution)/shard_map/ppermute | solution.py:446
  77.4 8.7 %collective-permute-start.23 = (bf16[768,128]{1,0:T(8,128)(2,1)S(1)}, bf16[768,128]{1,0:T(8,128)(2,1)S(1)}, u32[]{:S(2)}, u32[]{:S(2)}) collective-permute-start(bf16[768,128]{1,0:T(8,128)(2,1)S(1)} %get-tuple-element.61), channel_id=1, source_target_pairs={{0,32},{1,33},{2,34},{3,35},{4,36},{5,37},{6,38},{7,39},{8,40},{9,... | collective-permute-start | bytes 589832 | tf_op jit(solution)/shard_map/ppermute | solution.py:446
  81.2 1.3 %collective-permute-start.19 = (bf16[128,384]{1,0:T(8,128)(2,1)S(1)}, bf16[128,384]{1,0:T(8,128)(2,1)S(1)}, u32[]{:S(2)}, u32[]{:S(2)}) collective-permute-start(bf16[128,384]{1,0:T(8,128)(2,1)S(1)} %get-tuple-element.55.own_ref), channel_id=1, source_target_pairs={{0,1},{1,0},{2,3},{3,2},{4,5},{5,4},{6,7},{7,6},{8,9},{9,8},{10,11... | collective-permute-start | bytes 294920 | tf_op jit(solution)/shard_map/ppermute | solution.py:532

commit v6 on v5

--- a/solution.py
+++ b/solution.py
@@ -527,7 +527,7 @@
     key_parts = [key_parts[0]] + [
         places.along_z(part, -d) for part, d in zip(key_parts[1:], z_shifts[1:])
     ]
-    row_got = places.query_partner(partner_sum(row_parts, key_parts[0]))
+    row_got = places.query_partner(partner_sum(row_parts, key_own))
     attn, grad_queries = sum_parts(row_parts + far_parts + [row_got], "sum_rows")
     other_attn = lax.ppermute(attn, "head", swap)
     mixed_output, token = project(attn, other_attn, out_weight, other_weight)

time: 87.1 us -> 86 us (0.987)
  waiting for transfers between devices: 17.9 us -> 16.9 us
    ppermute x22, waiting for transfers between devices: 16.6 us -> 15.6 us  [send(): return lax.ppermute(array, ('row', 'col', 'head'), pairs)]
  transfers between devices with their start and end apart: 24 -> 24, of which waited for: 14 -> 13; matrix products, arithmetic and copies ran while one was open for 1% -> 1% of each run, Pallas kernels for 29% -> 29%
where the time goes in v6:
time: 86 us; the launch traced here: 85.8 us
  starting transfers between devices  37.9 us (44%)
  Pallas kernels  28.2 us (33%)
  waiting for transfers between devices  16.9 us (20%)
  other arithmetic  2.03 us (2%)
    ppermute x22, starting transfers between devices, send(): return lax.ppermute(array, ('row', 'col', 'head'), pairs)  37.9 us
    pallas_call x17, Pallas kernels, call(): pl.pallas_call(kernel, out_shape=out_shape, in_specs=[ANYWHERE] * anywher...  28.2 us
    ppermute x22, waiting for transfers between devices, send(): return lax.ppermute(array, ('row', 'col', 'head'), pairs)  15.6 us
  transfers between devices with their start and end apart: 24, of which 13 were waited for; matrix products, arithmetic and copies ran while one was open for 1% of the time, Pallas kernels for 29%

profile of v6, /device:TPU:0, one launch (start us, length us, event | category | flops | bytes accessed | tf_op | source)
XLA Modules:
  0.0 85.8 jit_solution(7174967170736486189)
XLA Ops:
  0.6 2.9 %pack.1 = (bf16[784,128]{1,0:T(8,128)(2,1)}, bf16[784,128]{1,0:T(8,128)(2,1)}) custom-call(s32[1,128]{1,0:T(1,128)} %bitcast.17, bf16[128,384]{1,0:T(8,128)(2,1)} %refs_1_.1, bf16[128,384]{1,0:T(8,128)(2,1)} %refs_2_.1, bf16[128,384]{1,0:T(8,128)(2,1)} %refs_3_.1, bf16[128,1536]{1,0:T(8,128)(2,1)} %refs_4_.1, bf16[384,1536]{1,0:T(8,128)(2,1)} %own_weight.1), custom_call_target="tpu_custom_call" | custom-call | tf_op jit(solution)/shard_map/pack/pallas_call | solution.py:31
  3.5 2.9 %collective-permute-start.3 = (bf16[784,128]{1,0:T(8,128)(2,1)}, bf16[784,128]{1,0:T(8,128)(2,1)S(1)}, u32[]{:S(2)}, u32[]{:S(2)}) collective-permute-start(bf16[784,128]{1,0:T(8,128)(2,1)} %get-tuple-element.35), channel_id=1, source_target_pairs={{0,66},{1,65},{2,64},{3,67},{4,70},{5,69},{6,68},{7,71},{8,74},{9,... | collective-permute-start | bytes 602120 | tf_op jit(solution)/shard_map/ppermute | solution.py:446
  6.5 3.2 %collective-permute-start.4 = (bf16[784,128]{1,0:T(8,128)(2,1)}, bf16[784,128]{1,0:T(8,128)(2,1)S(1)}, u32[]{:S(2)}, u32[]{:S(2)}) collective-permute-start(bf16[784,128]{1,0:T(8,128)(2,1)} %get-tuple-element.35), channel_id=1, source_target_pairs={{0,8},{1,9},{2,10},{3,11},{4,12},{5,13},{6,14},{7,15},{8,0},{9,1},... | collective-permute-start | bytes 602120 | tf_op jit(solution)/shard_map/ppermute | solution.py:446
  9.8 2.0 %collective-permute-start = (bf16[784,128]{1,0:T(8,128)(2,1)}, bf16[784,128]{1,0:T(8,128)(2,1)S(1)}, u32[]{:S(2)}, u32[]{:S(2)}) collective-permute-start(bf16[784,128]{1,0:T(8,128)(2,1)} %get-tuple-element.36), channel_id=1, source_target_pairs={{0,16},{1,17},{2,18},{3,19},{4,20},{5,21},{6,22},{7,23},{8,24},{9,... | collective-permute-start | bytes 602120 | tf_op jit(solution)/shard_map/ppermute | solution.py:446
  11.8 2.1 %collective-permute-start.1 = (bf16[784,128]{1,0:T(8,128)(2,1)}, bf16[784,128]{1,0:T(8,128)(2,1)S(1)}, u32[]{:S(2)}, u32[]{:S(2)}) collective-permute-start(bf16[784,128]{1,0:T(8,128)(2,1)} %get-tuple-element.36), channel_id=1, source_target_pairs={{0,48},{1,49},{2,50},{3,51},{4,52},{5,53},{6,54},{7,55},{8,56},{9,... | collective-permute-start | bytes 602120 | tf_op jit(solution)/shard_map/ppermute | solution.py:446
  13.9 1.9 %collective-permute-start.2 = (bf16[784,128]{1,0:T(8,128)(2,1)}, bf16[784,128]{1,0:T(8,128)(2,1)S(1)}, u32[]{:S(2)}, u32[]{:S(2)}) collective-permute-start(bf16[784,128]{1,0:T(8,128)(2,1)} %get-tuple-element.36), channel_id=1, source_target_pairs={{0,32},{1,33},{2,34},{3,35},{4,36},{5,37},{6,38},{7,39},{8,40},{9,... | collective-permute-start | bytes 602120 | tf_op jit(solution)/shard_map/ppermute | solution.py:446
  15.8 1.0 %pad_maximum_fusion.1.refs_0_ = bf16[2,784,128]{2,1,0:T(8,128)(2,1)S(1)} fusion(bf16[1,784,128]{2,1,0:T(8,128)(2,1)S(1)} %bitcast.16, bf16[1,784,128]{2,1,0:T(8,128)(2,1)} %bitcast.15), kind=kLoop, calls=%fused_computation.1 | loop fusion | flops 200704 | bytes 802816 | tf_op jit(solution)/shard_map/stack | solution.py:477
  16.8 0.2 collective-permute-done.4
  17.0 2.2 %collective-permute-done.5 = bf16[784,128]{1,0:T(8,128)(2,1)S(1)} collective-permute-done((bf16[784,128]{1,0:T(8,128)(2,1)}, bf16[784,128]{1,0:T(8,128)(2,1)S(1)}, u32[]{:S(2)}, u32[]{:S(2)}) %collective-permute-start.5) | collective-permute-done | bytes 200736 | tf_op jit(solution)/shard_map/ppermute | solution.py:446
  19.2 0.8 collective-permute-done
  20.0 0.8 collective-permute-done.1
  20.8 1.8 %collective-permute-done.2 = bf16[784,128]{1,0:T(8,128)(2,1)S(1)} collective-permute-done((bf16[784,128]{1,0:T(8,128)(2,1)}, bf16[784,128]{1,0:T(8,128)(2,1)S(1)}, u32[]{:S(2)}, u32[]{:S(2)}) %collective-permute-start.2) | collective-permute-done | bytes 200736 | tf_op jit(solution)/shard_map/ppermute | solution.py:446
  22.6 1.0 %pad_maximum_fusion.refs_2_.refs_4_.k_ref = bf16[4,784,128]{2,1,0:T(8,128)(2,1)S(1)} fusion(bf16[1,784,128]{2,1,0:T(8,128)(2,1)S(1)} %bitcast.12, bf16[1,784,128]{2,1,0:T(8,128)(2,1)S(1)} %bitcast.11, bf16[1,784,128]{2,1,0:T(8,128)(2,1)S(1)} %bitcast.10, bf16[1,784,128]{2,1,0:T(8,128)(2,1)} %bitcast.9), kind=kLoop, calls=%fused_computation | loop fusion | flops 1204224 | bytes 1605632 | tf_op jit(solution)/shard_map/stack | solution.py:488
  23.6 1.5 %collective-permute-start.6 = (bf16[4,784,128]{2,1,0:T(8,128)(2,1)S(1)}, bf16[4,784,128]{2,1,0:T(8,128)(2,1)S(1)}, u32[]{:S(2)}, u32[]{:S(2)}) collective-permute-start(bf16[4,784,128]{2,1,0:T(8,128)(2,1)S(1)} %pad_maximum_fusion.refs_2_.refs_4_.k_ref), channel_id=1, source_target_pairs={{0,64},{1,67},{2,66},{3,65},{4,68},{5,71},{6,70},{7,69},{8,72},{9,... | collective-permute-start | bytes 2408456 | tf_op jit(solution)/shard_map/ppermute | solution.py:446
  25.2 1.6 %collective-permute-start.7 = (bf16[2,784,128]{2,1,0:T(8,128)(2,1)S(1)}, bf16[2,784,128]{2,1,0:T(8,128)(2,1)S(1)}, u32[]{:S(2)}, u32[]{:S(2)}) collective-permute-start(bf16[2,784,128]{2,1,0:T(8,128)(2,1)S(1)} %pad_maximum_fusion.1.refs_0_), channel_id=1, source_target_pairs={{0,4},{1,5},{2,6},{3,7},{4,8},{5,9},{6,10},{7,11},{8,12},{9,13},{1... | collective-permute-start | bytes 1204232 | tf_op jit(solution)/shard_map/ppermute | solution.py:446
  26.7 1.7 %collective-permute-start.8 = (bf16[2,784,128]{2,1,0:T(8,128)(2,1)S(1)}, bf16[2,784,128]{2,1,0:T(8,128)(2,1)S(1)}, u32[]{:S(2)}, u32[]{:S(2)}) collective-permute-start(bf16[2,784,128]{2,1,0:T(8,128)(2,1)S(1)} %pad_maximum_fusion.1.refs_0_), channel_id=1, source_target_pairs={{0,12},{1,13},{2,14},{3,15},{4,0},{5,1},{6,2},{7,3},{8,4},{9,5},{1... | collective-permute-start | bytes 1204232 | tf_op jit(solution)/shard_map/ppermute | solution.py:446
  28.5 1.9 %stats_early.1 = (f32[512,128]{1,0:T(8,128)S(1)}, f32[8,512]{1,0:T(8,128)S(1)}, bf16[512,128]{1,0:T(8,128)(2,1)S(1)}, bf16[512,128]{1,0:T(8,128)(2,1)S(1)}) custom-call(bf16[2,784,128]{2,1,0:T(8,128)(2,1)S(1)} %pad_maximum_fusion.1.refs_0_, bf16[2,784,128]{2,1,0:T(8,128)(2,1)S(1)} %pad_maximum_fusion.2.refs_1_.refs_3_, ...), custom_call_target="tpu_custom_call" | custom-call | tf_op jit(solution)/shard_map/stats_early/pallas_call | solution.py:31
  30.3 1.9 %forward_early.1.refs_2_ = f32[3,512,384]{2,1,0:T(8,128)S(1)} custom-call(bf16[2,784,128]{2,1,0:T(8,128)(2,1)S(1)} %pad_maximum_fusion.1.refs_0_, bf16[2,784,128]{2,1,0:T(8,128)(2,1)S(1)} %pad_maximum_fusion.2.refs_1_.refs_3_, bf16[4,784,128]{2,1,0:T(8,128)(2,1)S(1)} %pad_maximum_fusion.refs_2_.refs_4_.k_ref, ...), custom_call_target="tpu_custom_call" | custom-call | tf_op jit(solution)/shard_map/forward_early/pallas_call | solution.py:31
  32.2 3.0 %collective-permute-done.7.refs_1_ = bf16[2,784,128]{2,1,0:T(8,128)(2,1)S(1)} collective-permute-done((bf16[2,784,128]{2,1,0:T(8,128)(2,1)S(1)}, bf16[2,784,128]{2,1,0:T(8,128)(2,1)S(1)}, u32[]{:S(2)}, u32[]{:S(2)}) %collective-permute-start.7) | collective-permute-done | bytes 401440 | tf_op jit(solution)/shard_map/ppermute | solution.py:446
  35.3 0.6 collective-permute-done.6.refs_5_.refs_3_.k_ref
  35.9 4.2 %stats_all.1 = (f32[1024,128]{1,0:T(8,128)S(1)}, f32[8,1024]{1,0:T(8,128)S(1)}, bf16[1024,128]{1,0:T(8,128)(2,1)S(1)}, bf16[512,128]{1,0:T(8,128)(2,1)S(1)}) custom-call(bf16[2,784,128]{2,1,0:T(8,128)(2,1)S(1)} %pad_maximum_fusion.1.refs_0_, bf16[2,784,128]{2,1,0:T(8,128)(2,1)S(1)} %collective-permute-done.7.refs_1_, ...), custom_call_target="tpu_custom_call" | custom-call | tf_op jit(solution)/shard_map/stats_all/pallas_call | solution.py:31
  40.1 3.0 %collective-permute-start.9 = (f32[8,1024]{1,0:T(8,128)S(1)}, f32[8,1024]{1,0:T(8,128)S(1)}, u32[]{:S(2)}, u32[]{:S(2)}) collective-permute-start(f32[8,1024]{1,0:T(8,128)S(1)} %get-tuple-element.48.refs_0_.rows_ref), channel_id=1, source_target_pairs={{0,66},{1,65},{2,64},{3,67},{4,70},{5,69},{6,68},{7,71},{8,74},{9,... | collective-permute-start | bytes 98312 | tf_op jit(solution)/shard_map/ppermute | solution.py:446
  43.1 2.8 %forward_near.1.later_ref.refs_0_ = f32[3,512,384]{2,1,0:T(8,128)S(1)} custom-call(bf16[2,784,128]{2,1,0:T(8,128)(2,1)S(1)} %pad_maximum_fusion.1.refs_0_, bf16[2,784,128]{2,1,0:T(8,128)(2,1)S(1)} %collective-permute-done.7.refs_1_, bf16[4,784,128]{2,1,0:T(8,128)(2,1)S(1)} %pad_maximum_fusion.refs_2_.refs_4_.k_ref, ...), custom_call_target="tpu_custom_call" | custom-call | flops 3000000000 | tf_op jit(solution)/shard_map/forward_near/pallas_call | solution.py:31
  46.0 1.6 %collective-permute-start.10 = (f32[8,1024]{1,0:T(8,128)S(1)}, f32[8,1024]{1,0:T(8,128)S(1)}, u32[]{:S(2)}, u32[]{:S(2)}) collective-permute-start(f32[8,1024]{1,0:T(8,128)S(1)} %pair_rows.1.refs_0_), channel_id=1, source_target_pairs={{0,4},{1,5},{2,6},{3,7},{4,8},{5,9},{6,10},{7,11},{8,12},{9,13},{1... | collective-permute-start | bytes 98312 | tf_op jit(solution)/shard_map/ppermute | solution.py:446
  47.6 1.7 %collective-permute-start.11 = (f32[8,1024]{1,0:T(8,128)S(1)}, f32[8,1024]{1,0:T(8,128)S(1)}, u32[]{:S(2)}, u32[]{:S(2)}) collective-permute-start(f32[8,1024]{1,0:T(8,128)S(1)} %pair_rows.1.refs_0_), channel_id=1, source_target_pairs={{0,12},{1,13},{2,14},{3,15},{4,0},{5,1},{6,2},{7,3},{8,4},{9,5},{1... | collective-permute-start | bytes 98312 | tf_op jit(solution)/shard_map/ppermute | solution.py:446
  49.3 2.0 %collective-permute-start.12 = (f32[8,1024]{1,0:T(8,128)S(1)}, f32[8,1024]{1,0:T(8,128)S(1)}, u32[]{:S(2)}, u32[]{:S(2)}) collective-permute-start(f32[8,1024]{1,0:T(8,128)S(1)} %pair_rows.1.refs_0_), channel_id=1, source_target_pairs={{0,8},{1,9},{2,10},{3,11},{4,12},{5,13},{6,14},{7,15},{8,0},{9,1},... | collective-permute-start | bytes 98312 | tf_op jit(solution)/shard_map/ppermute | solution.py:446
  51.2 2.7 %forward_far.1.later_ref.refs_1_ = f32[3,512,384]{2,1,0:T(8,128)S(1)} custom-call(bf16[2,784,128]{2,1,0:T(8,128)(2,1)S(1)} %collective-permute-done.8.refs_2_.refs_0_, bf16[2,784,128]{2,1,0:T(8,128)(2,1)S(1)} %pad_maximum_fusion.2.refs_1_.refs_3_, bf16[4,784,128]{2,1,0:T(8,128)(2,1)S(1)} %pad_maximum_fusion.refs_2_.refs_4_.k_ref, ...), custom_call_target="tpu_custom_call" | custom-call | flops 3000000000 | tf_op jit(solution)/shard_map/forward_far/pallas_call | solution.py:31
  54.0 0.7 collective-permute-done.12.refs_3_
  54.8 3.6 %backward_partner.1.later_ref = bf16[4,768,128]{2,1,0:T(8,128)(2,1)S(1)} custom-call(bf16[4,784,128]{2,1,0:T(8,128)(2,1)S(1)} %collective-permute-done.6.refs_5_.refs_3_.k_ref, bf16[2,784,128]{2,1,0:T(8,128)(2,1)S(1)} %pad_maximum_fusion.1.refs_0_, bf16[2,784,128]{2,1,0:T(8,128)(2,1)S(1)} %collective-permute-done.7.refs_1_, ...), custom_call_target="tpu_custom_call" | custom-call | flops 4026531840 | bytes 8388608 | tf_op jit(solution)/shard_map/backward_partner/pallas_call | solution.py:31
  58.4 0.3 collective-permute-start.20
  58.6 1.4 %share_rows.1 = (bf16[2,768,128]{2,1,0:T(8,128)(2,1)S(1)}, bf16[2,768,128]{2,1,0:T(8,128)(2,1)S(1)}, bf16[2,768,128]{2,1,0:T(8,128)(2,1)S(1)}, bf16[1,768,128]{2,1,0:T(8,128)(2,1)S(1)}, bf16[768,128]{1,0:T(8,128)(2,1)S(1)}) custom-call(bf16[4,768,128]{2,1,0:T(8,128)(2,1)S(1)} %backward_partner.1.later_ref, ...), custom_call_target="tpu_custom_call" | custom-call | bytes 4194304 | tf_op jit(solution)/shard_map/share_rows/pallas_call | solution.py:31
  60.1 2.1 %collective-permute-start.13 = (bf16[2,768,128]{2,1,0:T(8,128)(2,1)S(1)}, bf16[2,768,128]{2,1,0:T(8,128)(2,1)S(1)}, u32[]{:S(2)}, u32[]{:S(2)}) collective-permute-start(bf16[2,768,128]{2,1,0:T(8,128)(2,1)S(1)} %get-tuple-element.50), channel_id=1, source_target_pairs={{0,12},{1,13},{2,14},{3,15},{4,0},{5,1},{6,2},{7,3},{8,4},{9,5},{1... | collective-permute-start | bytes 1179656 | tf_op jit(solution)/shard_map/ppermute | solution.py:446
  62.2 0.2 collective-permute-start.14
  62.4 2.2 %collective-permute-start.15 = (bf16[768,128]{1,0:T(8,128)(2,1)S(1)}, bf16[768,128]{1,0:T(8,128)(2,1)S(1)}, u32[]{:S(2)}, u32[]{:S(2)}) collective-permute-start(bf16[768,128]{1,0:T(8,128)(2,1)S(1)} %get-tuple-element.53), channel_id=1, source_target_pairs={{0,66},{1,65},{2,64},{3,67},{4,70},{5,69},{6,68},{7,71},{8,74},{9,... | collective-permute-start | bytes 589832 | tf_op jit(solution)/shard_map/ppermute | solution.py:446
  64.6 3.6 %backward_own.1.later_ref.own_ref = bf16[4,768,128]{2,1,0:T(8,128)(2,1)S(1)} custom-call(bf16[4,784,128]{2,1,0:T(8,128)(2,1)S(1)} %pad_maximum_fusion.refs_2_.refs_4_.k_ref, bf16[2,784,128]{2,1,0:T(8,128)(2,1)S(1)} %pad_maximum_fusion.1.refs_0_, bf16[2,784,128]{2,1,0:T(8,128)(2,1)S(1)} %collective-permute-done.7.refs_1_, ...), custom_call_target="tpu_custom_call" | custom-call | flops 4026531840 | bytes 8388608 | tf_op jit(solution)/shard_map/backward_own/pallas_call | solution.py:31
  68.2 1.1 %collective-permute-done.15.got_ref = bf16[768,128]{1,0:T(8,128)(2,1)S(1)} collective-permute-done((bf16[768,128]{1,0:T(8,128)(2,1)S(1)}, bf16[768,128]{1,0:T(8,128)(2,1)S(1)}, u32[]{:S(2)}, u32[]{:S(2)}) %collective-permute-start.15) | collective-permute-done | bytes 196640 | tf_op jit(solution)/shard_map/ppermute | solution.py:446
  69.3 2.1 %collective-permute-start.16 = (bf16[768,128]{1,0:T(8,128)(2,1)S(1)}, bf16[768,128]{1,0:T(8,128)(2,1)S(1)}, u32[]{:S(2)}, u32[]{:S(2)}) collective-permute-start(bf16[768,128]{1,0:T(8,128)(2,1)S(1)} %sum_far.1), channel_id=1, source_target_pairs={{0,8},{1,9},{2,10},{3,11},{4,12},{5,13},{6,14},{7,15},{8,0},{9,1},... | collective-permute-start | bytes 589832 | tf_op jit(solution)/shard_map/ppermute | solution.py:446
  71.4 1.8 %collective-permute-done.14.refs_2_ = bf16[2,768,128]{2,1,0:T(8,128)(2,1)S(1)} collective-permute-done((bf16[2,768,128]{2,1,0:T(8,128)(2,1)S(1)}, bf16[2,768,128]{2,1,0:T(8,128)(2,1)S(1)}, u32[]{:S(2)}, u32[]{:S(2)}) %collective-permute-start.14) | collective-permute-done | bytes 393248 | tf_op jit(solution)/shard_map/ppermute | solution.py:446
  73.3 1.2 %collective-permute-start.17 = (bf16[768,128]{1,0:T(8,128)(2,1)S(1)}, bf16[768,128]{1,0:T(8,128)(2,1)S(1)}, u32[]{:S(2)}, u32[]{:S(2)}) collective-permute-start(bf16[768,128]{1,0:T(8,128)(2,1)S(1)} %sum_partner.1), channel_id=1, source_target_pairs={{0,66},{1,65},{2,64},{3,67},{4,70},{5,69},{6,68},{7,71},{8,74},{9,... | collective-permute-start | bytes 589832 | tf_op jit(solution)/shard_map/ppermute | solution.py:446
  74.7 1.3 %collective-permute-start.21 = (bf16[768,128]{1,0:T(8,128)(2,1)S(1)}, bf16[768,128]{1,0:T(8,128)(2,1)S(1)}, u32[]{:S(2)}, u32[]{:S(2)}) collective-permute-start(bf16[768,128]{1,0:T(8,128)(2,1)S(1)} %get-tuple-element.59), channel_id=1, source_target_pairs={{0,48},{1,49},{2,50},{3,51},{4,52},{5,53},{6,54},{7,55},{8,56},{9,... | collective-permute-start | bytes 589832 | tf_op jit(solution)/shard_map/ppermute | solution.py:446
  76.0 0.8 collective-permute-start.22
  76.8 2.4 %collective-permute-start.23 = (bf16[768,128]{1,0:T(8,128)(2,1)S(1)}, bf16[768,128]{1,0:T(8,128)(2,1)S(1)}, u32[]{:S(2)}, u32[]{:S(2)}) collective-permute-start(bf16[768,128]{1,0:T(8,128)(2,1)S(1)} %get-tuple-element.61), channel_id=1, source_target_pairs={{0,32},{1,33},{2,34},{3,35},{4,36},{5,37},{6,38},{7,39},{8,40},{9,... | collective-permute-start | bytes 589832 | tf_op jit(solution)/shard_map/ppermute | solution.py:446
  79.2 1.1 %collective-permute-done.17.refs_4_ = bf16[768,128]{1,0:T(8,128)(2,1)S(1)} collective-permute-done((bf16[768,128]{1,0:T(8,128)(2,1)S(1)}, bf16[768,128]{1,0:T(8,128)(2,1)S(1)}, u32[]{:S(2)}, u32[]{:S(2)}) %collective-permute-start.17) | collective-permute-done | bytes 196640 | tf_op jit(solution)/shard_map/ppermute | solution.py:446
  80.3 0.7 sum_rows.1
  81.0 1.3 %collective-permute-done.18.other_ref = bf16[128,384]{1,0:T(8,128)(2,1)S(1)} collective-permute-done((bf16[128,384]{1,0:T(8,128)(2,1)S(1)}, bf16[128,384]{1,0:T(8,128)(2,1)S(1)}, u32[]{:S(2)}, u32[]{:S(2)}) %collective-permute-start.18) | collective-permute-done | bytes 98336 | tf_op jit(solution)/shard_map/ppermute | solution.py:532
  82.3 1.3 %project.1 = (bf16[128,1536]{1,0:T(8,128)(2,1)}, f32[8,128]{1,0:T(8,128)S(1)}) custom-call(bf16[128,384]{1,0:T(8,128)(2,1)S(1)} %get-tuple-element.54.own_ref, bf16[128,384]{1,0:T(8,128)(2,1)S(1)} %collective-permute-done.18.other_ref, bf16[384,1536]{1,0:T(8,128)(2,1)S(1)} %copy-done, bf16[384,1536]{1,0:T(8,128)(2,1)S(1)} %collective-permute-done.19.other_weight), custom_call_target="tpu_custom_call" | custom-call | flops 301989888 | bytes 2359296 | tf_op jit(solution)/shard_map/project/pallas_call | solution.py:31
  83.6 1.4 %collective-permute-done.23.refs_4_ = bf16[768,128]{1,0:T(8,128)(2,1)S(1)} collective-permute-done((bf16[768,128]{1,0:T(8,128)(2,1)S(1)}, bf16[768,128]{1,0:T(8,128)(2,1)S(1)}, u32[]{:S(2)}, u32[]{:S(2)}) %collective-permute-start.23) | collective-permute-done | bytes 196640 | tf_op jit(solution)/shard_map/ppermute | solution.py:446
  85.0 0.8 sum_keys.1
  (22 shorter events, 0.8 us)
Async XLA Ops:
  0.6 27.8 %copy-start = (bf16[384,1536]{1,0:T(8,128)(2,1)S(1)}, bf16[384,1536]{1,0:T(8,128)(2,1)}, u32[]{:S(2)}) copy-start(bf16[384,1536]{1,0:T(8,128)(2,1)} %own_weight.1) | copy-start | bytes 3538948
  3.5 10.4 %collective-permute-start.3 = (bf16[784,128]{1,0:T(8,128)(2,1)}, bf16[784,128]{1,0:T(8,128)(2,1)S(1)}, u32[]{:S(2)}, u32[]{:S(2)}) collective-permute-start(bf16[784,128]{1,0:T(8,128)(2,1)} %get-tuple-element.35), channel_id=1, source_target_pairs={{0,66},{1,65},{2,64},{3,67},{4,70},{5,69},{6,68},{7,71},{8,74},{9,... | collective-permute-start | bytes 602120 | tf_op jit(solution)/shard_map/ppermute | solution.py:446
  6.5 10.5 %collective-permute-start.4 = (bf16[784,128]{1,0:T(8,128)(2,1)}, bf16[784,128]{1,0:T(8,128)(2,1)S(1)}, u32[]{:S(2)}, u32[]{:S(2)}) collective-permute-start(bf16[784,128]{1,0:T(8,128)(2,1)} %get-tuple-element.35), channel_id=1, source_target_pairs={{0,8},{1,9},{2,10},{3,11},{4,12},{5,13},{6,14},{7,15},{8,0},{9,1},... | collective-permute-start | bytes 602120 | tf_op jit(solution)/shard_map/ppermute | solution.py:446
  9.7 9.5 %collective-permute-start.5 = (bf16[784,128]{1,0:T(8,128)(2,1)}, bf16[784,128]{1,0:T(8,128)(2,1)S(1)}, u32[]{:S(2)}, u32[]{:S(2)}) collective-permute-start(bf16[784,128]{1,0:T(8,128)(2,1)} %get-tuple-element.35), channel_id=1, source_target_pairs={{0,74},{1,73},{2,72},{3,75},{4,78},{5,77},{6,76},{7,79},{8,66},{9,... | collective-permute-start | bytes 602120 | tf_op jit(solution)/shard_map/ppermute | solution.py:446
  9.8 10.2 %collective-permute-start = (bf16[784,128]{1,0:T(8,128)(2,1)}, bf16[784,128]{1,0:T(8,128)(2,1)S(1)}, u32[]{:S(2)}, u32[]{:S(2)}) collective-permute-start(bf16[784,128]{1,0:T(8,128)(2,1)} %get-tuple-element.36), channel_id=1, source_target_pairs={{0,16},{1,17},{2,18},{3,19},{4,20},{5,21},{6,22},{7,23},{8,24},{9,... | collective-permute-start | bytes 602120 | tf_op jit(solution)/shard_map/ppermute | solution.py:446
  11.8 9.0 %collective-permute-start.1 = (bf16[784,128]{1,0:T(8,128)(2,1)}, bf16[784,128]{1,0:T(8,128)(2,1)S(1)}, u32[]{:S(2)}, u32[]{:S(2)}) collective-permute-start(bf16[784,128]{1,0:T(8,128)(2,1)} %get-tuple-element.36), channel_id=1, source_target_pairs={{0,48},{1,49},{2,50},{3,51},{4,52},{5,53},{6,54},{7,55},{8,56},{9,... | collective-permute-start | bytes 602120 | tf_op jit(solution)/shard_map/ppermute | solution.py:446
  13.9 8.7 %collective-permute-start.2 = (bf16[784,128]{1,0:T(8,128)(2,1)}, bf16[784,128]{1,0:T(8,128)(2,1)S(1)}, u32[]{:S(2)}, u32[]{:S(2)}) collective-permute-start(bf16[784,128]{1,0:T(8,128)(2,1)} %get-tuple-element.36), channel_id=1, source_target_pairs={{0,32},{1,33},{2,34},{3,35},{4,36},{5,37},{6,38},{7,39},{8,40},{9,... | collective-permute-start | bytes 602120 | tf_op jit(solution)/shard_map/ppermute | solution.py:446
  23.6 12.2 %collective-permute-start.6 = (bf16[4,784,128]{2,1,0:T(8,128)(2,1)S(1)}, bf16[4,784,128]{2,1,0:T(8,128)(2,1)S(1)}, u32[]{:S(2)}, u32[]{:S(2)}) collective-permute-start(bf16[4,784,128]{2,1,0:T(8,128)(2,1)S(1)} %pad_maximum_fusion.refs_2_.refs_4_.k_ref), channel_id=1, source_target_pairs={{0,64},{1,67},{2,66},{3,65},{4,68},{5,71},{6,70},{7,69},{8,72},{9,... | collective-permute-start | bytes 2408456 | tf_op jit(solution)/shard_map/ppermute | solution.py:446
  25.2 10.1 %collective-permute-start.7 = (bf16[2,784,128]{2,1,0:T(8,128)(2,1)S(1)}, bf16[2,784,128]{2,1,0:T(8,128)(2,1)S(1)}, u32[]{:S(2)}, u32[]{:S(2)}) collective-permute-start(bf16[2,784,128]{2,1,0:T(8,128)(2,1)S(1)} %pad_maximum_fusion.1.refs_0_), channel_id=1, source_target_pairs={{0,4},{1,5},{2,6},{3,7},{4,8},{5,9},{6,10},{7,11},{8,12},{9,13},{1... | collective-permute-start | bytes 1204232 | tf_op jit(solution)/shard_map/ppermute | solution.py:446
  26.7 8.6 %collective-permute-start.8 = (bf16[2,784,128]{2,1,0:T(8,128)(2,1)S(1)}, bf16[2,784,128]{2,1,0:T(8,128)(2,1)S(1)}, u32[]{:S(2)}, u32[]{:S(2)}) collective-permute-start(bf16[2,784,128]{2,1,0:T(8,128)(2,1)S(1)} %pad_maximum_fusion.1.refs_0_), channel_id=1, source_target_pairs={{0,12},{1,13},{2,14},{3,15},{4,0},{5,1},{6,2},{7,3},{8,4},{9,5},{1... | collective-permute-start | bytes 1204232 | tf_op jit(solution)/shard_map/ppermute | solution.py:446
  28.4 52.6 %collective-permute-start.19 = (bf16[384,1536]{1,0:T(8,128)(2,1)S(1)}, bf16[384,1536]{1,0:T(8,128)(2,1)S(1)}, u32[]{:S(2)}, u32[]{:S(2)}) collective-permute-start(bf16[384,1536]{1,0:T(8,128)(2,1)S(1)} %copy-done), channel_id=1, source_target_pairs={{0,1},{1,0},{2,3},{3,2},{4,5},{5,4},{6,7},{7,6},{8,9},{9,8},{10,11... | collective-permute-start | bytes 3538952 | tf_op jit(solution)/shard_map/ppermute | solution.py:490
  40.1 5.8 %collective-permute-start.9 = (f32[8,1024]{1,0:T(8,128)S(1)}, f32[8,1024]{1,0:T(8,128)S(1)}, u32[]{:S(2)}, u32[]{:S(2)}) collective-permute-start(f32[8,1024]{1,0:T(8,128)S(1)} %get-tuple-element.48.refs_0_.rows_ref), channel_id=1, source_target_pairs={{0,66},{1,65},{2,64},{3,67},{4,70},{5,69},{6,68},{7,71},{8,74},{9,... | collective-permute-start | bytes 98312 | tf_op jit(solution)/shard_map/ppermute | solution.py:446
  46.0 8.0 %collective-permute-start.10 = (f32[8,1024]{1,0:T(8,128)S(1)}, f32[8,1024]{1,0:T(8,128)S(1)}, u32[]{:S(2)}, u32[]{:S(2)}) collective-permute-start(f32[8,1024]{1,0:T(8,128)S(1)} %pair_rows.1.refs_0_), channel_id=1, source_target_pairs={{0,4},{1,5},{2,6},{3,7},{4,8},{5,9},{6,10},{7,11},{8,12},{9,13},{1... | collective-permute-start | bytes 98312 | tf_op jit(solution)/shard_map/ppermute | solution.py:446
  47.6 6.4 %collective-permute-start.11 = (f32[8,1024]{1,0:T(8,128)S(1)}, f32[8,1024]{1,0:T(8,128)S(1)}, u32[]{:S(2)}, u32[]{:S(2)}) collective-permute-start(f32[8,1024]{1,0:T(8,128)S(1)} %pair_rows.1.refs_0_), channel_id=1, source_target_pairs={{0,12},{1,13},{2,14},{3,15},{4,0},{5,1},{6,2},{7,3},{8,4},{9,5},{1... | collective-permute-start | bytes 98312 | tf_op jit(solution)/shard_map/ppermute | solution.py:446
  49.3 5.4 %collective-permute-start.12 = (f32[8,1024]{1,0:T(8,128)S(1)}, f32[8,1024]{1,0:T(8,128)S(1)}, u32[]{:S(2)}, u32[]{:S(2)}) collective-permute-start(f32[8,1024]{1,0:T(8,128)S(1)} %pair_rows.1.refs_0_), channel_id=1, source_target_pairs={{0,8},{1,9},{2,10},{3,11},{4,12},{5,13},{6,14},{7,15},{8,0},{9,1},... | collective-permute-start | bytes 98312 | tf_op jit(solution)/shard_map/ppermute | solution.py:446
  58.4 16.1 %collective-permute-start.20 = (bf16[4,768,128]{2,1,0:T(8,128)(2,1)S(1)}, bf16[4,768,128]{2,1,0:T(8,128)(2,1)S(1)}, u32[]{:S(2)}, u32[]{:S(2)}) collective-permute-start(bf16[4,768,128]{2,1,0:T(8,128)(2,1)S(1)} %backward_partner.1.later_ref), channel_id=1, source_target_pairs={{0,64},{1,67},{2,66},{3,65},{4,68},{5,71},{6,70},{7,69},{8,72},{9,... | collective-permute-start | bytes 2359304 | tf_op jit(solution)/shard_map/ppermute | solution.py:446
  60.1 11.3 %collective-permute-start.13 = (bf16[2,768,128]{2,1,0:T(8,128)(2,1)S(1)}, bf16[2,768,128]{2,1,0:T(8,128)(2,1)S(1)}, u32[]{:S(2)}, u32[]{:S(2)}) collective-permute-start(bf16[2,768,128]{2,1,0:T(8,128)(2,1)S(1)} %get-tuple-element.50), channel_id=1, source_target_pairs={{0,12},{1,13},{2,14},{3,15},{4,0},{5,1},{6,2},{7,3},{8,4},{9,5},{1... | collective-permute-start | bytes 1179656 | tf_op jit(solution)/shard_map/ppermute | solution.py:446
  62.2 11.1 %collective-permute-start.14 = (bf16[2,768,128]{2,1,0:T(8,128)(2,1)S(1)}, bf16[2,768,128]{2,1,0:T(8,128)(2,1)S(1)}, u32[]{:S(2)}, u32[]{:S(2)}) collective-permute-start(bf16[2,768,128]{2,1,0:T(8,128)(2,1)S(1)} %get-tuple-element.51), channel_id=1, source_target_pairs={{0,4},{1,5},{2,6},{3,7},{4,8},{5,9},{6,10},{7,11},{8,12},{9,13},{1... | collective-permute-start | bytes 1179656 | tf_op jit(solution)/shard_map/ppermute | solution.py:446
  62.4 6.9 %collective-permute-start.15 = (bf16[768,128]{1,0:T(8,128)(2,1)S(1)}, bf16[768,128]{1,0:T(8,128)(2,1)S(1)}, u32[]{:S(2)}, u32[]{:S(2)}) collective-permute-start(bf16[768,128]{1,0:T(8,128)(2,1)S(1)} %get-tuple-element.53), channel_id=1, source_target_pairs={{0,66},{1,65},{2,64},{3,67},{4,70},{5,69},{6,68},{7,71},{8,74},{9,... | collective-permute-start | bytes 589832 | tf_op jit(solution)/shard_map/ppermute | solution.py:446
  69.3 7.5 %collective-permute-start.16 = (bf16[768,128]{1,0:T(8,128)(2,1)S(1)}, bf16[768,128]{1,0:T(8,128)(2,1)S(1)}, u32[]{:S(2)}, u32[]{:S(2)}) collective-permute-start(bf16[768,128]{1,0:T(8,128)(2,1)S(1)} %sum_far.1), channel_id=1, source_target_pairs={{0,8},{1,9},{2,10},{3,11},{4,12},{5,13},{6,14},{7,15},{8,0},{9,1},... | collective-permute-start | bytes 589832 | tf_op jit(solution)/shard_map/ppermute | solution.py:446
  73.3 7.0 %collective-permute-start.17 = (bf16[768,128]{1,0:T(8,128)(2,1)S(1)}, bf16[768,128]{1,0:T(8,128)(2,1)S(1)}, u32[]{:S(2)}, u32[]{:S(2)}) collective-permute-start(bf16[768,128]{1,0:T(8,128)(2,1)S(1)} %sum_partner.1), channel_id=1, source_target_pairs={{0,66},{1,65},{2,64},{3,67},{4,70},{5,69},{6,68},{7,71},{8,74},{9,... | collective-permute-start | bytes 589832 | tf_op jit(solution)/shard_map/ppermute | solution.py:446
  74.7 8.9 %collective-permute-start.21 = (bf16[768,128]{1,0:T(8,128)(2,1)S(1)}, bf16[768,128]{1,0:T(8,128)(2,1)S(1)}, u32[]{:S(2)}, u32[]{:S(2)}) collective-permute-start(bf16[768,128]{1,0:T(8,128)(2,1)S(1)} %get-tuple-element.59), channel_id=1, source_target_pairs={{0,48},{1,49},{2,50},{3,51},{4,52},{5,53},{6,54},{7,55},{8,56},{9,... | collective-permute-start | bytes 589832 | tf_op jit(solution)/shard_map/ppermute | solution.py:446
  76.0 7.6 %collective-permute-start.22 = (bf16[768,128]{1,0:T(8,128)(2,1)S(1)}, bf16[768,128]{1,0:T(8,128)(2,1)S(1)}, u32[]{:S(2)}, u32[]{:S(2)}) collective-permute-start(bf16[768,128]{1,0:T(8,128)(2,1)S(1)} %get-tuple-element.60), channel_id=1, source_target_pairs={{0,16},{1,17},{2,18},{3,19},{4,20},{5,21},{6,22},{7,23},{8,24},{9,... | collective-permute-start | bytes 589832 | tf_op jit(solution)/shard_map/ppermute | solution.py:446
  76.8 8.2 %collective-permute-start.23 = (bf16[768,128]{1,0:T(8,128)(2,1)S(1)}, bf16[768,128]{1,0:T(8,128)(2,1)S(1)}, u32[]{:S(2)}, u32[]{:S(2)}) collective-permute-start(bf16[768,128]{1,0:T(8,128)(2,1)S(1)} %get-tuple-element.61), channel_id=1, source_target_pairs={{0,32},{1,33},{2,34},{3,35},{4,36},{5,37},{6,38},{7,39},{8,40},{9,... | collective-permute-start | bytes 589832 | tf_op jit(solution)/shard_map/ppermute | solution.py:446
  81.0 1.3 %collective-permute-start.18 = (bf16[128,384]{1,0:T(8,128)(2,1)S(1)}, bf16[128,384]{1,0:T(8,128)(2,1)S(1)}, u32[]{:S(2)}, u32[]{:S(2)}) collective-permute-start(bf16[128,384]{1,0:T(8,128)(2,1)S(1)} %get-tuple-element.54.own_ref), channel_id=1, source_target_pairs={{0,1},{1,0},{2,3},{3,2},{4,5},{5,4},{6,7},{7,6},{8,9},{9,8},{10,11... | collective-permute-start | bytes 294920 | tf_op jit(solution)/shard_map/ppermute | solution.py:532

commit v7 on v6

--- a/solution.py
+++ b/solution.py
@@ -122,7 +122,6 @@
 
 
 def stats_part(tasks, qmark, cols_ref, rows_ref):
-    cols_ref[...] = jnp.zeros_like(cols_ref)
     for h in range(HP):
         for key_refs, kmarks, chunks in tasks:
             marks = jnp.concatenate([m[...] for m in kmarks], axis=0)

time: 86 us -> 85.9 us (level)
  no operation moved by 1% of the time
where the time goes in v7:
time: 85.9 us; the launch traced here: 85.7 us
  starting transfers between devices  37.9 us (44%)
  Pallas kernels  28.1 us (33%)
  waiting for transfers between devices  16.9 us (20%)
  other arithmetic  2.03 us (2%)
    ppermute x22, starting transfers between devices, send(): return lax.ppermute(array, ('row', 'col', 'head'), pairs)  37.9 us
    pallas_call x17, Pallas kernels, call(): pl.pallas_call(kernel, out_shape=out_shape, in_specs=[ANYWHERE] * anywher...  28.1 us
    ppermute x22, waiting for transfers between devices, send(): return lax.ppermute(array, ('row', 'col', 'head'), pairs)  15.6 us
  transfers between devices with their start and end apart: 24, of which 13 were waited for; matrix products, arithmetic and copies ran while one was open for 1% of the time, Pallas kernels for 29%

profile of v7, /device:TPU:0, one launch (start us, length us, event | category | flops | bytes accessed | tf_op | source)
XLA Modules:
  0.0 85.7 jit_solution(281860914422244550)
XLA Ops:
  0.6 2.9 %pack.1 = (bf16[784,128]{1,0:T(8,128)(2,1)}, bf16[784,128]{1,0:T(8,128)(2,1)}) custom-call(s32[1,128]{1,0:T(1,128)} %bitcast.17, bf16[128,384]{1,0:T(8,128)(2,1)} %refs_1_.1, bf16[128,384]{1,0:T(8,128)(2,1)} %refs_2_.1, bf16[128,384]{1,0:T(8,128)(2,1)} %refs_3_.1, bf16[128,1536]{1,0:T(8,128)(2,1)} %refs_4_.1, bf16[384,1536]{1,0:T(8,128)(2,1)} %own_weight.1), custom_call_target="tpu_custom_call" | custom-call | tf_op jit(solution)/shard_map/pack/pallas_call | solution.py:31
  3.5 2.9 %collective-permute-start.3 = (bf16[784,128]{1,0:T(8,128)(2,1)}, bf16[784,128]{1,0:T(8,128)(2,1)S(1)}, u32[]{:S(2)}, u32[]{:S(2)}) collective-permute-start(bf16[784,128]{1,0:T(8,128)(2,1)} %get-tuple-element.35), channel_id=1, source_target_pairs={{0,66},{1,65},{2,64},{3,67},{4,70},{5,69},{6,68},{7,71},{8,74},{9,... | collective-permute-start | bytes 602120 | tf_op jit(solution)/shard_map/ppermute | solution.py:445
  6.5 3.2 %collective-permute-start.4 = (bf16[784,128]{1,0:T(8,128)(2,1)}, bf16[784,128]{1,0:T(8,128)(2,1)S(1)}, u32[]{:S(2)}, u32[]{:S(2)}) collective-permute-start(bf16[784,128]{1,0:T(8,128)(2,1)} %get-tuple-element.35), channel_id=1, source_target_pairs={{0,8},{1,9},{2,10},{3,11},{4,12},{5,13},{6,14},{7,15},{8,0},{9,1},... | collective-permute-start | bytes 602120 | tf_op jit(solution)/shard_map/ppermute | solution.py:445
  9.8 2.0 %collective-permute-start = (bf16[784,128]{1,0:T(8,128)(2,1)}, bf16[784,128]{1,0:T(8,128)(2,1)S(1)}, u32[]{:S(2)}, u32[]{:S(2)}) collective-permute-start(bf16[784,128]{1,0:T(8,128)(2,1)} %get-tuple-element.36), channel_id=1, source_target_pairs={{0,16},{1,17},{2,18},{3,19},{4,20},{5,21},{6,22},{7,23},{8,24},{9,... | collective-permute-start | bytes 602120 | tf_op jit(solution)/shard_map/ppermute | solution.py:445
  11.8 2.1 %collective-permute-start.1 = (bf16[784,128]{1,0:T(8,128)(2,1)}, bf16[784,128]{1,0:T(8,128)(2,1)S(1)}, u32[]{:S(2)}, u32[]{:S(2)}) collective-permute-start(bf16[784,128]{1,0:T(8,128)(2,1)} %get-tuple-element.36), channel_id=1, source_target_pairs={{0,48},{1,49},{2,50},{3,51},{4,52},{5,53},{6,54},{7,55},{8,56},{9,... | collective-permute-start | bytes 602120 | tf_op jit(solution)/shard_map/ppermute | solution.py:445
  13.9 1.9 %collective-permute-start.2 = (bf16[784,128]{1,0:T(8,128)(2,1)}, bf16[784,128]{1,0:T(8,128)(2,1)S(1)}, u32[]{:S(2)}, u32[]{:S(2)}) collective-permute-start(bf16[784,128]{1,0:T(8,128)(2,1)} %get-tuple-element.36), channel_id=1, source_target_pairs={{0,32},{1,33},{2,34},{3,35},{4,36},{5,37},{6,38},{7,39},{8,40},{9,... | collective-permute-start | bytes 602120 | tf_op jit(solution)/shard_map/ppermute | solution.py:445
  15.8 1.0 %pad_maximum_fusion.1.refs_0_ = bf16[2,784,128]{2,1,0:T(8,128)(2,1)S(1)} fusion(bf16[1,784,128]{2,1,0:T(8,128)(2,1)S(1)} %bitcast.16, bf16[1,784,128]{2,1,0:T(8,128)(2,1)} %bitcast.15), kind=kLoop, calls=%fused_computation.1 | loop fusion | flops 200704 | bytes 802816 | tf_op jit(solution)/shard_map/stack | solution.py:476
  16.8 0.2 collective-permute-done.4
  17.0 2.2 %collective-permute-done.5 = bf16[784,128]{1,0:T(8,128)(2,1)S(1)} collective-permute-done((bf16[784,128]{1,0:T(8,128)(2,1)}, bf16[784,128]{1,0:T(8,128)(2,1)S(1)}, u32[]{:S(2)}, u32[]{:S(2)}) %collective-permute-start.5) | collective-permute-done | bytes 200736 | tf_op jit(solution)/shard_map/ppermute | solution.py:445
  19.2 0.8 collective-permute-done
  20.0 0.8 collective-permute-done.1
  20.8 1.8 %collective-permute-done.2 = bf16[784,128]{1,0:T(8,128)(2,1)S(1)} collective-permute-done((bf16[784,128]{1,0:T(8,128)(2,1)}, bf16[784,128]{1,0:T(8,128)(2,1)S(1)}, u32[]{:S(2)}, u32[]{:S(2)}) %collective-permute-start.2) | collective-permute-done | bytes 200736 | tf_op jit(solution)/shard_map/ppermute | solution.py:445
  22.6 1.0 %pad_maximum_fusion.refs_2_.refs_4_.k_ref = bf16[4,784,128]{2,1,0:T(8,128)(2,1)S(1)} fusion(bf16[1,784,128]{2,1,0:T(8,128)(2,1)S(1)} %bitcast.12, bf16[1,784,128]{2,1,0:T(8,128)(2,1)S(1)} %bitcast.11, bf16[1,784,128]{2,1,0:T(8,128)(2,1)S(1)} %bitcast.10, bf16[1,784,128]{2,1,0:T(8,128)(2,1)} %bitcast.9), kind=kLoop, calls=%fused_computation | loop fusion | flops 1204224 | bytes 1605632 | tf_op jit(solution)/shard_map/stack | solution.py:487
  23.6 1.5 %collective-permute-start.6 = (bf16[4,784,128]{2,1,0:T(8,128)(2,1)S(1)}, bf16[4,784,128]{2,1,0:T(8,128)(2,1)S(1)}, u32[]{:S(2)}, u32[]{:S(2)}) collective-permute-start(bf16[4,784,128]{2,1,0:T(8,128)(2,1)S(1)} %pad_maximum_fusion.refs_2_.refs_4_.k_ref), channel_id=1, source_target_pairs={{0,64},{1,67},{2,66},{3,65},{4,68},{5,71},{6,70},{7,69},{8,72},{9,... | collective-permute-start | bytes 2408456 | tf_op jit(solution)/shard_map/ppermute | solution.py:445
  25.2 1.6 %collective-permute-start.7 = (bf16[2,784,128]{2,1,0:T(8,128)(2,1)S(1)}, bf16[2,784,128]{2,1,0:T(8,128)(2,1)S(1)}, u32[]{:S(2)}, u32[]{:S(2)}) collective-permute-start(bf16[2,784,128]{2,1,0:T(8,128)(2,1)S(1)} %pad_maximum_fusion.1.refs_0_), channel_id=1, source_target_pairs={{0,4},{1,5},{2,6},{3,7},{4,8},{5,9},{6,10},{7,11},{8,12},{9,13},{1... | collective-permute-start | bytes 1204232 | tf_op jit(solution)/shard_map/ppermute | solution.py:445
  26.7 1.7 %collective-permute-start.8 = (bf16[2,784,128]{2,1,0:T(8,128)(2,1)S(1)}, bf16[2,784,128]{2,1,0:T(8,128)(2,1)S(1)}, u32[]{:S(2)}, u32[]{:S(2)}) collective-permute-start(bf16[2,784,128]{2,1,0:T(8,128)(2,1)S(1)} %pad_maximum_fusion.1.refs_0_), channel_id=1, source_target_pairs={{0,12},{1,13},{2,14},{3,15},{4,0},{5,1},{6,2},{7,3},{8,4},{9,5},{1... | collective-permute-start | bytes 1204232 | tf_op jit(solution)/shard_map/ppermute | solution.py:445
  28.5 1.8 %stats_early.1 = (f32[512,128]{1,0:T(8,128)S(1)}, f32[8,512]{1,0:T(8,128)S(1)}, bf16[512,128]{1,0:T(8,128)(2,1)S(1)}, bf16[512,128]{1,0:T(8,128)(2,1)S(1)}) custom-call(bf16[2,784,128]{2,1,0:T(8,128)(2,1)S(1)} %pad_maximum_fusion.1.refs_0_, bf16[2,784,128]{2,1,0:T(8,128)(2,1)S(1)} %pad_maximum_fusion.2.refs_1_.refs_3_, ...), custom_call_target="tpu_custom_call" | custom-call | tf_op jit(solution)/shard_map/stats_early/pallas_call | solution.py:31
  30.3 1.9 %forward_early.1.refs_2_ = f32[3,512,384]{2,1,0:T(8,128)S(1)} custom-call(bf16[2,784,128]{2,1,0:T(8,128)(2,1)S(1)} %pad_maximum_fusion.1.refs_0_, bf16[2,784,128]{2,1,0:T(8,128)(2,1)S(1)} %pad_maximum_fusion.2.refs_1_.refs_3_, bf16[4,784,128]{2,1,0:T(8,128)(2,1)S(1)} %pad_maximum_fusion.refs_2_.refs_4_.k_ref, ...), custom_call_target="tpu_custom_call" | custom-call | tf_op jit(solution)/shard_map/forward_early/pallas_call | solution.py:31
  32.2 3.1 %collective-permute-done.7.refs_1_ = bf16[2,784,128]{2,1,0:T(8,128)(2,1)S(1)} collective-permute-done((bf16[2,784,128]{2,1,0:T(8,128)(2,1)S(1)}, bf16[2,784,128]{2,1,0:T(8,128)(2,1)S(1)}, u32[]{:S(2)}, u32[]{:S(2)}) %collective-permute-start.7) | collective-permute-done | bytes 401440 | tf_op jit(solution)/shard_map/ppermute | solution.py:445
  35.3 0.6 collective-permute-done.6.refs_5_.refs_3_.k_ref
  35.9 4.1 %stats_all.1 = (f32[1024,128]{1,0:T(8,128)S(1)}, f32[8,1024]{1,0:T(8,128)S(1)}, bf16[1024,128]{1,0:T(8,128)(2,1)S(1)}, bf16[512,128]{1,0:T(8,128)(2,1)S(1)}) custom-call(bf16[2,784,128]{2,1,0:T(8,128)(2,1)S(1)} %pad_maximum_fusion.1.refs_0_, bf16[2,784,128]{2,1,0:T(8,128)(2,1)S(1)} %collective-permute-done.7.refs_1_, ...), custom_call_target="tpu_custom_call" | custom-call | tf_op jit(solution)/shard_map/stats_all/pallas_call | solution.py:31
  40.0 3.0 %collective-permute-start.9 = (f32[8,1024]{1,0:T(8,128)S(1)}, f32[8,1024]{1,0:T(8,128)S(1)}, u32[]{:S(2)}, u32[]{:S(2)}) collective-permute-start(f32[8,1024]{1,0:T(8,128)S(1)} %get-tuple-element.48.refs_0_.rows_ref), channel_id=1, source_target_pairs={{0,66},{1,65},{2,64},{3,67},{4,70},{5,69},{6,68},{7,71},{8,74},{9,... | collective-permute-start | bytes 98312 | tf_op jit(solution)/shard_map/ppermute | solution.py:445
  43.0 2.7 %forward_near.1.later_ref.refs_0_ = f32[3,512,384]{2,1,0:T(8,128)S(1)} custom-call(bf16[2,784,128]{2,1,0:T(8,128)(2,1)S(1)} %pad_maximum_fusion.1.refs_0_, bf16[2,784,128]{2,1,0:T(8,128)(2,1)S(1)} %collective-permute-done.7.refs_1_, bf16[4,784,128]{2,1,0:T(8,128)(2,1)S(1)} %pad_maximum_fusion.refs_2_.refs_4_.k_ref, ...), custom_call_target="tpu_custom_call" | custom-call | flops 3000000000 | tf_op jit(solution)/shard_map/forward_near/pallas_call | solution.py:31
  45.9 1.6 %collective-permute-start.10 = (f32[8,1024]{1,0:T(8,128)S(1)}, f32[8,1024]{1,0:T(8,128)S(1)}, u32[]{:S(2)}, u32[]{:S(2)}) collective-permute-start(f32[8,1024]{1,0:T(8,128)S(1)} %pair_rows.1.refs_0_), channel_id=1, source_target_pairs={{0,4},{1,5},{2,6},{3,7},{4,8},{5,9},{6,10},{7,11},{8,12},{9,13},{1... | collective-permute-start | bytes 98312 | tf_op jit(solution)/shard_map/ppermute | solution.py:445
  47.5 1.7 %collective-permute-start.11 = (f32[8,1024]{1,0:T(8,128)S(1)}, f32[8,1024]{1,0:T(8,128)S(1)}, u32[]{:S(2)}, u32[]{:S(2)}) collective-permute-start(f32[8,1024]{1,0:T(8,128)S(1)} %pair_rows.1.refs_0_), channel_id=1, source_target_pairs={{0,12},{1,13},{2,14},{3,15},{4,0},{5,1},{6,2},{7,3},{8,4},{9,5},{1... | collective-permute-start | bytes 98312 | tf_op jit(solution)/shard_map/ppermute | solution.py:445
  49.2 2.0 %collective-permute-start.12 = (f32[8,1024]{1,0:T(8,128)S(1)}, f32[8,1024]{1,0:T(8,128)S(1)}, u32[]{:S(2)}, u32[]{:S(2)}) collective-permute-start(f32[8,1024]{1,0:T(8,128)S(1)} %pair_rows.1.refs_0_), channel_id=1, source_target_pairs={{0,8},{1,9},{2,10},{3,11},{4,12},{5,13},{6,14},{7,15},{8,0},{9,1},... | collective-permute-start | bytes 98312 | tf_op jit(solution)/shard_map/ppermute | solution.py:445
  51.2 2.7 %forward_far.1.later_ref.refs_1_ = f32[3,512,384]{2,1,0:T(8,128)S(1)} custom-call(bf16[2,784,128]{2,1,0:T(8,128)(2,1)S(1)} %collective-permute-done.8.refs_2_.refs_0_, bf16[2,784,128]{2,1,0:T(8,128)(2,1)S(1)} %pad_maximum_fusion.2.refs_1_.refs_3_, bf16[4,784,128]{2,1,0:T(8,128)(2,1)S(1)} %pad_maximum_fusion.refs_2_.refs_4_.k_ref, ...), custom_call_target="tpu_custom_call" | custom-call | flops 3000000000 | tf_op jit(solution)/shard_map/forward_far/pallas_call | solution.py:31
  54.0 0.6 collective-permute-done.12.refs_3_
  54.7 3.6 %backward_partner.1.later_ref = bf16[4,768,128]{2,1,0:T(8,128)(2,1)S(1)} custom-call(bf16[4,784,128]{2,1,0:T(8,128)(2,1)S(1)} %collective-permute-done.6.refs_5_.refs_3_.k_ref, bf16[2,784,128]{2,1,0:T(8,128)(2,1)S(1)} %pad_maximum_fusion.1.refs_0_, bf16[2,784,128]{2,1,0:T(8,128)(2,1)S(1)} %collective-permute-done.7.refs_1_, ...), custom_call_target="tpu_custom_call" | custom-call | flops 4026531840 | bytes 8388608 | tf_op jit(solution)/shard_map/backward_partner/pallas_call | solution.py:31
  58.3 0.3 collective-permute-start.20
  58.6 1.4 %share_rows.1 = (bf16[2,768,128]{2,1,0:T(8,128)(2,1)S(1)}, bf16[2,768,128]{2,1,0:T(8,128)(2,1)S(1)}, bf16[2,768,128]{2,1,0:T(8,128)(2,1)S(1)}, bf16[1,768,128]{2,1,0:T(8,128)(2,1)S(1)}, bf16[768,128]{1,0:T(8,128)(2,1)S(1)}) custom-call(bf16[4,768,128]{2,1,0:T(8,128)(2,1)S(1)} %backward_partner.1.later_ref, ...), custom_call_target="tpu_custom_call" | custom-call | bytes 4194304 | tf_op jit(solution)/shard_map/share_rows/pallas_call | solution.py:31
  60.0 2.1 %collective-permute-start.13 = (bf16[2,768,128]{2,1,0:T(8,128)(2,1)S(1)}, bf16[2,768,128]{2,1,0:T(8,128)(2,1)S(1)}, u32[]{:S(2)}, u32[]{:S(2)}) collective-permute-start(bf16[2,768,128]{2,1,0:T(8,128)(2,1)S(1)} %get-tuple-element.50), channel_id=1, source_target_pairs={{0,12},{1,13},{2,14},{3,15},{4,0},{5,1},{6,2},{7,3},{8,4},{9,5},{1... | collective-permute-start | bytes 1179656 | tf_op jit(solution)/shard_map/ppermute | solution.py:445
  62.1 0.2 collective-permute-start.14
  62.3 2.2 %collective-permute-start.15 = (bf16[768,128]{1,0:T(8,128)(2,1)S(1)}, bf16[768,128]{1,0:T(8,128)(2,1)S(1)}, u32[]{:S(2)}, u32[]{:S(2)}) collective-permute-start(bf16[768,128]{1,0:T(8,128)(2,1)S(1)} %get-tuple-element.53), channel_id=1, source_target_pairs={{0,66},{1,65},{2,64},{3,67},{4,70},{5,69},{6,68},{7,71},{8,74},{9,... | collective-permute-start | bytes 589832 | tf_op jit(solution)/shard_map/ppermute | solution.py:445
  64.5 3.6 %backward_own.1.later_ref.own_ref = bf16[4,768,128]{2,1,0:T(8,128)(2,1)S(1)} custom-call(bf16[4,784,128]{2,1,0:T(8,128)(2,1)S(1)} %pad_maximum_fusion.refs_2_.refs_4_.k_ref, bf16[2,784,128]{2,1,0:T(8,128)(2,1)S(1)} %pad_maximum_fusion.1.refs_0_, bf16[2,784,128]{2,1,0:T(8,128)(2,1)S(1)} %collective-permute-done.7.refs_1_, ...), custom_call_target="tpu_custom_call" | custom-call | flops 4026531840 | bytes 8388608 | tf_op jit(solution)/shard_map/backward_own/pallas_call | solution.py:31
  68.1 1.1 %collective-permute-done.15.got_ref = bf16[768,128]{1,0:T(8,128)(2,1)S(1)} collective-permute-done((bf16[768,128]{1,0:T(8,128)(2,1)S(1)}, bf16[768,128]{1,0:T(8,128)(2,1)S(1)}, u32[]{:S(2)}, u32[]{:S(2)}) %collective-permute-start.15) | collective-permute-done | bytes 196640 | tf_op jit(solution)/shard_map/ppermute | solution.py:445
  69.3 2.1 %collective-permute-start.16 = (bf16[768,128]{1,0:T(8,128)(2,1)S(1)}, bf16[768,128]{1,0:T(8,128)(2,1)S(1)}, u32[]{:S(2)}, u32[]{:S(2)}) collective-permute-start(bf16[768,128]{1,0:T(8,128)(2,1)S(1)} %sum_far.1), channel_id=1, source_target_pairs={{0,8},{1,9},{2,10},{3,11},{4,12},{5,13},{6,14},{7,15},{8,0},{9,1},... | collective-permute-start | bytes 589832 | tf_op jit(solution)/shard_map/ppermute | solution.py:445
  71.3 1.8 %collective-permute-done.14.refs_2_ = bf16[2,768,128]{2,1,0:T(8,128)(2,1)S(1)} collective-permute-done((bf16[2,768,128]{2,1,0:T(8,128)(2,1)S(1)}, bf16[2,768,128]{2,1,0:T(8,128)(2,1)S(1)}, u32[]{:S(2)}, u32[]{:S(2)}) %collective-permute-start.14) | collective-permute-done | bytes 393248 | tf_op jit(solution)/shard_map/ppermute | solution.py:445
  73.3 1.2 %collective-permute-start.17 = (bf16[768,128]{1,0:T(8,128)(2,1)S(1)}, bf16[768,128]{1,0:T(8,128)(2,1)S(1)}, u32[]{:S(2)}, u32[]{:S(2)}) collective-permute-start(bf16[768,128]{1,0:T(8,128)(2,1)S(1)} %sum_partner.1), channel_id=1, source_target_pairs={{0,66},{1,65},{2,64},{3,67},{4,70},{5,69},{6,68},{7,71},{8,74},{9,... | collective-permute-start | bytes 589832 | tf_op jit(solution)/shard_map/ppermute | solution.py:445
  74.6 1.3 %collective-permute-start.21 = (bf16[768,128]{1,0:T(8,128)(2,1)S(1)}, bf16[768,128]{1,0:T(8,128)(2,1)S(1)}, u32[]{:S(2)}, u32[]{:S(2)}) collective-permute-start(bf16[768,128]{1,0:T(8,128)(2,1)S(1)} %get-tuple-element.59), channel_id=1, source_target_pairs={{0,48},{1,49},{2,50},{3,51},{4,52},{5,53},{6,54},{7,55},{8,56},{9,... | collective-permute-start | bytes 589832 | tf_op jit(solution)/shard_map/ppermute | solution.py:445
  76.0 0.8 collective-permute-start.22
  76.7 2.4 %collective-permute-start.23 = (bf16[768,128]{1,0:T(8,128)(2,1)S(1)}, bf16[768,128]{1,0:T(8,128)(2,1)S(1)}, u32[]{:S(2)}, u32[]{:S(2)}) collective-permute-start(bf16[768,128]{1,0:T(8,128)(2,1)S(1)} %get-tuple-element.61), channel_id=1, source_target_pairs={{0,32},{1,33},{2,34},{3,35},{4,36},{5,37},{6,38},{7,39},{8,40},{9,... | collective-permute-start | bytes 589832 | tf_op jit(solution)/shard_map/ppermute | solution.py:445
  79.1 1.1 %collective-permute-done.17.refs_4_ = bf16[768,128]{1,0:T(8,128)(2,1)S(1)} collective-permute-done((bf16[768,128]{1,0:T(8,128)(2,1)S(1)}, bf16[768,128]{1,0:T(8,128)(2,1)S(1)}, u32[]{:S(2)}, u32[]{:S(2)}) %collective-permute-start.17) | collective-permute-done | bytes 196640 | tf_op jit(solution)/shard_map/ppermute | solution.py:445
  80.2 0.7 sum_rows.1
  80.9 1.3 %collective-permute-done.18.other_ref = bf16[128,384]{1,0:T(8,128)(2,1)S(1)} collective-permute-done((bf16[128,384]{1,0:T(8,128)(2,1)S(1)}, bf16[128,384]{1,0:T(8,128)(2,1)S(1)}, u32[]{:S(2)}, u32[]{:S(2)}) %collective-permute-start.18) | collective-permute-done | bytes 98336 | tf_op jit(solution)/shard_map/ppermute | solution.py:531
  82.2 1.3 %project.1 = (bf16[128,1536]{1,0:T(8,128)(2,1)}, f32[8,128]{1,0:T(8,128)S(1)}) custom-call(bf16[128,384]{1,0:T(8,128)(2,1)S(1)} %get-tuple-element.54.own_ref, bf16[128,384]{1,0:T(8,128)(2,1)S(1)} %collective-permute-done.18.other_ref, bf16[384,1536]{1,0:T(8,128)(2,1)S(1)} %copy-done, bf16[384,1536]{1,0:T(8,128)(2,1)S(1)} %collective-permute-done.19.other_weight), custom_call_target="tpu_custom_call" | custom-call | flops 301989888 | bytes 2359296 | tf_op jit(solution)/shard_map/project/pallas_call | solution.py:31
  83.6 1.4 %collective-permute-done.23.refs_4_ = bf16[768,128]{1,0:T(8,128)(2,1)S(1)} collective-permute-done((bf16[768,128]{1,0:T(8,128)(2,1)S(1)}, bf16[768,128]{1,0:T(8,128)(2,1)S(1)}, u32[]{:S(2)}, u32[]{:S(2)}) %collective-permute-start.23) | collective-permute-done | bytes 196640 | tf_op jit(solution)/shard_map/ppermute | solution.py:445
  85.0 0.8 sum_keys.1
  (22 shorter events, 0.8 us)
Async XLA Ops:
  0.6 27.8 %copy-start = (bf16[384,1536]{1,0:T(8,128)(2,1)S(1)}, bf16[384,1536]{1,0:T(8,128)(2,1)}, u32[]{:S(2)}) copy-start(bf16[384,1536]{1,0:T(8,128)(2,1)} %own_weight.1) | copy-start | bytes 3538948
  3.5 10.4 %collective-permute-start.3 = (bf16[784,128]{1,0:T(8,128)(2,1)}, bf16[784,128]{1,0:T(8,128)(2,1)S(1)}, u32[]{:S(2)}, u32[]{:S(2)}) collective-permute-start(bf16[784,128]{1,0:T(8,128)(2,1)} %get-tuple-element.35), channel_id=1, source_target_pairs={{0,66},{1,65},{2,64},{3,67},{4,70},{5,69},{6,68},{7,71},{8,74},{9,... | collective-permute-start | bytes 602120 | tf_op jit(solution)/shard_map/ppermute | solution.py:445
  6.5 10.5 %collective-permute-start.4 = (bf16[784,128]{1,0:T(8,128)(2,1)}, bf16[784,128]{1,0:T(8,128)(2,1)S(1)}, u32[]{:S(2)}, u32[]{:S(2)}) collective-permute-start(bf16[784,128]{1,0:T(8,128)(2,1)} %get-tuple-element.35), channel_id=1, source_target_pairs={{0,8},{1,9},{2,10},{3,11},{4,12},{5,13},{6,14},{7,15},{8,0},{9,1},... | collective-permute-start | bytes 602120 | tf_op jit(solution)/shard_map/ppermute | solution.py:445
  9.7 9.5 %collective-permute-start.5 = (bf16[784,128]{1,0:T(8,128)(2,1)}, bf16[784,128]{1,0:T(8,128)(2,1)S(1)}, u32[]{:S(2)}, u32[]{:S(2)}) collective-permute-start(bf16[784,128]{1,0:T(8,128)(2,1)} %get-tuple-element.35), channel_id=1, source_target_pairs={{0,74},{1,73},{2,72},{3,75},{4,78},{5,77},{6,76},{7,79},{8,66},{9,... | collective-permute-start | bytes 602120 | tf_op jit(solution)/shard_map/ppermute | solution.py:445
  9.8 10.2 %collective-permute-start = (bf16[784,128]{1,0:T(8,128)(2,1)}, bf16[784,128]{1,0:T(8,128)(2,1)S(1)}, u32[]{:S(2)}, u32[]{:S(2)}) collective-permute-start(bf16[784,128]{1,0:T(8,128)(2,1)} %get-tuple-element.36), channel_id=1, source_target_pairs={{0,16},{1,17},{2,18},{3,19},{4,20},{5,21},{6,22},{7,23},{8,24},{9,... | collective-permute-start | bytes 602120 | tf_op jit(solution)/shard_map/ppermute | solution.py:445
  11.8 9.0 %collective-permute-start.1 = (bf16[784,128]{1,0:T(8,128)(2,1)}, bf16[784,128]{1,0:T(8,128)(2,1)S(1)}, u32[]{:S(2)}, u32[]{:S(2)}) collective-permute-start(bf16[784,128]{1,0:T(8,128)(2,1)} %get-tuple-element.36), channel_id=1, source_target_pairs={{0,48},{1,49},{2,50},{3,51},{4,52},{5,53},{6,54},{7,55},{8,56},{9,... | collective-permute-start | bytes 602120 | tf_op jit(solution)/shard_map/ppermute | solution.py:445
  13.9 8.7 %collective-permute-start.2 = (bf16[784,128]{1,0:T(8,128)(2,1)}, bf16[784,128]{1,0:T(8,128)(2,1)S(1)}, u32[]{:S(2)}, u32[]{:S(2)}) collective-permute-start(bf16[784,128]{1,0:T(8,128)(2,1)} %get-tuple-element.36), channel_id=1, source_target_pairs={{0,32},{1,33},{2,34},{3,35},{4,36},{5,37},{6,38},{7,39},{8,40},{9,... | collective-permute-start | bytes 602120 | tf_op jit(solution)/shard_map/ppermute | solution.py:445
  23.6 12.2 %collective-permute-start.6 = (bf16[4,784,128]{2,1,0:T(8,128)(2,1)S(1)}, bf16[4,784,128]{2,1,0:T(8,128)(2,1)S(1)}, u32[]{:S(2)}, u32[]{:S(2)}) collective-permute-start(bf16[4,784,128]{2,1,0:T(8,128)(2,1)S(1)} %pad_maximum_fusion.refs_2_.refs_4_.k_ref), channel_id=1, source_target_pairs={{0,64},{1,67},{2,66},{3,65},{4,68},{5,71},{6,70},{7,69},{8,72},{9,... | collective-permute-start | bytes 2408456 | tf_op jit(solution)/shard_map/ppermute | solution.py:445
  25.2 10.1 %collective-permute-start.7 = (bf16[2,784,128]{2,1,0:T(8,128)(2,1)S(1)}, bf16[2,784,128]{2,1,0:T(8,128)(2,1)S(1)}, u32[]{:S(2)}, u32[]{:S(2)}) collective-permute-start(bf16[2,784,128]{2,1,0:T(8,128)(2,1)S(1)} %pad_maximum_fusion.1.refs_0_), channel_id=1, source_target_pairs={{0,4},{1,5},{2,6},{3,7},{4,8},{5,9},{6,10},{7,11},{8,12},{9,13},{1... | collective-permute-start | bytes 1204232 | tf_op jit(solution)/shard_map/ppermute | solution.py:445
  26.7 8.6 %collective-permute-start.8 = (bf16[2,784,128]{2,1,0:T(8,128)(2,1)S(1)}, bf16[2,784,128]{2,1,0:T(8,128)(2,1)S(1)}, u32[]{:S(2)}, u32[]{:S(2)}) collective-permute-start(bf16[2,784,128]{2,1,0:T(8,128)(2,1)S(1)} %pad_maximum_fusion.1.refs_0_), channel_id=1, source_target_pairs={{0,12},{1,13},{2,14},{3,15},{4,0},{5,1},{6,2},{7,3},{8,4},{9,5},{1... | collective-permute-start | bytes 1204232 | tf_op jit(solution)/shard_map/ppermute | solution.py:445
  28.4 52.5 %collective-permute-start.19 = (bf16[384,1536]{1,0:T(8,128)(2,1)S(1)}, bf16[384,1536]{1,0:T(8,128)(2,1)S(1)}, u32[]{:S(2)}, u32[]{:S(2)}) collective-permute-start(bf16[384,1536]{1,0:T(8,128)(2,1)S(1)} %copy-done), channel_id=1, source_target_pairs={{0,1},{1,0},{2,3},{3,2},{4,5},{5,4},{6,7},{7,6},{8,9},{9,8},{10,11... | collective-permute-start | bytes 3538952 | tf_op jit(solution)/shard_map/ppermute | solution.py:489
  40.0 5.8 %collective-permute-start.9 = (f32[8,1024]{1,0:T(8,128)S(1)}, f32[8,1024]{1,0:T(8,128)S(1)}, u32[]{:S(2)}, u32[]{:S(2)}) collective-permute-start(f32[8,1024]{1,0:T(8,128)S(1)} %get-tuple-element.48.refs_0_.rows_ref), channel_id=1, source_target_pairs={{0,66},{1,65},{2,64},{3,67},{4,70},{5,69},{6,68},{7,71},{8,74},{9,... | collective-permute-start | bytes 98312 | tf_op jit(solution)/shard_map/ppermute | solution.py:445
  45.9 8.1 %collective-permute-start.10 = (f32[8,1024]{1,0:T(8,128)S(1)}, f32[8,1024]{1,0:T(8,128)S(1)}, u32[]{:S(2)}, u32[]{:S(2)}) collective-permute-start(f32[8,1024]{1,0:T(8,128)S(1)} %pair_rows.1.refs_0_), channel_id=1, source_target_pairs={{0,4},{1,5},{2,6},{3,7},{4,8},{5,9},{6,10},{7,11},{8,12},{9,13},{1... | collective-permute-start | bytes 98312 | tf_op jit(solution)/shard_map/ppermute | solution.py:445
  47.5 6.4 %collective-permute-start.11 = (f32[8,1024]{1,0:T(8,128)S(1)}, f32[8,1024]{1,0:T(8,128)S(1)}, u32[]{:S(2)}, u32[]{:S(2)}) collective-permute-start(f32[8,1024]{1,0:T(8,128)S(1)} %pair_rows.1.refs_0_), channel_id=1, source_target_pairs={{0,12},{1,13},{2,14},{3,15},{4,0},{5,1},{6,2},{7,3},{8,4},{9,5},{1... | collective-permute-start | bytes 98312 | tf_op jit(solution)/shard_map/ppermute | solution.py:445
  49.2 5.4 %collective-permute-start.12 = (f32[8,1024]{1,0:T(8,128)S(1)}, f32[8,1024]{1,0:T(8,128)S(1)}, u32[]{:S(2)}, u32[]{:S(2)}) collective-permute-start(f32[8,1024]{1,0:T(8,128)S(1)} %pair_rows.1.refs_0_), channel_id=1, source_target_pairs={{0,8},{1,9},{2,10},{3,11},{4,12},{5,13},{6,14},{7,15},{8,0},{9,1},... | collective-permute-start | bytes 98312 | tf_op jit(solution)/shard_map/ppermute | solution.py:445
  58.3 16.1 %collective-permute-start.20 = (bf16[4,768,128]{2,1,0:T(8,128)(2,1)S(1)}, bf16[4,768,128]{2,1,0:T(8,128)(2,1)S(1)}, u32[]{:S(2)}, u32[]{:S(2)}) collective-permute-start(bf16[4,768,128]{2,1,0:T(8,128)(2,1)S(1)} %backward_partner.1.later_ref), channel_id=1, source_target_pairs={{0,64},{1,67},{2,66},{3,65},{4,68},{5,71},{6,70},{7,69},{8,72},{9,... | collective-permute-start | bytes 2359304 | tf_op jit(solution)/shard_map/ppermute | solution.py:445
  60.0 11.3 %collective-permute-start.13 = (bf16[2,768,128]{2,1,0:T(8,128)(2,1)S(1)}, bf16[2,768,128]{2,1,0:T(8,128)(2,1)S(1)}, u32[]{:S(2)}, u32[]{:S(2)}) collective-permute-start(bf16[2,768,128]{2,1,0:T(8,128)(2,1)S(1)} %get-tuple-element.50), channel_id=1, source_target_pairs={{0,12},{1,13},{2,14},{3,15},{4,0},{5,1},{6,2},{7,3},{8,4},{9,5},{1... | collective-permute-start | bytes 1179656 | tf_op jit(solution)/shard_map/ppermute | solution.py:445
  62.1 11.1 %collective-permute-start.14 = (bf16[2,768,128]{2,1,0:T(8,128)(2,1)S(1)}, bf16[2,768,128]{2,1,0:T(8,128)(2,1)S(1)}, u32[]{:S(2)}, u32[]{:S(2)}) collective-permute-start(bf16[2,768,128]{2,1,0:T(8,128)(2,1)S(1)} %get-tuple-element.51), channel_id=1, source_target_pairs={{0,4},{1,5},{2,6},{3,7},{4,8},{5,9},{6,10},{7,11},{8,12},{9,13},{1... | collective-permute-start | bytes 1179656 | tf_op jit(solution)/shard_map/ppermute | solution.py:445
  62.3 6.9 %collective-permute-start.15 = (bf16[768,128]{1,0:T(8,128)(2,1)S(1)}, bf16[768,128]{1,0:T(8,128)(2,1)S(1)}, u32[]{:S(2)}, u32[]{:S(2)}) collective-permute-start(bf16[768,128]{1,0:T(8,128)(2,1)S(1)} %get-tuple-element.53), channel_id=1, source_target_pairs={{0,66},{1,65},{2,64},{3,67},{4,70},{5,69},{6,68},{7,71},{8,74},{9,... | collective-permute-start | bytes 589832 | tf_op jit(solution)/shard_map/ppermute | solution.py:445
  69.3 7.5 %collective-permute-start.16 = (bf16[768,128]{1,0:T(8,128)(2,1)S(1)}, bf16[768,128]{1,0:T(8,128)(2,1)S(1)}, u32[]{:S(2)}, u32[]{:S(2)}) collective-permute-start(bf16[768,128]{1,0:T(8,128)(2,1)S(1)} %sum_far.1), channel_id=1, source_target_pairs={{0,8},{1,9},{2,10},{3,11},{4,12},{5,13},{6,14},{7,15},{8,0},{9,1},... | collective-permute-start | bytes 589832 | tf_op jit(solution)/shard_map/ppermute | solution.py:445
  73.3 7.0 %collective-permute-start.17 = (bf16[768,128]{1,0:T(8,128)(2,1)S(1)}, bf16[768,128]{1,0:T(8,128)(2,1)S(1)}, u32[]{:S(2)}, u32[]{:S(2)}) collective-permute-start(bf16[768,128]{1,0:T(8,128)(2,1)S(1)} %sum_partner.1), channel_id=1, source_target_pairs={{0,66},{1,65},{2,64},{3,67},{4,70},{5,69},{6,68},{7,71},{8,74},{9,... | collective-permute-start | bytes 589832 | tf_op jit(solution)/shard_map/ppermute | solution.py:445
  74.6 8.9 %collective-permute-start.21 = (bf16[768,128]{1,0:T(8,128)(2,1)S(1)}, bf16[768,128]{1,0:T(8,128)(2,1)S(1)}, u32[]{:S(2)}, u32[]{:S(2)}) collective-permute-start(bf16[768,128]{1,0:T(8,128)(2,1)S(1)} %get-tuple-element.59), channel_id=1, source_target_pairs={{0,48},{1,49},{2,50},{3,51},{4,52},{5,53},{6,54},{7,55},{8,56},{9,... | collective-permute-start | bytes 589832 | tf_op jit(solution)/shard_map/ppermute | solution.py:445
  76.0 7.6 %collective-permute-start.22 = (bf16[768,128]{1,0:T(8,128)(2,1)S(1)}, bf16[768,128]{1,0:T(8,128)(2,1)S(1)}, u32[]{:S(2)}, u32[]{:S(2)}) collective-permute-start(bf16[768,128]{1,0:T(8,128)(2,1)S(1)} %get-tuple-element.60), channel_id=1, source_target_pairs={{0,16},{1,17},{2,18},{3,19},{4,20},{5,21},{6,22},{7,23},{8,24},{9,... | collective-permute-start | bytes 589832 | tf_op jit(solution)/shard_map/ppermute | solution.py:445
  76.7 8.2 %collective-permute-start.23 = (bf16[768,128]{1,0:T(8,128)(2,1)S(1)}, bf16[768,128]{1,0:T(8,128)(2,1)S(1)}, u32[]{:S(2)}, u32[]{:S(2)}) collective-permute-start(bf16[768,128]{1,0:T(8,128)(2,1)S(1)} %get-tuple-element.61), channel_id=1, source_target_pairs={{0,32},{1,33},{2,34},{3,35},{4,36},{5,37},{6,38},{7,39},{8,40},{9,... | collective-permute-start | bytes 589832 | tf_op jit(solution)/shard_map/ppermute | solution.py:445
  80.9 1.3 %collective-permute-start.18 = (bf16[128,384]{1,0:T(8,128)(2,1)S(1)}, bf16[128,384]{1,0:T(8,128)(2,1)S(1)}, u32[]{:S(2)}, u32[]{:S(2)}) collective-permute-start(bf16[128,384]{1,0:T(8,128)(2,1)S(1)} %get-tuple-element.54.own_ref), channel_id=1, source_target_pairs={{0,1},{1,0},{2,3},{3,2},{4,5},{5,4},{6,7},{7,6},{8,9},{9,8},{10,11... | collective-permute-start | bytes 294920 | tf_op jit(solution)/shard_map/ppermute | solution.py:531
